TPU v7x, 32 devices: a whole 2x2x4 slice. The times are simulated.
32 devices in a mesh: pair: 4 (over y, x), wide: 8 (over z, core).
Axes of the slice: x: 2, y: 2, z: 4, core: 2. Of those that a mesh axis runs over, the one named last changes fastest.
Arguments:
- noisy: bfloat16 [4, 10, 2048], P('pair', None, 'wide'), may hold values from -6 to 6
- action_mask: int32 [10, 128], P(None, 'wide'), may hold values 0 or 1
- time_index: int32 [4, 128], P('pair', 'wide'), may hold values from 0 to 39
- obs_embed: bfloat16 [4, 32, 1024], P('pair', 'wide'), may hold values from -6 to 6
- obs_slot: int32 [128], P('wide'), may hold values from 0 to 15, as said below
- cotangent: float32 [4, 256, 2048], P('pair', None, 'wide'), may hold values from -6 to 6
- params: float32 [256, 12627], P('wide'), may hold values from -1.264911 to 1.8782971
- first_moment: float32 [256, 12627], P('wide'), may hold values from -0.0078125 to 0.0078125
- second_moment: float32 [256, 12627], P('wide'), may hold values from 3.0935692e-07 to 1.2374277e-06
Outputs:
- activations: bfloat16 [4, 256, 2048], P('pair', None, 'wide')
- noisy_grad: float32 [4, 10, 2048], P('pair', None, 'wide')
- observation_grad: float32 [4, 32, 1024], P('pair', 'wide')
- grad_norm: float32 [], replicated
- new_params: float32 [256, 12627], P('wide')
- new_first: float32 [256, 12627], P('wide')
- new_second: float32 [256, 12627], P('wide')
- params_copy: bfloat16 [256, 12627], P('wide')
Inputs may be any that keep to these rules, and one draw needn't show every extreme that they name: `obs_slot`: in each aligned block of 16 samples the values are a permutation of 0 to 15.
All inputs are finite; a program needn't handle non-finite values. No bound on the sum of `action_mask` on one device may be relied on, other than what follows from the above.
Results may differ from a plain program's by a relative error of at most 0.014.
Values may be sent and summed in bfloat16 or wider, within the bound.
A program may use at most 128 MiB of HBM per device.

v0:
```python
import math

import jax
import jax.numpy as jnp
import numpy as np
from jax import lax
from jax.experimental import pallas as pl
from jax.experimental.pallas import tpu as pltpu
from jax.sharding import PartitionSpec as P

C = 256
OBS = 1024
TE = 128
TH = 512
ADIM = 10
FR = 16
LEVELS = 40
ADAM_STEP = 7
Q = 12627
SAM = 16
ROWS = 32
NB = 36

sigma_top = 80.0 ** (1.0 / 7.0)
sigma_low = 0.002 ** (1.0 / 7.0)
clip_limit = 1.0
learn_rate = 0.02
decay_first = 0.5
decay_second = 0.5
adam_eps = 1e-08
weight_decay = 0.01
norm_eps = 1e-05

f32 = jnp.float32
bf16 = jnp.bfloat16

AT_DOWN_RES = 1330
AT_TAIL = 12604
TAIL = 23
AT_FILM = (1340, 2492, 9788, 10940)
AT_TIME = (12092, 12348)
AT_UP_RES = 9276
B_MISC, B_INNER, B_OUTER, B_FILM = 0, 1, 2, 3
B_DS, B_POOL, B_SPREAD, B_UF, B_US, B_UR = 5, 10, 13, 17, 27, 32
LANE_TAIL = 64
CONVS = (
    (50, 5, 2, lambda t, h: B_DS + t),
    (5436, 5, 4, lambda t, h: B_UF + 2 * t + h // 2),
    (7996, 5, 2, lambda t, h: B_US + t),
    (3644, 3, 2, lambda t, h: B_POOL + t),
    (4412, 4, 2, lambda t, h: B_SPREAD + t),
)
(T_BIAS_A, T_BIAS_B, T_OUT, D_B1, D_G1, D_S1, D_FS, D_FO, D_B2, D_G2, D_S2, D_RB, PB, SB,
 U_B1, U_G1, U_S1, U_FS, U_FO, U_B2, U_G2, U_S2, U_RB) = range(TAIL)


def dot_nt(a, b):
    return lax.dot_general(a, b, (((1,), (1,)), ((), ())), preferred_element_type=f32)


def dot_nn(a, b):
    return lax.dot_general(a, b, (((1,), (0,)), ((), ())), preferred_element_type=f32)


def dot_tn(a, b):
    return lax.dot_general(a, b, (((0,), (0,)), ((), ())), preferred_element_type=f32)


def split2(v):
    high = v.astype(bf16)
    return high, (v - high.astype(f32)).astype(bf16)


def split3(v):
    high, rest = v.astype(bf16), None
    rest = v - high.astype(f32)
    mid = rest.astype(bf16)
    return high, mid, (rest - mid.astype(f32)).astype(bf16)


def tap_order(taps):
    n = 128 * taps
    row = lax.broadcasted_iota(jnp.int32, (n, n), 0)
    col = lax.broadcasted_iota(jnp.int32, (1, n), 1)
    source = (col & 127) * taps + (col >> 7)
    return jnp.where(row == source, 1.0, 0.0).astype(bf16)


def first_order():
    table = np.zeros((128, 128), np.float32)
    for i in range(ADIM):
        for t in range(5):
            table[i * 5 + t, t * ADIM + i] = 1.0
    return table


def level_table():
    levels = np.arange(LEVELS, dtype=np.float64)
    tau = 250.0 * 7.0 * np.log(sigma_top + levels / (LEVELS - 1) * (sigma_low - sigma_top))
    freq = np.exp(-math.log(10000.0) * np.arange(TE // 2) / (TE // 2 - 1))
    angles = tau[:, None] * freq[None, :]
    table = np.zeros((64, TE), np.float32)
    table[:LEVELS] = np.concatenate([np.sin(angles), np.cos(angles)], axis=1)
    return table


def pack_kernel(params_ref, order_ref, own_ref, film_ref):
    def low(start, width):
        return params_ref[:, start : start + width].astype(bf16)

    first = dot_nn(low(0, 128), order_ref[...])
    pieces = [
        first[:, :50],
        params_ref[:, AT_DOWN_RES : AT_DOWN_RES + ADIM],
        jnp.zeros((ROWS, LANE_TAIL - 60), f32),
        params_ref[:, AT_TAIL : AT_TAIL + TAIL],
        jnp.zeros((ROWS, 256 - LANE_TAIL - TAIL), f32),
    ]
    own_ref[B_MISC] = jnp.concatenate(pieces, axis=1).astype(bf16)
    own_ref[B_INNER] = low(AT_TIME[0], 256)
    own_ref[B_OUTER] = low(AT_TIME[1], 256)
    for q in range(4):
        film_ref[q * ROWS : (q + 1) * ROWS] = low(AT_FILM[q], OBS)
        own_ref[B_FILM + q // 2, :, (q % 2) * 128 : (q % 2) * 128 + 128] = low(AT_FILM[q] + OBS, TE)
    own_ref[B_UR] = low(AT_UP_RES, 256)
    own_ref[B_UR + 1] = low(AT_UP_RES + 256, 256)
    own_ref[NB - 2] = jnp.zeros((ROWS, 256), bf16)
    own_ref[NB - 1] = jnp.zeros((ROWS, 256), bf16)
    for taps in (5, 3, 4):
        places = [(at, h, block) for at, k, groups, block in CONVS if k == taps for h in range(groups)]
        stacked = jnp.concatenate([low(at + h * 128 * taps, 128 * taps) for at, h, _ in places], axis=0)
        moved = dot_nn(stacked, tap_order(taps)).astype(bf16)
        for n, (_, h, block) in enumerate(places):
            for t in range(taps):
                own_ref[block(t, h), :, (h % 2) * 128 : (h % 2) * 128 + 128] = moved[
                    n * ROWS : (n + 1) * ROWS, t * 128 : (t + 1) * 128
                ]


def pack(params):
    vmem = pl.BlockSpec(memory_space=pltpu.VMEM)
    return pl.pallas_call(
        pack_kernel,
        out_shape=(
            jax.ShapeDtypeStruct((NB, ROWS, 256), bf16),
            jax.ShapeDtypeStruct((4 * ROWS, OBS), bf16),
        ),
        in_specs=[vmem, vmem],
        out_specs=(vmem, vmem),
        compiler_params=pltpu.CompilerParams(vmem_limit_bytes=40 << 20),
        name="pack",
    )(params, jnp.asarray(first_order(), bf16))


def mish_parts(v):
    e = jnp.exp(jnp.minimum(v, 20.0))
    n = e * (e + 2.0)
    r = 1.0 / (n + 2.0)
    t = n * r
    return v * t, t + 4.0 * v * (e * r) * ((e + 1.0) * r)


def step_frames(v, step):
    if step == 0:
        return v
    zeros = jnp.zeros((SAM * abs(step), v.shape[1]), v.dtype)
    if step > 0:
        return jnp.concatenate([v[SAM * step :], zeros], axis=0)
    return jnp.concatenate([zeros, v[: SAM * step]], axis=0)


def over_frames(v):
    return jnp.sum(v.reshape(-1, SAM, v.shape[1]), axis=0)


def each_frame(v, s):
    return v.reshape(-1, SAM, v.shape[1]), s[None]


def group_means(values, ones):
    parts = [p for v in values for p in split3(v)]
    sums = dot_nn(jnp.concatenate(parts, axis=0), ones)
    out = []
    for i in range(len(values)):
        a, b, c = (sums[(3 * i + k) * SAM : (3 * i + k + 1) * SAM] for k in range(3))
        out.append((a + (b + c)) * (1.0 / (32 * FR)))
    return out


def minus(v, s):
    a, b = each_frame(v, s)
    return (a - b).reshape(v.shape)


def times(v, s):
    a, b = each_frame(v, s)
    return (a * b).reshape(v.shape)


def plus(v, s):
    a, b = each_frame(v, s)
    return (a + b).reshape(v.shape)


def norm_forward(before, gain, shift, ones):
    (center,) = group_means([over_frames(before)], ones)
    away = minus(before, center)
    (spread,) = group_means([over_frames(away * away)], ones)
    scale = lax.rsqrt(spread + norm_eps)
    normal = times(away, scale)
    act, slope = mish_parts(normal * gain + shift)
    return act, normal, slope, scale


def norm_backward(grad_act, normal, slope, scale, gain, ones):
    grad_out = grad_act * slope
    shift_rows = over_frames(grad_out)
    gain_rows = over_frames(grad_out * normal)
    mean_grad, mean_both = group_means([shift_rows * gain, gain_rows * gain], ones)
    inner = minus(grad_out * gain, mean_grad) - times(normal, mean_both)
    return (
        times(inner, scale),
        jnp.sum(gain_rows, axis=0, keepdims=True),
        jnp.sum(shift_rows, axis=0, keepdims=True),
    )


def conv_forward(source, weight):
    total = dot_nt(step_frames(source, -2), weight(0))
    for t in range(1, 5):
        total = total + dot_nt(step_frames(source, t - 2), weight(t))
    return total


def conv_source(grad_low, weight):
    total = dot_nn(step_frames(grad_low, 2), weight(0))
    for t in range(1, 5):
        total = total + dot_nn(step_frames(grad_low, 2 - t), weight(t))
    return total


def row_sum(v):
    return jnp.sum(over_frames(v), axis=0, keepdims=True)


def halves(v):
    cube = v.reshape(FR // 2, 2, SAM, v.shape[1])
    return cube[:, 0].reshape(-1, v.shape[1]), cube[:, 1].reshape(-1, v.shape[1])


def interleave(even, odd):
    width = even.shape[1]
    pair = [v.reshape(FR // 2, 1, SAM, width) for v in (even, odd)]
    return jnp.concatenate(pair, axis=1).reshape(FR * SAM, width)


def train_kernel(
    w_ref, seen_ref, slot_ref, noisy_ref, mask_ref, level_ref, cot_ref, table_ref,
    act_ref, noisy_grad_ref, grad_ref, film_grad_ref,
):
    iota = lambda shape, dim: lax.broadcasted_iota(jnp.int32, shape, dim)
    row = iota((256, 256), 0)
    col = iota((256, 256), 1)
    ones = jnp.where((row >> 5) == (col >> 5), 1.0, 0.0).astype(bf16)
    swap = jnp.where(col == ((row & 15) << 4) + (row >> 4), 1.0, 0.0).astype(bf16)
    misc = w_ref[B_MISC, :, :128]
    lane = iota((256, 128), 1)
    misc_first = jnp.where(lane < 50, misc, jnp.zeros_like(misc))
    misc_res = jnp.where((lane >= 50) & (lane < 60), misc, jnp.zeros_like(misc))
    singles = misc.astype(f32).T[LANE_TAIL : LANE_TAIL + 32]
    vec = lambda k: singles[k : k + 1]

    at_level = jnp.where(iota((64, SAM), 0) == level_ref[...], 1.0, 0.0).astype(bf16)
    feats = dot_tn(at_level, table_ref[...]).astype(bf16)
    inner = [w_ref[B_INNER, :, j * 128 : (j + 1) * 128] for j in range(2)]
    outer = [w_ref[B_OUTER, :, j * 128 : (j + 1) * 128] for j in range(2)]
    film_time = [w_ref[B_FILM + q // 2, :, (q % 2) * 128 : (q % 2) * 128 + 128] for q in range(4)]
    hidden = [mish_parts(dot_nt(feats, inner[j]) + vec(T_BIAS_A + j)) for j in range(2)]
    hidden_low = [h[0].astype(bf16) for h in hidden]
    embed = dot_nn(hidden_low[0], outer[0]) + dot_nn(hidden_low[1], outer[1]) + vec(T_OUT)[:, :TE]
    cond, cond_slope = mish_parts(embed)
    cond_low = cond.astype(bf16)
    at_slot = jnp.where(iota((SAM, SAM), 0) == slot_ref[...], 1.0, 0.0).astype(bf16)
    seen_parts = split3(seen_ref[...])
    seen_film = sum(dot_tn(at_slot, part) for part in seen_parts)
    film = [
        seen_film[:, q * C : (q + 1) * C] + dot_nt(cond_low, film_time[q]) + vec((D_FS, D_FO, U_FS, U_FO)[q])
        for q in range(4)
    ]

    spread_mask = jnp.where((iota((SAM, 256), 1) >> 4) == iota((SAM, 256), 0), 1.0, 0.0).astype(bf16)
    keep = dot_nn(mask_ref[...].astype(f32).astype(bf16), spread_mask)
    start_cols = noisy_ref[...].astype(f32) * keep
    start_cols = jnp.concatenate([start_cols, jnp.zeros((6, 256), f32)], axis=0).astype(bf16)
    start = dot_nt(swap, start_cols).astype(bf16)
    lane16 = iota((16, 128), 1)
    row16 = iota((16, 128), 0)
    inputs = jnp.zeros((256, 128), f32)
    for t in range(5):
        place = lane16 == row16 + t * ADIM
        if t == 2:
            place = place | (lane16 == row16 + 50)
        place = place & (row16 < ADIM)
        inputs = inputs + dot_nn(step_frames(start, t - 2), jnp.where(place, 1.0, 0.0).astype(bf16))
    inputs = inputs.astype(bf16)
    pre = dot_nt(inputs, misc_first) + vec(D_B1)
    act_one, normal_one, slope_one, scale_one = norm_forward(pre, vec(D_G1), vec(D_S1), ones)
    mid_one = plus(times(act_one, film[0]), film[1]).astype(bf16)
    down = lambda t: w_ref[B_DS + t]
    pre = conv_forward(mid_one, down) + vec(D_B2)
    act, normal_two, slope_two, scale_two = norm_forward(pre, vec(D_G2), vec(D_S2), ones)
    skip = (act + dot_nt(inputs, misc_res) + vec(D_RB)).astype(bf16)
    even, odd = halves(skip)
    odd_prev = step_frames(odd, -1)
    pool_sources = (odd_prev, even, odd)
    pooled = sum(dot_nt(s, w_ref[B_POOL + t]) for t, s in enumerate(pool_sources)) + vec(PB)
    pooled = pooled.astype(bf16)
    pooled_prev = step_frames(pooled, -1)
    pooled_next = step_frames(pooled, 1)
    even_out = dot_nt(pooled, w_ref[B_SPREAD + 1]) + dot_nt(pooled_prev, w_ref[B_SPREAD + 3])
    odd_out = dot_nt(pooled_next, w_ref[B_SPREAD]) + dot_nt(pooled, w_ref[B_SPREAD + 2])
    wide = (interleave(even_out, odd_out) + vec(SB)).astype(bf16)
    joined = (wide, skip)
    up_first = [lambda t, h=h: w_ref[B_UF + 2 * t + h] for h in range(2)]
    pre = conv_forward(wide, up_first[0]) + conv_forward(skip, up_first[1]) + vec(U_B1)
    act_three, normal_three, slope_three, scale_three = norm_forward(pre, vec(U_G1), vec(U_S1), ones)
    mid_three = plus(times(act_three, film[2]), film[3]).astype(bf16)
    up = lambda t: w_ref[B_US + t]
    pre = conv_forward(mid_three, up) + vec(U_B2)
    act, normal_four, slope_four, scale_four = norm_forward(pre, vec(U_G2), vec(U_S2), ones)
    result = act + dot_nt(wide, w_ref[B_UR]) + dot_nt(skip, w_ref[B_UR + 1]) + vec(U_RB)
    act_ref[...] = dot_tn(result.astype(bf16), swap).astype(bf16)

    single_grads = {}

    def conv_weights(grad_low, source, block):
        turned = grad_low.T
        for t in range(5):
            grad_ref[block(t)] = dot_nn(turned, step_frames(source, t - 2)).astype(bf16)

    cot_high, cot_low = split2(cot_ref[...])
    upstream = dot_nt(swap, cot_high) + dot_nt(swap, cot_low)
    grad, single_grads[U_G2], single_grads[U_S2] = norm_backward(
        upstream, normal_four, slope_four, scale_four, vec(U_G2), ones
    )
    single_grads[U_B2] = row_sum(grad)
    low = grad.astype(bf16)
    conv_weights(low, mid_three, lambda t: B_US + t)
    grad_mid = conv_source(low, up)
    shift_three = over_frames(grad_mid)
    gain_three = over_frames(grad_mid * act_three)
    grad, single_grads[U_G1], single_grads[U_S1] = norm_backward(
        times(grad_mid, film[2]), normal_three, slope_three, scale_three, vec(U_G1), ones
    )
    single_grads[U_B1] = row_sum(grad)
    low = grad.astype(bf16)
    for h in range(2):
        conv_weights(low, joined[h], lambda t, h=h: B_UF + 2 * t + h)
    single_grads[U_RB] = row_sum(upstream)
    upstream_low = upstream.astype(bf16)
    turned = upstream_low.T
    for h in range(2):
        grad_ref[B_UR + h] = dot_nn(turned, joined[h]).astype(bf16)
    grad_wide = conv_source(low, up_first[0]) + dot_nn(upstream_low, w_ref[B_UR])
    grad_skip = conv_source(low, up_first[1]) + dot_nn(upstream_low, w_ref[B_UR + 1])
    single_grads[SB] = row_sum(grad_wide)
    low_even, low_odd = halves(grad_wide.astype(bf16))
    turned_even, turned_odd = low_even.T, low_odd.T
    grad_ref[B_SPREAD] = dot_nn(turned_odd, pooled_next).astype(bf16)
    grad_ref[B_SPREAD + 1] = dot_nn(turned_even, pooled).astype(bf16)
    grad_ref[B_SPREAD + 2] = dot_nn(turned_odd, pooled).astype(bf16)
    grad_ref[B_SPREAD + 3] = dot_nn(turned_even, pooled_prev).astype(bf16)
    grad_pooled = dot_nn(low_even, w_ref[B_SPREAD + 1]) + dot_nn(low_odd, w_ref[B_SPREAD + 2])
    grad_pooled = grad_pooled + dot_nn(step_frames(low_even, 1), w_ref[B_SPREAD + 3])
    grad_pooled = grad_pooled + dot_nn(step_frames(low_odd, -1), w_ref[B_SPREAD])
    single_grads[PB] = row_sum(grad_pooled)
    low = grad_pooled.astype(bf16)
    turned = low.T
    for t in range(3):
        grad_ref[B_POOL + t] = dot_nn(turned, pool_sources[t]).astype(bf16)
    grad_even = dot_nn(low, w_ref[B_POOL + 1])
    grad_odd = dot_nn(low, w_ref[B_POOL + 2]) + dot_nn(step_frames(low, 1), w_ref[B_POOL])
    grad_skip = grad_skip + interleave(grad_even, grad_odd)
    single_grads[D_RB] = row_sum(grad_skip)
    skip_low = grad_skip.astype(bf16)
    misc_grad = jnp.where(lane < 50, 0.0, dot_nn(skip_low.T, inputs))
    back = dot_nn(skip_low, misc_res)
    grad, single_grads[D_G2], single_grads[D_S2] = norm_backward(
        grad_skip, normal_two, slope_two, scale_two, vec(D_G2), ones
    )
    single_grads[D_B2] = row_sum(grad)
    low = grad.astype(bf16)
    conv_weights(low, mid_one, lambda t: B_DS + t)
    grad_mid = conv_source(low, down)
    shift_one = over_frames(grad_mid)
    gain_one = over_frames(grad_mid * act_one)
    grad, single_grads[D_G1], single_grads[D_S1] = norm_backward(
        times(grad_mid, film[0]), normal_one, slope_one, scale_one, vec(D_G1), ones
    )
    single_grads[D_B1] = row_sum(grad)
    low = grad.astype(bf16)
    misc_grad = misc_grad + jnp.where(lane < 50, dot_nn(low.T, inputs), 0.0)
    back = back + dot_nn(low, misc_first)
    grad_start = back[:, 50:60]
    for t in range(5):
        grad_start = grad_start + step_frames(back[:, t * ADIM : (t + 1) * ADIM], 2 - t)
    grad_cols = sum(dot_tn(part, swap) for part in split3(jnp.concatenate([grad_start, jnp.zeros((256, 6), f32)], axis=1)))
    noisy_grad_ref[...] = grad_cols[:ADIM] * keep

    film_grads = (gain_one, shift_one, gain_three, shift_three)
    film_low = [g.astype(bf16) for g in film_grads]
    back_cond = None
    for q in range(4):
        single_grads[(D_FS, D_FO, U_FS, U_FO)[q]] = jnp.sum(film_grads[q], axis=0, keepdims=True)
        grad_ref[B_FILM + q // 2, :, (q % 2) * 128 : (q % 2) * 128 + 128] = dot_tn(film_low[q], cond_low).astype(bf16)
        part = dot_nn(film_low[q], film_time[q])
        back_cond = part if back_cond is None else back_cond + part
        film_grad_ref[:, q * C : (q + 1) * C] = dot_nn(at_slot, film_low[q]).astype(bf16)
    grad_embed = back_cond * cond_slope
    single_grads[T_OUT] = jnp.concatenate(
        [jnp.sum(grad_embed, axis=0, keepdims=True), jnp.zeros((1, C - TE), f32)], axis=1
    )
    embed_low = grad_embed.astype(bf16)
    for j in range(2):
        grad_ref[B_OUTER, :, j * 128 : (j + 1) * 128] = dot_tn(hidden_low[j], embed_low).astype(bf16)
        grad_hidden = dot_nt(embed_low, outer[j]) * hidden[j][1]
        single_grads[T_BIAS_A + j] = jnp.sum(grad_hidden, axis=0, keepdims=True)
        grad_ref[B_INNER, :, j * 128 : (j + 1) * 128] = dot_tn(grad_hidden.astype(bf16), feats).astype(bf16)
    stack = [jnp.zeros((LANE_TAIL, 256), f32)] + [single_grads[k] for k in range(TAIL)]
    stack = jnp.concatenate(stack + [jnp.zeros((128 - LANE_TAIL - TAIL, 256), f32)], axis=0)
    grad_ref[B_MISC, :, :128] = (misc_grad + stack.T).astype(bf16)
    grad_ref[B_MISC, :, 128:] = jnp.zeros((256, 128), bf16)
    for b in range(B_UR + 2, NB):
        grad_ref[b] = jnp.zeros((256, 256), bf16)


def train(weights, seen_film, slots, noisy, mask, levels, cotangent):
    vmem = pl.BlockSpec(memory_space=pltpu.VMEM)
    return pl.pallas_call(
        train_kernel,
        out_shape=(
            jax.ShapeDtypeStruct((C, 256), bf16),
            jax.ShapeDtypeStruct((ADIM, 256), f32),
            jax.ShapeDtypeStruct((NB, 256, 256), bf16),
            jax.ShapeDtypeStruct((SAM, 4 * C), bf16),
        ),
        in_specs=[vmem] * 8,
        out_specs=(vmem,) * 4,
        compiler_params=pltpu.CompilerParams(vmem_limit_bytes=48 << 20),
        name="train",
    )(weights, seen_film, slots, noisy, mask, levels, cotangent, jnp.asarray(level_table(), bf16))


def adam_kernel(
    own_ref, film_ref, square_ref, params_ref, first_ref, second_ref, order_ref,
    norm_ref, new_params_ref, new_first_ref, new_second_ref, copy_ref, grad_ref,
):
    norm = jnp.sqrt(jnp.sum(square_ref[...], axis=(0, 1), keepdims=True))
    norm_ref[...] = norm
    factor = jnp.minimum(1.0, clip_limit / (norm + 1e-06))
    misc = own_ref[B_MISC]
    first = dot_nt(misc[:, :128], order_ref[...])
    misc = misc.astype(f32)
    grad_ref[:, 0:50] = first[:, :50]
    grad_ref[:, AT_DOWN_RES : AT_DOWN_RES + ADIM] = misc[:, 50:60]
    grad_ref[:, AT_TAIL : AT_TAIL + TAIL] = misc[:, LANE_TAIL : LANE_TAIL + TAIL]
    grad_ref[:, AT_TIME[0] : AT_TIME[0] + 256] = own_ref[B_INNER].astype(f32)
    grad_ref[:, AT_TIME[1] : AT_TIME[1] + 256] = own_ref[B_OUTER].astype(f32)
    for q in range(4):
        grad_ref[:, AT_FILM[q] : AT_FILM[q] + OBS] = film_ref[q * ROWS : (q + 1) * ROWS]
        part = own_ref[B_FILM + q // 2, :, (q % 2) * 128 : (q % 2) * 128 + 128]
        grad_ref[:, AT_FILM[q] + OBS : AT_FILM[q] + OBS + TE] = part.astype(f32)
    grad_ref[:, AT_UP_RES : AT_UP_RES + 256] = own_ref[B_UR].astype(f32)
    grad_ref[:, AT_UP_RES + 256 : AT_UP_RES + 512] = own_ref[B_UR + 1].astype(f32)
    for taps in (5, 3, 4):
        places = [(at, h, block) for at, k, groups, block in CONVS if k == taps for h in range(groups)]
        stacked = jnp.concatenate(
            [
                jnp.concatenate(
                    [own_ref[block(t, h), :, (h % 2) * 128 : (h % 2) * 128 + 128] for t in range(taps)], axis=1
                )
                for _, h, block in places
            ],
            axis=0,
        )
        moved = dot_nt(stacked, tap_order(taps))
        for n, (at, h, _) in enumerate(places):
            begin = at + h * 128 * taps
            grad_ref[:, begin : begin + 128 * taps] = moved[n * ROWS : (n + 1) * ROWS]
    width = 1024
    for begin in range(0, Q, width):
        cols = slice(begin, min(begin + width, Q))
        clipped = grad_ref[:, cols] * factor
        new_first = decay_first * first_ref[:, cols] + (1.0 - decay_first) * clipped
        new_second = decay_second * second_ref[:, cols] + (1.0 - decay_second) * clipped * clipped
        first_hat = new_first * (1.0 / (1.0 - decay_first**ADAM_STEP))
        second_hat = new_second * (1.0 / (1.0 - decay_second**ADAM_STEP))
        old = params_ref[:, cols]
        new = old - learn_rate * (first_hat / (jnp.sqrt(second_hat) + adam_eps) + weight_decay * old)
        new_first_ref[:, cols] = new_first
        new_second_ref[:, cols] = new_second
        new_params_ref[:, cols] = new
        copy_ref[:, cols] = new.astype(bf16)


def adam(own, film, squares, params, first, second):
    vmem = pl.BlockSpec(memory_space=pltpu.VMEM)
    shape = jax.ShapeDtypeStruct((ROWS, Q), f32)
    return pl.pallas_call(
        adam_kernel,
        out_shape=(jax.ShapeDtypeStruct((1, 1), f32), shape, shape, shape, jax.ShapeDtypeStruct((ROWS, Q), bf16)),
        in_specs=[vmem] * 7,
        out_specs=(vmem,) * 5,
        scratch_shapes=[pltpu.VMEM((ROWS, Q), f32)],
        compiler_params=pltpu.CompilerParams(vmem_limit_bytes=56 << 20),
        name="adam",
    )(own, film, squares, params, first, second, jnp.asarray(first_order(), bf16))


def local_plain(noisy, action_mask, time_index, obs_embed, obs_slot, cotangent, params, first_moment, second_moment):
    rows = params.shape[0]
    padded = lambda v: jnp.pad(v, ((0, ROWS - rows), (0, 0))) if rows < ROWS else v
    if rows > ROWS:
        packed = [pack(params[r : r + ROWS]) for r in range(0, rows, ROWS)]
        own = jnp.concatenate([p[0] for p in packed], axis=1)
        film_own = jnp.concatenate([p[1].reshape(4, ROWS, OBS) for p in packed], axis=1)
    else:
        own, film_own = pack(padded(params))
        own = own[:, :rows]
        film_own = film_own.reshape(4, ROWS, OBS)[:, :rows]
    weights = lax.all_gather(own, "wide", axis=1, tiled=True)
    film_rows = lax.all_gather(film_own, "wide", axis=1, tiled=True).reshape(4 * C, OBS)
    seen = lax.all_gather(obs_embed, "pair", axis=0, tiled=True).reshape(-1, OBS).astype(f32)
    cond, slope = mish_parts(seen)
    cond = cond.astype(bf16)
    seen_film = dot_nt(cond, film_rows)
    act, noisy_grad, grads, film_grad = train(
        weights, seen_film, obs_slot[None], noisy[0], action_mask, time_index, cotangent[0]
    )
    film_total = lax.psum(dot_tn(film_grad, cond), ("pair", "wide")).reshape(4, C, OBS)
    back = lax.psum_scatter(
        (dot_nn(film_grad, film_rows) * slope).reshape(-1, obs_embed.shape[1], OBS),
        "pair", scatter_dimension=0, tiled=True,
    )
    total = lax.psum(grads.astype(f32), ("pair", "wide")).astype(bf16)
    squares = jnp.sum(jnp.square(total.astype(f32))) + jnp.sum(jnp.square(film_total))
    here = lax.axis_index("wide") * rows
    mine = lax.dynamic_slice_in_dim(total, here, rows, 1)
    film_mine = lax.dynamic_slice_in_dim(film_total, here, rows, 1)
    outs = []
    for r in range(0, rows, ROWS):
        take = lambda v: jnp.pad(v[:, r : r + ROWS], ((0, 0), (0, max(0, ROWS - rows)), (0, 0)))
        outs.append(
            adam(
                take(mine), take(film_mine).reshape(4 * ROWS, OBS), squares.reshape(1, 1),
                *(padded(v)[r : r + ROWS] for v in (params, first_moment, second_moment)),
            )
        )
    new = [jnp.concatenate([o[k] for o in outs], axis=0)[:rows] for k in range(1, 5)]
    return (act[None], noisy_grad[None], back, outs[0][0].reshape(()), *new)


def solution(mesh):
    in_specs = (
        P("pair", None, "wide"),
        P(None, "wide"),
        P("pair", "wide"),
        P("pair", "wide", None),
        P("wide"),
        P("pair", None, "wide"),
        P("wide", None),
        P("wide", None),
        P("wide", None),
    )
    out_specs = (
        P("pair", None, "wide"),
        P("pair", None, "wide"),
        P("pair", "wide", None),
        P(),
        P("wide", None),
        P("wide", None),
        P("wide", None),
        P("wide", None),
    )
    return jax.shard_map(local_plain, mesh=mesh, in_specs=in_specs, out_specs=out_specs, check_vma=False)
```

profile of v0, /device:TPU:0, one launch (start us, length us, event | category | flops | bytes accessed | tf_op | source)
XLA Modules:
  0.0 369.6 jit_solution(10830543633848079964)
XLA Ops:
  7.2 1.4 copy-done
  8.6 0.8 copy-done.3
  9.4 1.7 pack.1
  11.2 0.0 all-gather.3.cloned.1.call-start
  11.2 0.7 all-gather.3.cloned.1.call-update
  12.0 9.8 %all_gather.10 = bf16[4,4,1024]{2,1,0:T(4,128)(2,1)S(1)} all-gather(bf16[1,4,1024]{2,1,0:T(4,128)(2,1)} %param.15), channel_id=1, replica_groups=mesh['pair'=4,'wide'=8] {'pair'}, dimensions={0}, use_global_device_ids=true | all-gather | bytes 40960 | tf_op jit(solution)/shard_map/all_gather | solution.py:533
  21.8 0.1 fusion.1
  21.9 1.3 dynamic-slice
  23.2 20.0 %all-gather.5.cloned.1.call-done = bf16[4,256,1024]{2,1,0:T(8,128)(2,1)} async-done(((bf16[4,32,1024]{2,1,0:T(8,128)(2,1)}), bf16[4,256,1024]{2,1,0:T(8,128)(2,1)}) %all-gather.5.cloned.1.call-update) | async-done | bytes 2097168 | tf_op jit(solution)/shard_map/all_gather | solution.py:532
  43.2 2.4 fusion.10.seen_ref
  45.5 51.0 %all-gather.3.cloned.1.call-done.w_ref = bf16[36,256,256]{2,1,0:T(8,128)(2,1)} async-done(((bf16[36,32,256]{2,1,0:T(8,128)(2,1)}), bf16[36,256,256]{2,1,0:T(8,128)(2,1)}) %all-gather.3.cloned.1.call-update) | async-done | bytes 4718608 | tf_op jit(solution)/shard_map/all_gather | solution.py:531
  96.6 13.1 %train.1 = (bf16[256,256]{1,0:T(8,128)(2,1)}, f32[10,256]{1,0:T(8,128)S(1)}, bf16[36,256,256]{2,1,0:T(8,128)(2,1)S(1)}, bf16[16,1024]{1,0:T(8,128)(2,1)S(1)}) custom-call(bf16[36,256,256]{2,1,0:T(8,128)(2,1)} %all-gather.3.cloned.1.call-done.w_ref, f32[16,1024]{1,0:T(8,128)S(1)} %fusion.10.seen_ref, s32[1,16]{1,0:T(1,128)S(1)} %bitcast.20, ...), custom_call_target="tpu_custom_call" | custom-call | tf_op jit(solution)/shard_map/train/pallas_call | solution.py:439
  109.6 2.1 copy-done.1
  111.8 0.4 convolution_multiply_fusion
  112.1 2.8 fusion.3
  115.0 0.6 copy.21
  115.6 0.6 reshape.43
  116.3 225.0 %all-reduce.6 = (bf16[36,256,256]{2,1,0:T(8,128)(2,1)}, f32[1024,1024]{1,0:T(8,128)}) all-reduce(bf16[36,256,256]{2,1,0:T(8,128)(2,1)} %copy-done.1, f32[1024,1024]{1,0:T(8,128)} %fusion.3), channel_id=1, replica_groups=mesh['pair'=4,'wide'=8] {'pair','wide'}, use_global_device_ids=true, to_apply=%region_1.0 | all-reduce | flops 3407872 | bytes 17825792 | tf_op jit(solution)/shard_map/psum | solution.py:545
  341.3 5.5 %multiply_reduce_fusion = f32[]{:T(128)} fusion(bf16[36,256,256]{2,1,0:T(8,128)(2,1)} %get-tuple-element.46), kind=kLoop, calls=%fused_computation | loop fusion | flops 7077887 | bytes 4718596 | tf_op jit(solution)/shard_map/reduce_sum | solution.py:546
  346.8 1.9 constant_dynamic-slice_fusion.2.own_ref
  348.7 1.7 multiply_reduce_fusion.1
  351.7 1.9 constant_dynamic-slice_fusion.1
  353.6 7.6 %adam.1 = (f32[1,1]{1,0:T(1,128)}, f32[32,12627]{1,0:T(8,128)}, f32[32,12627]{1,0:T(8,128)}, f32[32,12627]{1,0:T(8,128)}, bf16[32,12627]{1,0:T(8,128)(2,1)}) custom-call(bf16[36,32,256]{2,1,0:T(8,128)(2,1)} %constant_dynamic-slice_fusion.2.own_ref, f32[128,1024]{1,0:T(8,128)} %bitcast.24, f32[1,1]{1,0:T(1,128)} %bitcast.9.square_ref, ...), custom_call_target="tpu_custom_call" | custom-call | tf_op jit(solution)/shard_map/adam/pallas_call | solution.py:509
  361.2 1.9 constant_dynamic-slice_fusion
  (26 shorter events, 0.2 us)
Async XLA Ops:
  7.2 36.0 %all-gather.5.cloned.1.call-start = ((), (), s32[]{:S(2)}) async-start(), calls=%async_computation.1 | async-start | bytes 2359296 | tf_op jit(solution)/shard_map/all_gather | solution.py:532
  7.2 1.4 copy-start
  8.6 0.8 copy-start.3
  9.4 87.1 %copy-start.2 = (f32[1,256,256]{2,1,0:T(8,128)S(1)}, f32[1,256,256]{2,1,0:T(8,128)}, u32[]{:S(2)}) copy-start(f32[1,256,256]{2,1,0:T(8,128)} %param.17) | copy-start | bytes 786436
  9.4 87.1 %copy-start.4 = (bf16[64,128]{1,0:T(8,128)(2,1)S(1)}, bf16[64,128]{1,0:T(8,128)(2,1)}, u32[]{:S(2)}) copy-start(bf16[64,128]{1,0:T(8,128)(2,1)} %constant.25.clone.table_ref) | copy-start | bytes 49156
  9.4 87.1 %copy-start.5 = (bf16[1,10,256]{2,1,0:T(8,128)(2,1)S(1)}, bf16[1,10,256]{2,1,0:T(8,128)(2,1)}, u32[]{:S(2)}) copy-start(bf16[1,10,256]{2,1,0:T(8,128)(2,1)} %param.12) | copy-start | bytes 15364
  9.4 87.1 %copy-start.6 = (s32[10,16]{1,0:T(8,128)S(1)}, s32[10,16]{1,0:T(8,128)}, u32[]{:S(2)}) copy-start(s32[10,16]{1,0:T(8,128)} %mask_ref.1) | copy-start | bytes 1924
  9.4 87.1 %copy-start.7 = (s32[16]{0:T(128)S(1)}, s32[16]{0:T(128)}, u32[]{:S(2)}) copy-start(s32[16]{0:T(128)} %param.16) | copy-start | bytes 196
  9.4 87.1 %copy-start.8 = (s32[1,16]{1,0:T(1,128)S(1)}, s32[1,16]{1,0:T(1,128)}, u32[]{:S(2)}) copy-start(s32[1,16]{1,0:T(1,128)} %level_ref.1) | copy-start | bytes 196
  11.2 85.3 %all-gather.3.cloned.1.call-start = ((), (), s32[]{:S(2)}) async-start(), calls=%async_computation | async-start | bytes 5308416 | tf_op jit(solution)/shard_map/all_gather | solution.py:531
  12.0 349.2 %all-reduce.5.cloned.1.call-start = ((), (), s32[]{:S(2)}) async-start(), calls=%async_computation.2 | async-start | bytes 131072
  43.2 68.6 %copy-start.9 = (bf16[4,256,1024]{2,1,0:T(8,128)(2,1)S(1)}, bf16[4,256,1024]{2,1,0:T(8,128)(2,1)}, u32[]{:S(2)}) copy-start(bf16[4,256,1024]{2,1,0:T(8,128)(2,1)} %all-gather.5.cloned.1.call-done) | copy-start | bytes 6291460
  109.6 2.1 copy-start.1
  341.3 7.5 %copy-start.10 = (f32[1024,1024]{1,0:T(8,128)S(1)}, f32[1024,1024]{1,0:T(8,128)}, u32[]{:S(2)}) copy-start(f32[1024,1024]{1,0:T(8,128)} %get-tuple-element.47) | copy-start | bytes 12582916
Sparse Core Ops, SparseCore 0:
  11.3 31.7 all-gather.4
  45.3 51.1 all-gather.2
  116.4 40.7 all-reduce.4
where the time goes:
time: 370 us
  blocking collectives  235 us (64%)
  waiting for transfers between devices  71.7 us (19%)
  Pallas kernels  22.3 us (6%)
  between operations  15.2 us (4%)
  local copies, waits for them, and re-layouts  12.7 us (3%)
  other arithmetic  7.25 us (2%)
  matrix products  5.6 us (2%)
    psum x1, blocking collectives, local_plain(): total = lax.psum(grads.astype(f32), ('pair', 'wide')).astype(bf16)  225 us
    all_gather x1, waiting for transfers between devices, local_plain(): weights = lax.all_gather(own, 'wide', axis=1, tiled=True)  51 us
    all_gather x1, waiting for transfers between devices, local_plain(): lax.all_gather(film_own, 'wide', axis=1, tiled=True).reshape(4 * C, OBS)  20 us
    pallas_call x1, Pallas kernels, train(): pl.pallas_call(train_kernel, out_shape=(jax.ShapeDtypeStruct((C, 256), bf...  13.1 us
    all_gather x1, blocking collectives, local_plain(): lax.all_gather(obs_embed, 'pair', axis=0, tiled=True).reshape(-1, OBS)  9.76 us
    unnamed x25, local copies, waits for them, and re-layouts  8.2 us
    pallas_call x1, Pallas kernels, adam(): pl.pallas_call(adam_kernel, out_shape=(jax.ShapeDtypeStruct((1, 1), f32),...  7.55 us
  transfers between devices with their start and end apart: 3, of which 2 were waited for; matrix products, arithmetic and copies ran while one was open for 4% of the time, Pallas kernels for 2%

commit v1 on v0

--- a/solution.py
+++ b/solution.py
@@ -105,6 +105,27 @@
 
 
 def pack_kernel(params_ref, order_ref, own_ref, film_ref):
+    pack_rows(params_ref, order_ref, own_ref, film_ref)
+
+
+class Blocks:
+    def __init__(self, ref):
+        self.ref = ref
+
+    def _at(self, key):
+        block, rest = (key[0], key[1:]) if isinstance(key, tuple) else (key, ())
+        return (block // 4, block % 4) + rest
+
+    def __getitem__(self, key):
+        return self.ref[self._at(key)]
+
+    def __setitem__(self, key, value):
+        self.ref[self._at(key)] = value
+
+
+def pack_rows(params_ref, order_ref, own_ref, film_ref):
+    own_ref = Blocks(own_ref)
+
     def low(start, width):
         return params_ref[:, start : start + width].astype(bf16)
 
@@ -142,7 +163,7 @@
     return pl.pallas_call(
         pack_kernel,
         out_shape=(
-            jax.ShapeDtypeStruct((NB, ROWS, 256), bf16),
+            jax.ShapeDtypeStruct((NB // 4, 4, ROWS, 256), bf16),
             jax.ShapeDtypeStruct((4 * ROWS, OBS), bf16),
         ),
         in_specs=[vmem, vmem],
@@ -281,10 +302,14 @@
     cond, cond_slope = mish_parts(embed)
     cond_low = cond.astype(bf16)
     at_slot = jnp.where(iota((SAM, SAM), 0) == slot_ref[...], 1.0, 0.0).astype(bf16)
-    seen_parts = split3(seen_ref[...])
-    seen_film = sum(dot_tn(at_slot, part) for part in seen_parts)
+    line = iota((32, SAM), 0)
+    at_line = ((line >> 3) * 4 + (line & 7) == slot_ref[...]) & ((line & 7) < 4)
+    at_line = jnp.where(at_line, 1.0, 0.0).astype(bf16)
+    seen_film = jnp.concatenate([seen_ref[:, k].reshape(32, 128) for k in range(8)], axis=1)
+    seen_film = sum(dot_tn(at_line, part) for part in split3(seen_film))
+    spans = lambda v, q: jnp.concatenate([v[:, k * 128 + q * 32 : k * 128 + q * 32 + 32] for k in range(8)], axis=1)
     film = [
-        seen_film[:, q * C : (q + 1) * C] + dot_nt(cond_low, film_time[q]) + vec((D_FS, D_FO, U_FS, U_FO)[q])
+        spans(seen_film, q) + dot_nt(cond_low, film_time[q]) + vec((D_FS, D_FO, U_FS, U_FO)[q])
         for q in range(4)
     ]
 
@@ -415,7 +440,9 @@
         grad_ref[B_FILM + q // 2, :, (q % 2) * 128 : (q % 2) * 128 + 128] = dot_tn(film_low[q], cond_low).astype(bf16)
         part = dot_nn(film_low[q], film_time[q])
         back_cond = part if back_cond is None else back_cond + part
-        film_grad_ref[:, q * C : (q + 1) * C] = dot_nn(at_slot, film_low[q]).astype(bf16)
+    at_slots = [dot_nn(at_slot, v) for v in film_low]
+    for k in range(8):
+        film_grad_ref[k] = jnp.concatenate([v[:, k * 32 : (k + 1) * 32] for v in at_slots], axis=1).astype(bf16)
     grad_embed = back_cond * cond_slope
     single_grads[T_OUT] = jnp.concatenate(
         [jnp.sum(grad_embed, axis=0, keepdims=True), jnp.zeros((1, C - TE), f32)], axis=1
@@ -442,7 +469,7 @@
             jax.ShapeDtypeStruct((C, 256), bf16),
             jax.ShapeDtypeStruct((ADIM, 256), f32),
             jax.ShapeDtypeStruct((NB, 256, 256), bf16),
-            jax.ShapeDtypeStruct((SAM, 4 * C), bf16),
+            jax.ShapeDtypeStruct((8, SAM, 128), bf16),
         ),
         in_specs=[vmem] * 8,
         out_specs=(vmem,) * 4,
@@ -522,21 +549,23 @@
     padded = lambda v: jnp.pad(v, ((0, ROWS - rows), (0, 0))) if rows < ROWS else v
     if rows > ROWS:
         packed = [pack(params[r : r + ROWS]) for r in range(0, rows, ROWS)]
-        own = jnp.concatenate([p[0] for p in packed], axis=1)
+        own = jnp.concatenate([p[0].reshape(NB, ROWS, 256) for p in packed], axis=1)
         film_own = jnp.concatenate([p[1].reshape(4, ROWS, OBS) for p in packed], axis=1)
     else:
         own, film_own = pack(padded(params))
-        own = own[:, :rows]
+        own = own.reshape(NB, ROWS, 256)[:, :rows]
         film_own = film_own.reshape(4, ROWS, OBS)[:, :rows]
     weights = lax.all_gather(own, "wide", axis=1, tiled=True)
     film_rows = lax.all_gather(film_own, "wide", axis=1, tiled=True).reshape(4 * C, OBS)
     seen = lax.all_gather(obs_embed, "pair", axis=0, tiled=True).reshape(-1, OBS).astype(f32)
     cond, slope = mish_parts(seen)
     cond = cond.astype(bf16)
-    seen_film = dot_nt(cond, film_rows)
+    seen_film = dot_nt(cond, film_rows).reshape(4, 4, 4, 8, 32).transpose(0, 3, 1, 2, 4).reshape(4, 8, 4, 128)
+    seen_film = jnp.pad(seen_film, ((0, 0), (0, 0), (0, 4), (0, 0)))
     act, noisy_grad, grads, film_grad = train(
         weights, seen_film, obs_slot[None], noisy[0], action_mask, time_index, cotangent[0]
     )
+    film_grad = film_grad.reshape(8, SAM, 4, 32).transpose(1, 2, 0, 3).reshape(SAM, 4 * C)
     film_total = lax.psum(dot_tn(film_grad, cond), ("pair", "wide")).reshape(4, C, OBS)
     back = lax.psum_scatter(
         (dot_nn(film_grad, film_rows) * slope).reshape(-1, obs_embed.shape[1], OBS),
@@ -560,6 +589,425 @@
     return (act[None], noisy_grad[None], back, outs[0][0].reshape(()), *new)
 
 
+MESH = pl.DeviceIdType.MESH
+GROUPS = 3
+EACH = NB // 4 // GROUPS
+
+
+def flipped(v, bits):
+    out = v
+    for k in range(3):
+        if bits >> k & 1:
+            bit = (v // (1 << k)) % 2
+            out = out + (1 << k) * (1 - 2 * bit)
+    return out
+
+
+class Place:
+    def __init__(self):
+        self.p = lax.axis_index("pair")
+        self.w = lax.axis_index("wide")
+        self.x, self.y = self.p % 2, self.p // 2
+        self.c, self.z = self.w % 2, self.w // 2
+
+    def line(self, l):
+        return (self.p, flipped(self.w, l))
+
+    def plane(self, k):
+        return (flipped(self.p, k), self.w)
+
+
+def meet(me):
+    barrier = pltpu.get_barrier_semaphore()
+    for l in range(1, 8):
+        pl.semaphore_signal(barrier, inc=1, device_id=me.line(l), device_id_type=MESH)
+    for k in range(1, 4):
+        pl.semaphore_signal(barrier, inc=1, device_id=me.plane(k), device_id_type=MESH)
+    pl.semaphore_wait(barrier, 10)
+
+
+def send(source, target, sems, at, device):
+    copy = pltpu.make_async_remote_copy(
+        src_ref=source, dst_ref=target, send_sem=sems[0].at[at], recv_sem=sems[1].at[at],
+        device_id=device, device_id_type=MESH,
+    )
+    copy.start()
+    return copy
+
+
+def fold_rows(v):
+    return jnp.concatenate([v[:, q * 256 : (q + 1) * 256] for q in range(4)], axis=0)
+
+
+def unfold_rows(v):
+    return jnp.concatenate([v[q * 4 : (q + 1) * 4] for q in range(4)], axis=1)
+
+
+def iota(shape, dim):
+    return lax.broadcasted_iota(jnp.int32, shape, dim)
+
+
+def one_hot(condition):
+    return jnp.where(condition, 1.0, 0.0).astype(bf16)
+
+
+def quarter_rows(parts):
+    quarter = (iota(parts[0].shape, 0) >> 2) & 3
+    return sum(jnp.where(quarter == q, part, 0.0) for q, part in enumerate(parts))
+
+
+def gather_kernel(
+    params_ref, order_ref, obs_ref,
+    w_ref, seen_ref, obs_all_ref, film_ref,
+    own_ref, film_part, film_line,
+    obs_sems, obs_sems2, part_sems, part_sems2, film_sems, film_sems2, more_sems, more_sems2,
+    z_sems, z_sems2, x_sems, x_sems2, y_sems, y_sems2, f_sems, f_sems2, c_sems, c_sems2, local_sem,
+):
+    me = Place()
+    obs_sems, part_sems, film_sems, more_sems = (
+        (obs_sems, obs_sems2), (part_sems, part_sems2), (film_sems, film_sems2), (more_sems, more_sems2)
+    )
+    z_sems, x_sems, y_sems, f_sems, c_sems = (
+        (z_sems, z_sems2), (x_sems, x_sems2), (y_sems, y_sems2), (f_sems, f_sems2), (c_sems, c_sems2)
+    )
+    obs_all_ref[me.p, me.w] = fold_rows(obs_ref[0].astype(f32)).astype(bf16)
+    meet(me)
+    obs_copies = [
+        send(obs_all_ref.at[me.p, me.w], obs_all_ref.at[me.p, me.w], obs_sems, l - 1, me.line(l)) for l in range(1, 8)
+    ]
+    pack_rows(params_ref, order_ref, own_ref, film_ref)
+    group = lambda g: pl.ds(g * EACH, EACH)
+    z_copies = [
+        [
+            send(own_ref.at[group(g), me.p], w_ref.at[group(g), me.p, me.z, me.c], z_sems, g * 3 + k - 1, me.line(2 * k))
+            for k in range(1, 4)
+        ]
+        for g in range(GROUPS)
+    ]
+    local = pltpu.make_async_copy(own_ref, w_ref.at[:, :, me.z, me.c], local_sem)
+    local.start()
+
+    for copy in obs_copies:
+        copy.wait_recv()
+    cond = mish_parts(obs_all_ref[me.p].reshape(128, 256).astype(f32))[0].astype(bf16)
+    film = quarter_rows([dot_nt(cond, film_ref[:, q * 256 : (q + 1) * 256]) for q in range(4)])
+    row, col = iota((64, 128), 0), iota((64, 128), 1)
+    gather = one_hot(((row >> 3) == (col >> 4)) & ((row & 7) == (col & 3)))
+    film = sum(dot_nn(gather, part) for part in split3(film))
+    film_part[...] = film.reshape(8, 8, 128)
+    part_copies = [
+        send(film_part.at[flipped(me.w, l)], film_line.at[me.w], part_sems, l - 1, me.line(l)) for l in range(1, 8)
+    ]
+    film_line[me.w] = film_part[me.w]
+
+    x_copies, y_copies, f_copies, c_copies = {}, {}, {}, {}
+    film_copies, more_copies = [], []
+
+    def first_hop(g):
+        for k in range(1, 4):
+            z_copies[g][k - 1].wait_recv()
+            piece = w_ref.at[group(g), me.p, flipped(me.z, k), me.c]
+            x_copies[g, k] = send(piece, piece, x_sems, g * 3 + k - 1, me.plane(1))
+            y_copies[g, k] = send(piece, piece, y_sems, g * 3 + k - 1, me.plane(2))
+
+    def second_hop(g):
+        for k in range(1, 4):
+            x_copies[g, k].wait_recv()
+            y_copies[g, k].wait_recv()
+            along_y = (g + k) % 2 == 0
+            piece = w_ref.at[group(g), flipped(me.p, 1 if along_y else 2), flipped(me.z, k), me.c]
+            f_copies[g, k] = send(piece, piece, f_sems, g * 3 + k - 1, me.plane(2 if along_y else 1))
+
+    def last_hop(g):
+        for k in range(1, 4):
+            f_copies[g, k].wait_recv()
+        piece = w_ref.at[group(g), :, :, me.c]
+        c_copies[g] = send(piece, piece, c_sems, g, me.line(1))
+
+    def film_hop():
+        for copy in part_copies:
+            copy.wait()
+        seen_ref[me.p] = film_line[...]
+        for k in range(1, 4):
+            film_copies.append(send(seen_ref.at[me.p], seen_ref.at[me.p], film_sems, k - 1, me.plane(k)))
+        for k in range(1, 4):
+            more_copies.append(send(obs_all_ref.at[me.p], obs_all_ref.at[me.p], more_sems, k - 1, me.plane(k)))
+
+    for step in range(GROUPS + 2):
+        if step < GROUPS:
+            first_hop(step)
+        if step == 0:
+            film_hop()
+        if 0 <= step - 1 < GROUPS:
+            second_hop(step - 1)
+        if 0 <= step - 2 < GROUPS:
+            if step == 2:
+                local.wait()
+            last_hop(step - 2)
+    for copy in film_copies + more_copies + list(c_copies.values()):
+        copy.wait()
+    for copy in obs_copies + [c for row in z_copies for c in row]:
+        copy.wait_send()
+    for copies in (x_copies, y_copies, f_copies):
+        for copy in copies.values():
+            copy.wait_send()
+
+
+def gather(params, obs):
+    vmem = pl.BlockSpec(memory_space=pltpu.VMEM)
+    pair = lambda n: [pltpu.SemaphoreType.DMA((n,))] * 2
+    n = 3 * GROUPS
+    return pl.pallas_call(
+        gather_kernel,
+        out_shape=(
+            jax.ShapeDtypeStruct((NB // 4, 4, 4, 2, ROWS, 256), bf16),
+            jax.ShapeDtypeStruct((4, 8, 8, 128), f32),
+            jax.ShapeDtypeStruct((4, 8, 16, 256), bf16),
+            jax.ShapeDtypeStruct((4 * ROWS, OBS), bf16),
+        ),
+        in_specs=[vmem] * 3,
+        out_specs=(vmem,) * 4,
+        scratch_shapes=[
+            pltpu.VMEM((NB // 4, 4, ROWS, 256), bf16),
+            pltpu.VMEM((8, 8, 128), f32),
+            pltpu.VMEM((8, 8, 128), f32),
+            *pair(7), *pair(7), *pair(3), *pair(3),
+            *pair(n), *pair(n), *pair(n), *pair(n), *pair(GROUPS),
+            pltpu.SemaphoreType.DMA,
+        ],
+        compiler_params=pltpu.CompilerParams(collective_id=0, has_side_effects=True, vmem_limit_bytes=56 << 20),
+        name="gather",
+    )(params, jnp.asarray(first_order(), bf16), obs)
+
+
+def scatter_kernel(
+    grad_ref, film_grad_ref, obs_all_ref, film_ref,
+    out_ref, film_out_ref, back_ref, square_ref,
+    half_ref, core_ref, x_ref, y_ref, u_ref, v_ref, z_ref, film_all, back_part, back_line, line_squares,
+    g_sems, g_sems2, h_sems, h_sems2, b_sems, b_sems2,
+    c_sems, c_sems2, x_sems, x_sems2, y_sems, y_sems2, u_sems, u_sems2, v_sems, v_sems2,
+    z_sems, z_sems2, r_sems, r_sems2, n_sems, n_sems2, m_sems, m_sems2,
+):
+    me = Place()
+    x, y, z, c = me.x, me.y, me.z, me.c
+    group = lambda g: pl.ds(g * EACH, EACH)
+    meet(me)
+    c_copies = [
+        send(grad_ref.at[group(g), :, :, 1 - c], core_ref.at[group(g)], (c_sems, c_sems2), g, me.line(1))
+        for g in range(GROUPS)
+    ]
+    film_all[me.p, me.w] = film_grad_ref[me.w]
+    g_copies = [
+        send(film_grad_ref.at[flipped(me.w, l)], film_all.at[me.p, me.w], (g_sems, g_sems2), l - 1, me.line(l))
+        for l in range(1, 8)
+    ]
+    x_copies, y_copies, u_copies, v_copies, z_copies, r_copies = {}, {}, {}, {}, {}, {}
+    low_z, high_z = pl.ds(0, 2), pl.ds(2, 2)
+
+    def core_sum(g):
+        c_copies[g].wait_recv()
+
+        def add(i, _):
+            j, q = g * EACH + i // 4, i % 4
+            total = grad_ref[j, q, :, c].astype(f32) + core_ref[j, q].astype(f32)
+            half_ref[j, q // 2, q % 2] = total.astype(bf16)
+            return 0
+
+        lax.fori_loop(0, EACH * 4, add, 0)
+        x_copies[g] = send(
+            half_ref.at[group(g), :, 1 - x, low_z], x_ref.at[group(g)], (x_sems, x_sems2), g, me.plane(1)
+        )
+        y_copies[g] = send(
+            half_ref.at[group(g), 1 - y, :, high_z], y_ref.at[group(g)], (y_sems, y_sems2), g, me.plane(2)
+        )
+
+    def first_sum(g):
+        x_copies[g].wait_recv()
+
+        def add_x(i, _):
+            j, q = g * EACH + i // 2, i % 2
+            total = half_ref[j, q, x, low_z].astype(f32) + x_ref[j, q].astype(f32)
+            half_ref[j, q, x, low_z] = total.astype(bf16)
+            return 0
+
+        lax.fori_loop(0, EACH * 2, add_x, 0)
+        y_copies[g].wait_recv()
+
+        def add_y(i, _):
+            j, q = g * EACH + i // 2, i % 2
+            total = half_ref[j, y, q, high_z].astype(f32) + y_ref[j, q].astype(f32)
+            half_ref[j, y, q, high_z] = total.astype(bf16)
+            return 0
+
+        lax.fori_loop(0, EACH * 2, add_y, 0)
+        x_copies[g].wait_send()
+        y_copies[g].wait_send()
+        u_copies[g] = send(
+            half_ref.at[group(g), 1 - y, x, low_z], u_ref.at[group(g)], (u_sems, u_sems2), g, me.plane(2)
+        )
+        v_copies[g] = send(
+            half_ref.at[group(g), y, 1 - x, high_z], v_ref.at[group(g)], (v_sems, v_sems2), g, me.plane(1)
+        )
+
+    def second_sum(g):
+        u_copies[g].wait_recv()
+        v_copies[g].wait_recv()
+        for j in range(g * EACH, (g + 1) * EACH):
+            total = half_ref[j, y, x, low_z].astype(f32) + u_ref[j].astype(f32)
+            half_ref[j, y, x, low_z] = total.astype(bf16)
+            total = half_ref[j, y, x, high_z].astype(f32) + v_ref[j].astype(f32)
+            half_ref[j, y, x, high_z] = total.astype(bf16)
+        for k in range(1, 4):
+            z_copies[g, k] = send(
+                half_ref.at[group(g), y, x, flipped(z, k)], z_ref.at[k - 1, group(g)],
+                (z_sems, z_sems2), g * 3 + k - 1, me.line(2 * k),
+            )
+
+    squares = []
+
+    def last_sum(g):
+        for k in range(1, 4):
+            z_copies[g, k].wait_recv()
+        for j in range(g * EACH, (g + 1) * EACH):
+            total = half_ref[j, y, x, z].astype(f32)
+            for k in range(3):
+                total = total + z_ref[k, j].astype(f32)
+            total = total.astype(bf16)
+            out_ref[j, me.p] = total
+            squares.append(jnp.sum(jnp.square(total.astype(f32)).reshape(4, 8, 256), axis=0))
+        piece = out_ref.at[group(g), me.p]
+        for k in range(1, 4):
+            r_copies[g, k] = send(piece, piece, (r_sems, r_sems2), g * 3 + k - 1, me.plane(k))
+
+    h_copies, b_copies = [], []
+
+    def film_line():
+        for copy in g_copies:
+            copy.wait()
+        piece = film_all.at[me.p]
+        for k in range(1, 4):
+            h_copies.append(send(piece, piece, (h_sems, h_sems2), k - 1, me.plane(k)))
+
+    def film_plane():
+        for copy in h_copies:
+            copy.wait()
+        copies = [film_all[k].reshape(128, 128) for k in range(4)]
+        row, col = iota((128, 512), 0), iota((128, 512), 1)
+        same = ((row >> 4) == ((col >> 4) & 7)) & (((row >> 2) & 3) == (col >> 7)) & ((row & 3) == (col & 3))
+        seen_all = obs_all_ref[...].reshape(512, 256)
+        for q in range(4):
+            pick = one_hot(same & (((col >> 2) & 3) == q))
+            cond = mish_parts(dot_nn(pick, seen_all))[0].astype(bf16)
+            total = sum(dot_tn(piece, cond) for piece in copies)
+            film_out_ref[:, q * 256 : (q + 1) * 256] = total
+        row, col = iota((128, 128), 0), iota((128, 128), 1)
+        mine = one_hot(((row >> 4) == (col >> 4)) & ((col & 15) == 4 * me.p + (row & 3)))
+        rows = [dot_nn(mine, piece).astype(bf16) for piece in copies]
+        parts = [sum(dot_nn(r, film_ref[:, q * 256 : (q + 1) * 256]) for r in rows) for q in range(4)]
+        back_part[...] = quarter_rows(parts).astype(bf16).reshape(8, 16, 256)
+        for l in range(1, 8):
+            b_copies.append(
+                send(back_part.at[flipped(me.w, l)], back_line.at[me.w], (b_sems, b_sems2), l - 1, me.line(l))
+            )
+        back_line[me.w] = back_part[me.w]
+
+    def film_back():
+        for copy in b_copies:
+            copy.wait()
+        total = jnp.sum(back_line[...].astype(f32), axis=0)
+        slope = mish_parts(obs_all_ref[me.p, me.w].astype(f32))[1]
+        back_ref[0] = unfold_rows(total * slope)
+
+    for step in range(GROUPS + 3):
+        if step < GROUPS:
+            core_sum(step)
+        if step == 0:
+            film_line()
+        if 0 <= step - 1 < GROUPS:
+            first_sum(step - 1)
+        if step == 1:
+            film_plane()
+        if 0 <= step - 2 < GROUPS:
+            second_sum(step - 2)
+        if step == 2:
+            film_back()
+        if 0 <= step - 3 < GROUPS:
+            last_sum(step - 3)
+
+    film_square = jnp.zeros((8, 256), f32)
+    for q in range(4):
+        part = jnp.square(film_out_ref[:, q * 256 : (q + 1) * 256])
+        film_square = film_square + jnp.sum(part.reshape(16, 8, 256), axis=0)
+    total = sum(squares) + 0.25 * film_square
+    line_squares[me.p, me.w] = total[:, :128] + total[:, 128:]
+    m_copies = [
+        send(line_squares.at[me.p, me.w], line_squares.at[me.p, me.w], (m_sems, m_sems2), l - 1, me.line(l))
+        for l in range(1, 8)
+    ]
+    for copy in m_copies:
+        copy.wait()
+    n_copies = [
+        send(line_squares.at[me.p], line_squares.at[me.p], (n_sems, n_sems2), k - 1, me.plane(k)) for k in range(1, 4)
+    ]
+    for copy in n_copies + list(r_copies.values()):
+        copy.wait()
+    square_ref[...] = jnp.sum(line_squares[...].reshape(32, 8, 128), axis=0)
+    for copies in (u_copies, v_copies, z_copies):
+        for copy in copies.values():
+            copy.wait_send()
+    for copy in c_copies:
+        copy.wait_send()
+
+
+def scatter(grads, film_grad, obs_all, film_own):
+    vmem = pl.BlockSpec(memory_space=pltpu.VMEM)
+    pair = lambda n: [pltpu.SemaphoreType.DMA((n,))] * 2
+    n = NB // 4
+    return pl.pallas_call(
+        scatter_kernel,
+        out_shape=(
+            jax.ShapeDtypeStruct((n, 4, ROWS, 256), bf16),
+            jax.ShapeDtypeStruct((4 * ROWS, OBS), f32),
+            jax.ShapeDtypeStruct((1, 4, OBS), f32),
+            jax.ShapeDtypeStruct((8, 128), f32),
+        ),
+        in_specs=[vmem] * 4,
+        out_specs=(vmem,) * 4,
+        scratch_shapes=[
+            pltpu.VMEM((n, 2, 2, 4, ROWS, 256), bf16),
+            pltpu.VMEM((n, 4, 4, ROWS, 256), bf16),
+            pltpu.VMEM((n, 2, 2, ROWS, 256), bf16),
+            pltpu.VMEM((n, 2, 2, ROWS, 256), bf16),
+            pltpu.VMEM((n, 2, ROWS, 256), bf16),
+            pltpu.VMEM((n, 2, ROWS, 256), bf16),
+            pltpu.VMEM((3, n, ROWS, 256), bf16),
+            pltpu.VMEM((4, 8, 16, 128), bf16),
+            pltpu.VMEM((8, 16, 256), bf16),
+            pltpu.VMEM((8, 16, 256), bf16),
+            pltpu.VMEM((4, 8, 8, 128), f32),
+            *pair(7), *pair(3), *pair(7),
+            *pair(GROUPS), *pair(GROUPS), *pair(GROUPS), *pair(GROUPS), *pair(GROUPS),
+            *pair(3 * GROUPS), *pair(3 * GROUPS), *pair(3), *pair(7),
+        ],
+        compiler_params=pltpu.CompilerParams(collective_id=1, has_side_effects=True, vmem_limit_bytes=56 << 20),
+        name="scatter",
+    )(grads, film_grad, obs_all, film_own)
+
+
+def local_fast(noisy, action_mask, time_index, obs_embed, obs_slot, cotangent, params, first_moment, second_moment):
+    weights, seen_film, obs_all, film_own = gather(params, obs_embed)
+    act, noisy_grad, grads, film_grad = train(
+        weights.reshape(NB, C, 256), seen_film.reshape(4, 8, 8, 128), obs_slot[None], noisy[0], action_mask, time_index, cotangent[0]
+    )
+    total, film_total, back, squares = scatter(
+        grads.reshape(NB // 4, 4, 4, 2, ROWS, 256), film_grad, obs_all, film_own
+    )
+    norm, *new = adam(
+        total.reshape(NB, ROWS, 256), film_total, squares, params, first_moment, second_moment
+    )
+    return (act[None], noisy_grad[None], back, norm.reshape(()), *new)
+
+
 def solution(mesh):
     in_specs = (
         P("pair", None, "wide"),
@@ -582,4 +1030,5 @@
         P("wide", None),
         P("wide", None),
     )
-    return jax.shard_map(local_plain, mesh=mesh, in_specs=in_specs, out_specs=out_specs, check_vma=False)
+    fast = mesh.shape["pair"] == 4 and mesh.shape["wide"] == 8
+    return jax.shard_map(local_fast if fast else local_plain, mesh=mesh, in_specs=in_specs, out_specs=out_specs, check_vma=False)

time: 370 us -> 121 us (0.33)
  blocking collectives: 235 us -> 0 us
  Pallas kernels: 22.3 us -> 115 us
  waiting for transfers between devices: 71.7 us -> 0 us
  between operations: 15.2 us -> 0.78 us
  local copies, waits for them, and re-layouts: 12.7 us -> 4.88 us
  other arithmetic: 7.25 us -> 0 us
  matrix products: 5.6 us -> 0 us
    psum x1 -> x0, blocking collectives: 225 us -> none  [local_plain(): total = lax.psum(grads.astype(f32), ('pair', 'wide')).astype(bf16)]
    pallas_call x1 -> x2, Pallas kernels: 1.74 us -> 94.3 us  [the longest x1 47.2 us: gather(): pl.pallas_call(gather_kernel, out_shape=(jax.ShapeDtypeStruct((NB // 4, 4...]
    all_gather x2 -> x0, waiting for transfers between devices: 71 us -> none  [the longest x1 51 us: local_plain(): weights = lax.all_gather(own, 'wide', axis=1, tiled=True)]
    all_gather x1 -> x0, blocking collectives: 9.76 us -> none  [local_plain(): lax.all_gather(obs_embed, 'pair', axis=0, tiled=True).reshape(-1, OBS)]
    reduce_sum x2 -> x0, other arithmetic: 7.19 us -> none  [the longest x1 5.52 us: local_plain(): jnp.sum(jnp.square(total.astype(f32))) + jnp.sum(jnp.square(film_total))]
    dot_general x3 -> x0, matrix products: 5.6 us -> none  [the longest x1 2.83 us: dot_tn(): lax.dot_general(a, b, (((0,), (0,)), ((), ())), preferred_element_type=f32)]
    dynamic_slice x2 -> x0, local copies, waits for them, and re-layouts: 3.83 us -> none  [the longest x1 1.93 us: local_plain(): mine = lax.dynamic_slice_in_dim(total, here, rows, 1)]
    unnamed x25 -> x22, local copies, waits for them, and re-layouts: 8.2 us -> 4.88 us
  transfers between devices with their start and end apart: 3 -> 0, of which waited for: 2 -> 0; matrix products, arithmetic and copies ran while one was open for 4% -> 0% of each run, Pallas kernels for 2% -> 0%
where the time goes in v1:
time: 121 us; the launch traced here: 120 us
  Pallas kernels  115 us (95%)
  local copies, waits for them, and re-layouts  4.88 us (4%)
    pallas_call x1, Pallas kernels, gather(): pl.pallas_call(gather_kernel, out_shape=(jax.ShapeDtypeStruct((NB // 4, 4...  47.2 us
    pallas_call x1, Pallas kernels, scatter(): pl.pallas_call(scatter_kernel, out_shape=(jax.ShapeDtypeStruct((n, 4, ROW...  47 us
    pallas_call x1, Pallas kernels, train(): pl.pallas_call(train_kernel, out_shape=(jax.ShapeDtypeStruct((C, 256), bf...  13 us
    pallas_call x1, Pallas kernels, adam(): pl.pallas_call(adam_kernel, out_shape=(jax.ShapeDtypeStruct((1, 1), f32),...  7.55 us
    unnamed x22, local copies, waits for them, and re-layouts  4.88 us

profile of v1, /device:TPU:0, one launch (start us, length us, event | category | flops | bytes accessed | tf_op | source)
XLA Modules:
  0.0 120.5 jit_solution(9890196229981951758)
XLA Ops:
  0.6 0.0 copy-start.4
  0.6 0.0 copy-start.1
  0.7 0.0 copy-start.7
  0.7 0.0 copy-start.8
  0.7 0.0 copy-start.6
  0.7 0.0 copy-start.5
  0.7 47.2 %gather.1 = (bf16[9,4,4,2,32,256]{5,4,3,2,1,0:T(8,128)(2,1)}, f32[4,8,8,128]{3,2,1,0:T(8,128)}, bf16[4,8,16,256]{3,2,1,0:T(8,128)(2,1)}, bf16[128,1024]{1,0:T(8,128)(2,1)}) custom-call(f32[32,12627]{1,0:T(8,128)} %params_ref.3, bf16[128,128]{1,0:T(8,128)(2,1)} %constant.4.clone.order_ref, bf16[1,4,1024]{2,1,0:T(4,128)(2,1)} %obs_ref.1), custom_call_target="tpu_custom_call" | custom-call | tf_op jit(solution)/shard_map/gather/pallas_call | solution.py:760
  47.9 0.0 copy-done.4
  48.0 0.0 copy-done.1
  48.0 0.0 copy-done.7
  48.0 0.0 copy-done.8
  48.0 0.0 copy-done.6
  48.0 0.0 copy-done.5
  48.0 0.0 copy-start.2
  48.0 0.9 copy-done.2
  48.9 13.0 %train.1 = (bf16[256,256]{1,0:T(8,128)(2,1)}, f32[10,256]{1,0:T(8,128)S(1)}, bf16[36,256,256]{2,1,0:T(8,128)(2,1)S(1)}, bf16[8,16,128]{2,1,0:T(8,128)(2,1)S(1)}) custom-call(bf16[36,256,256]{2,1,0:T(8,128)(2,1)} %bitcast.14, f32[4,8,8,128]{3,2,1,0:T(8,128)S(1)} %copy-done.2, s32[1,16]{1,0:T(1,128)S(1)} %bitcast.13, bf16[10,256]{1,0:T(8,128)(2,1)S(1)} %bitcast.12, ...), custom_call_target="tpu_custom_call" | custom-call | tf_op jit(solution)/shard_map/train/pallas_call | solution.py:466
  61.9 0.0 copy-start
  61.9 2.1 %copy-done = bf16[36,256,256]{2,1,0:T(8,128)(2,1)} copy-done((bf16[36,256,256]{2,1,0:T(8,128)(2,1)}, bf16[36,256,256]{2,1,0:T(8,128)(2,1)S(1)}, u32[]{:S(2)}) %copy-start) | copy-done | bytes 4718616
  64.1 0.6 copy-done.3
  64.7 0.6 copy.20
  65.3 47.0 %scatter.1 = (bf16[9,4,32,256]{3,2,1,0:T(8,128)(2,1)}, f32[128,1024]{1,0:T(8,128)}, f32[1,4,1024]{2,1,0:T(4,128)}, f32[8,128]{1,0:T(8,128)}) custom-call(bf16[9,4,4,2,32,256]{5,4,3,2,1,0:T(8,128)(2,1)} %bitcast.9, bf16[8,16,128]{2,1,0:T(8,128)(2,1)} %copy-done.3, bf16[4,8,16,256]{3,2,1,0:T(8,128)(2,1)} %get-tuple-element.31.obs_all_ref, ...), custom_call_target="tpu_custom_call" | custom-call | tf_op jit(solution)/shard_map/scatter/pallas_call | solution.py:966
  112.3 0.0 copy-start.9
  112.3 7.6 %adam.1 = (f32[1,1]{1,0:T(1,128)}, f32[32,12627]{1,0:T(8,128)}, f32[32,12627]{1,0:T(8,128)}, f32[32,12627]{1,0:T(8,128)}, bf16[32,12627]{1,0:T(8,128)(2,1)}) custom-call(bf16[36,32,256]{2,1,0:T(8,128)(2,1)} %bitcast.15, f32[128,1024]{1,0:T(8,128)} %get-tuple-element.35.film_ref, f32[8,128]{1,0:T(8,128)} %get-tuple-element.36.square_ref, ...), custom_call_target="tpu_custom_call" | custom-call | tf_op jit(solution)/shard_map/adam/pallas_call | solution.py:536
  119.9 0.6 copy.22
  (2 shorter events, 0.0 us)
Async XLA Ops:
  0.6 47.3 %copy-start.4 = (bf16[64,128]{1,0:T(8,128)(2,1)S(1)}, bf16[64,128]{1,0:T(8,128)(2,1)}, u32[]{:S(2)}) copy-start(bf16[64,128]{1,0:T(8,128)(2,1)} %constant.5.clone.table_ref) | copy-start | bytes 49156
  0.6 47.3 %copy-start.1 = (f32[1,256,256]{2,1,0:T(8,128)S(1)}, f32[1,256,256]{2,1,0:T(8,128)}, u32[]{:S(2)}) copy-start(f32[1,256,256]{2,1,0:T(8,128)} %param.17) | copy-start | bytes 786436
  0.7 47.3 %copy-start.7 = (s32[16]{0:T(128)S(1)}, s32[16]{0:T(128)}, u32[]{:S(2)}) copy-start(s32[16]{0:T(128)} %param.16) | copy-start | bytes 196
  0.7 47.3 %copy-start.8 = (s32[1,16]{1,0:T(1,128)S(1)}, s32[1,16]{1,0:T(1,128)}, u32[]{:S(2)}) copy-start(s32[1,16]{1,0:T(1,128)} %level_ref.1) | copy-start | bytes 196
  0.7 47.3 %copy-start.6 = (s32[10,16]{1,0:T(8,128)S(1)}, s32[10,16]{1,0:T(8,128)}, u32[]{:S(2)}) copy-start(s32[10,16]{1,0:T(8,128)} %mask_ref.1) | copy-start | bytes 1924
  0.7 47.3 %copy-start.5 = (bf16[1,10,256]{2,1,0:T(8,128)(2,1)S(1)}, bf16[1,10,256]{2,1,0:T(8,128)(2,1)}, u32[]{:S(2)}) copy-start(bf16[1,10,256]{2,1,0:T(8,128)(2,1)} %param.12) | copy-start | bytes 15364
  48.0 0.9 copy-start.2
  61.9 2.1 %copy-start = (bf16[36,256,256]{2,1,0:T(8,128)(2,1)}, bf16[36,256,256]{2,1,0:T(8,128)(2,1)S(1)}, u32[]{:S(2)}) copy-start(bf16[36,256,256]{2,1,0:T(8,128)(2,1)S(1)} %get-tuple-element.29) | copy-start | bytes 14155780
  64.1 0.6 copy-start.3
  112.3 7.6 %copy-start.9 = (f32[1,4,1024]{2,1,0:T(4,128)S(1)}, f32[1,4,1024]{2,1,0:T(4,128)}, u32[]{:S(2)}) copy-start(f32[1,4,1024]{2,1,0:T(4,128)} %get-tuple-element.60) | copy-start | bytes 49156

commit v2 on v0

--- a/solution.py
+++ b/solution.py
@@ -41,7 +41,8 @@
 AT_TIME = (12092, 12348)
 AT_UP_RES = 9276
 B_MISC, B_INNER, B_OUTER, B_FILM = 0, 1, 2, 3
-B_DS, B_POOL, B_SPREAD, B_UF, B_US, B_UR = 5, 10, 13, 17, 27, 32
+B_DS, B_POOL, B_SPREAD, B_UF, B_US, B_UR = 5, 10, 13, 18, 28, 33
+B_NONE = (17, 35)
 LANE_TAIL = 64
 CONVS = (
     (50, 5, 2, lambda t, h: B_DS + t),
@@ -78,6 +79,14 @@
     return high, mid, (rest - mid.astype(f32)).astype(bf16)
 
 
+def iota(shape, dim):
+    return lax.broadcasted_iota(jnp.int32, shape, dim)
+
+
+def one_hot(condition):
+    return jnp.where(condition, 1.0, 0.0).astype(bf16)
+
+
 def tap_order(taps):
     n = 128 * taps
     row = lax.broadcasted_iota(jnp.int32, (n, n), 0)
@@ -105,6 +114,27 @@
 
 
 def pack_kernel(params_ref, order_ref, own_ref, film_ref):
+    pack_rows(params_ref, order_ref, own_ref, film_ref)
+
+
+class Blocks:
+    def __init__(self, ref):
+        self.ref = ref
+
+    def _at(self, key):
+        block, rest = (key[0], key[1:]) if isinstance(key, tuple) else (key, ())
+        return (block // 4, block % 4) + rest
+
+    def __getitem__(self, key):
+        return self.ref[self._at(key)]
+
+    def __setitem__(self, key, value):
+        self.ref[self._at(key)] = value
+
+
+def pack_rows(params_ref, order_ref, own_ref, film_ref):
+    own_ref = Blocks(own_ref)
+
     def low(start, width):
         return params_ref[:, start : start + width].astype(bf16)
 
@@ -124,8 +154,8 @@
         own_ref[B_FILM + q // 2, :, (q % 2) * 128 : (q % 2) * 128 + 128] = low(AT_FILM[q] + OBS, TE)
     own_ref[B_UR] = low(AT_UP_RES, 256)
     own_ref[B_UR + 1] = low(AT_UP_RES + 256, 256)
-    own_ref[NB - 2] = jnp.zeros((ROWS, 256), bf16)
-    own_ref[NB - 1] = jnp.zeros((ROWS, 256), bf16)
+    for b in B_NONE:
+        own_ref[b] = jnp.zeros((ROWS, 256), bf16)
     for taps in (5, 3, 4):
         places = [(at, h, block) for at, k, groups, block in CONVS if k == taps for h in range(groups)]
         stacked = jnp.concatenate([low(at + h * 128 * taps, 128 * taps) for at, h, _ in places], axis=0)
@@ -142,7 +172,7 @@
     return pl.pallas_call(
         pack_kernel,
         out_shape=(
-            jax.ShapeDtypeStruct((NB, ROWS, 256), bf16),
+            jax.ShapeDtypeStruct((NB // 4, 4, ROWS, 256), bf16),
             jax.ShapeDtypeStruct((4 * ROWS, OBS), bf16),
         ),
         in_specs=[vmem, vmem],
@@ -254,41 +284,21 @@
     return jnp.concatenate(pair, axis=1).reshape(FR * SAM, width)
 
 
-def train_kernel(
+def train_kernel(*refs):
+    train_body(*refs, lambda point: None)
+
+
+def train_body(
     w_ref, seen_ref, slot_ref, noisy_ref, mask_ref, level_ref, cot_ref, table_ref,
-    act_ref, noisy_grad_ref, grad_ref, film_grad_ref,
+    act_ref, noisy_grad_ref, grad_ref, film_grad_ref, reach,
 ):
-    iota = lambda shape, dim: lax.broadcasted_iota(jnp.int32, shape, dim)
     row = iota((256, 256), 0)
     col = iota((256, 256), 1)
     ones = jnp.where((row >> 5) == (col >> 5), 1.0, 0.0).astype(bf16)
     swap = jnp.where(col == ((row & 15) << 4) + (row >> 4), 1.0, 0.0).astype(bf16)
-    misc = w_ref[B_MISC, :, :128]
-    lane = iota((256, 128), 1)
-    misc_first = jnp.where(lane < 50, misc, jnp.zeros_like(misc))
-    misc_res = jnp.where((lane >= 50) & (lane < 60), misc, jnp.zeros_like(misc))
-    singles = misc.astype(f32).T[LANE_TAIL : LANE_TAIL + 32]
-    vec = lambda k: singles[k : k + 1]
-
-    at_level = jnp.where(iota((64, SAM), 0) == level_ref[...], 1.0, 0.0).astype(bf16)
-    feats = dot_tn(at_level, table_ref[...]).astype(bf16)
-    inner = [w_ref[B_INNER, :, j * 128 : (j + 1) * 128] for j in range(2)]
-    outer = [w_ref[B_OUTER, :, j * 128 : (j + 1) * 128] for j in range(2)]
-    film_time = [w_ref[B_FILM + q // 2, :, (q % 2) * 128 : (q % 2) * 128 + 128] for q in range(4)]
-    hidden = [mish_parts(dot_nt(feats, inner[j]) + vec(T_BIAS_A + j)) for j in range(2)]
-    hidden_low = [h[0].astype(bf16) for h in hidden]
-    embed = dot_nn(hidden_low[0], outer[0]) + dot_nn(hidden_low[1], outer[1]) + vec(T_OUT)[:, :TE]
-    cond, cond_slope = mish_parts(embed)
-    cond_low = cond.astype(bf16)
-    at_slot = jnp.where(iota((SAM, SAM), 0) == slot_ref[...], 1.0, 0.0).astype(bf16)
-    seen_parts = split3(seen_ref[...])
-    seen_film = sum(dot_tn(at_slot, part) for part in seen_parts)
-    film = [
-        seen_film[:, q * C : (q + 1) * C] + dot_nt(cond_low, film_time[q]) + vec((D_FS, D_FO, U_FS, U_FO)[q])
-        for q in range(4)
-    ]
-
-    spread_mask = jnp.where((iota((SAM, 256), 1) >> 4) == iota((SAM, 256), 0), 1.0, 0.0).astype(bf16)
+    for b in B_NONE:
+        grad_ref[b] = jnp.zeros((256, 256), bf16)
+    spread_mask = one_hot((iota((SAM, 256), 1) >> 4) == iota((SAM, 256), 0))
     keep = dot_nn(mask_ref[...].astype(f32).astype(bf16), spread_mask)
     start_cols = noisy_ref[...].astype(f32) * keep
     start_cols = jnp.concatenate([start_cols, jnp.zeros((6, 256), f32)], axis=0).astype(bf16)
@@ -300,31 +310,72 @@
         place = lane16 == row16 + t * ADIM
         if t == 2:
             place = place | (lane16 == row16 + 50)
-        place = place & (row16 < ADIM)
-        inputs = inputs + dot_nn(step_frames(start, t - 2), jnp.where(place, 1.0, 0.0).astype(bf16))
+        inputs = inputs + dot_nn(step_frames(start, t - 2), one_hot(place & (row16 < ADIM)))
     inputs = inputs.astype(bf16)
+    cot_high, cot_low = split2(cot_ref[...])
+    upstream = dot_nt(swap, cot_high) + dot_nt(swap, cot_low)
+    upstream_low = upstream.astype(bf16)
+    at_level = one_hot(iota((64, SAM), 0) == level_ref[...])
+    feats = dot_tn(at_level, table_ref[...]).astype(bf16)
+    reach(0)
+    misc = w_ref[B_MISC, :, :128]
+    lane = iota((256, 128), 1)
+    misc_first = jnp.where(lane < 50, misc, jnp.zeros_like(misc))
+    misc_res = jnp.where((lane >= 50) & (lane < 60), misc, jnp.zeros_like(misc))
+    singles = misc.astype(f32).T[LANE_TAIL : LANE_TAIL + 32]
+    vec = lambda k: singles[k : k + 1]
+
+    inner = [w_ref[B_INNER, :, j * 128 : (j + 1) * 128] for j in range(2)]
+    outer = [w_ref[B_OUTER, :, j * 128 : (j + 1) * 128] for j in range(2)]
+    film_time = lambda q: w_ref[B_FILM + q // 2, :, (q % 2) * 128 : (q % 2) * 128 + 128]
+    hidden = [mish_parts(dot_nt(feats, inner[j]) + vec(T_BIAS_A + j)) for j in range(2)]
+    hidden_low = [h[0].astype(bf16) for h in hidden]
+    embed = dot_nn(hidden_low[0], outer[0]) + dot_nn(hidden_low[1], outer[1]) + vec(T_OUT)[:, :TE]
+    cond, cond_slope = mish_parts(embed)
+    cond_low = cond.astype(bf16)
     pre = dot_nt(inputs, misc_first) + vec(D_B1)
     act_one, normal_one, slope_one, scale_one = norm_forward(pre, vec(D_G1), vec(D_S1), ones)
+    reach(1)
+    at_slot = one_hot(iota((SAM, SAM), 0) == slot_ref[...])
+    line = iota((32, SAM), 0)
+    seen_film = jnp.concatenate([seen_ref[:, k].reshape(32, 128) for k in range(4)], axis=1)
+    seen_film = split3(seen_film)
+    sides = []
+    for side in range(2):
+        at_line = one_hot(((line >> 3) * 4 + (line & 3) == slot_ref[...]) & ((line >> 2) & 1 == side))
+        sides.append(sum(dot_tn(at_line, part) for part in seen_film))
+    seen_film = jnp.concatenate(
+        [sides[k % 2][:, (k // 2) * 128 : (k // 2) * 128 + 128] for k in range(8)], axis=1
+    )
+    spans = lambda v, q: jnp.concatenate([v[:, k * 128 + q * 32 : k * 128 + q * 32 + 32] for k in range(8)], axis=1)
+    film_of = lambda q: spans(seen_film, q) + dot_nt(cond_low, film_time(q)) + vec((D_FS, D_FO, U_FS, U_FO)[q])
+    film = [film_of(0), film_of(1)]
     mid_one = plus(times(act_one, film[0]), film[1]).astype(bf16)
+    reach(2)
     down = lambda t: w_ref[B_DS + t]
     pre = conv_forward(mid_one, down) + vec(D_B2)
     act, normal_two, slope_two, scale_two = norm_forward(pre, vec(D_G2), vec(D_S2), ones)
     skip = (act + dot_nt(inputs, misc_res) + vec(D_RB)).astype(bf16)
+    reach(3)
     even, odd = halves(skip)
     odd_prev = step_frames(odd, -1)
     pool_sources = (odd_prev, even, odd)
     pooled = sum(dot_nt(s, w_ref[B_POOL + t]) for t, s in enumerate(pool_sources)) + vec(PB)
     pooled = pooled.astype(bf16)
+    reach(4)
     pooled_prev = step_frames(pooled, -1)
     pooled_next = step_frames(pooled, 1)
     even_out = dot_nt(pooled, w_ref[B_SPREAD + 1]) + dot_nt(pooled_prev, w_ref[B_SPREAD + 3])
     odd_out = dot_nt(pooled_next, w_ref[B_SPREAD]) + dot_nt(pooled, w_ref[B_SPREAD + 2])
     wide = (interleave(even_out, odd_out) + vec(SB)).astype(bf16)
     joined = (wide, skip)
+    reach(5)
     up_first = [lambda t, h=h: w_ref[B_UF + 2 * t + h] for h in range(2)]
     pre = conv_forward(wide, up_first[0]) + conv_forward(skip, up_first[1]) + vec(U_B1)
     act_three, normal_three, slope_three, scale_three = norm_forward(pre, vec(U_G1), vec(U_S1), ones)
+    film += [film_of(2), film_of(3)]
     mid_three = plus(times(act_three, film[2]), film[3]).astype(bf16)
+    reach(6)
     up = lambda t: w_ref[B_US + t]
     pre = conv_forward(mid_three, up) + vec(U_B2)
     act, normal_four, slope_four, scale_four = norm_forward(pre, vec(U_G2), vec(U_S2), ones)
@@ -338,14 +389,17 @@
         for t in range(5):
             grad_ref[block(t)] = dot_nn(turned, step_frames(source, t - 2)).astype(bf16)
 
-    cot_high, cot_low = split2(cot_ref[...])
-    upstream = dot_nt(swap, cot_high) + dot_nt(swap, cot_low)
+    reach(7)
     grad, single_grads[U_G2], single_grads[U_S2] = norm_backward(
         upstream, normal_four, slope_four, scale_four, vec(U_G2), ones
     )
     single_grads[U_B2] = row_sum(grad)
     low = grad.astype(bf16)
     conv_weights(low, mid_three, lambda t: B_US + t)
+    turned = upstream_low.T
+    for h in range(2):
+        grad_ref[B_UR + h] = dot_nn(turned, joined[h]).astype(bf16)
+    reach(8)
     grad_mid = conv_source(low, up)
     shift_three = over_frames(grad_mid)
     gain_three = over_frames(grad_mid * act_three)
@@ -357,10 +411,7 @@
     for h in range(2):
         conv_weights(low, joined[h], lambda t, h=h: B_UF + 2 * t + h)
     single_grads[U_RB] = row_sum(upstream)
-    upstream_low = upstream.astype(bf16)
-    turned = upstream_low.T
-    for h in range(2):
-        grad_ref[B_UR + h] = dot_nn(turned, joined[h]).astype(bf16)
+    reach(9)
     grad_wide = conv_source(low, up_first[0]) + dot_nn(upstream_low, w_ref[B_UR])
     grad_skip = conv_source(low, up_first[1]) + dot_nn(upstream_low, w_ref[B_UR + 1])
     single_grads[SB] = row_sum(grad_wide)
@@ -370,6 +421,7 @@
     grad_ref[B_SPREAD + 1] = dot_nn(turned_even, pooled).astype(bf16)
     grad_ref[B_SPREAD + 2] = dot_nn(turned_odd, pooled).astype(bf16)
     grad_ref[B_SPREAD + 3] = dot_nn(turned_even, pooled_prev).astype(bf16)
+    reach(10)
     grad_pooled = dot_nn(low_even, w_ref[B_SPREAD + 1]) + dot_nn(low_odd, w_ref[B_SPREAD + 2])
     grad_pooled = grad_pooled + dot_nn(step_frames(low_even, 1), w_ref[B_SPREAD + 3])
     grad_pooled = grad_pooled + dot_nn(step_frames(low_odd, -1), w_ref[B_SPREAD])
@@ -378,6 +430,7 @@
     turned = low.T
     for t in range(3):
         grad_ref[B_POOL + t] = dot_nn(turned, pool_sources[t]).astype(bf16)
+    reach(11)
     grad_even = dot_nn(low, w_ref[B_POOL + 1])
     grad_odd = dot_nn(low, w_ref[B_POOL + 2]) + dot_nn(step_frames(low, 1), w_ref[B_POOL])
     grad_skip = grad_skip + interleave(grad_even, grad_odd)
@@ -391,6 +444,7 @@
     single_grads[D_B2] = row_sum(grad)
     low = grad.astype(bf16)
     conv_weights(low, mid_one, lambda t: B_DS + t)
+    reach(12)
     grad_mid = conv_source(low, down)
     shift_one = over_frames(grad_mid)
     gain_one = over_frames(grad_mid * act_one)
@@ -400,6 +454,18 @@
     single_grads[D_B1] = row_sum(grad)
     low = grad.astype(bf16)
     misc_grad = misc_grad + jnp.where(lane < 50, dot_nn(low.T, inputs), 0.0)
+    film_grads = (gain_one, shift_one, gain_three, shift_three)
+    film_low = [g.astype(bf16) for g in film_grads]
+    back_cond = None
+    for q in range(4):
+        single_grads[(D_FS, D_FO, U_FS, U_FO)[q]] = jnp.sum(film_grads[q], axis=0, keepdims=True)
+        grad_ref[B_FILM + q // 2, :, (q % 2) * 128 : (q % 2) * 128 + 128] = dot_tn(film_low[q], cond_low).astype(bf16)
+        part = dot_nn(film_low[q], film_time(q))
+        back_cond = part if back_cond is None else back_cond + part
+    at_slots = [dot_nn(at_slot, v) for v in film_low]
+    for k in range(8):
+        film_grad_ref[k] = jnp.concatenate([v[:, k * 32 : (k + 1) * 32] for v in at_slots], axis=1).astype(bf16)
+    reach(13)
     back = back + dot_nn(low, misc_first)
     grad_start = back[:, 50:60]
     for t in range(5):
@@ -407,15 +473,6 @@
     grad_cols = sum(dot_tn(part, swap) for part in split3(jnp.concatenate([grad_start, jnp.zeros((256, 6), f32)], axis=1)))
     noisy_grad_ref[...] = grad_cols[:ADIM] * keep
 
-    film_grads = (gain_one, shift_one, gain_three, shift_three)
-    film_low = [g.astype(bf16) for g in film_grads]
-    back_cond = None
-    for q in range(4):
-        single_grads[(D_FS, D_FO, U_FS, U_FO)[q]] = jnp.sum(film_grads[q], axis=0, keepdims=True)
-        grad_ref[B_FILM + q // 2, :, (q % 2) * 128 : (q % 2) * 128 + 128] = dot_tn(film_low[q], cond_low).astype(bf16)
-        part = dot_nn(film_low[q], film_time[q])
-        back_cond = part if back_cond is None else back_cond + part
-        film_grad_ref[:, q * C : (q + 1) * C] = dot_nn(at_slot, film_low[q]).astype(bf16)
     grad_embed = back_cond * cond_slope
     single_grads[T_OUT] = jnp.concatenate(
         [jnp.sum(grad_embed, axis=0, keepdims=True), jnp.zeros((1, C - TE), f32)], axis=1
@@ -430,8 +487,6 @@
     stack = jnp.concatenate(stack + [jnp.zeros((128 - LANE_TAIL - TAIL, 256), f32)], axis=0)
     grad_ref[B_MISC, :, :128] = (misc_grad + stack.T).astype(bf16)
     grad_ref[B_MISC, :, 128:] = jnp.zeros((256, 128), bf16)
-    for b in range(B_UR + 2, NB):
-        grad_ref[b] = jnp.zeros((256, 256), bf16)
 
 
 def train(weights, seen_film, slots, noisy, mask, levels, cotangent):
@@ -442,7 +497,7 @@
             jax.ShapeDtypeStruct((C, 256), bf16),
             jax.ShapeDtypeStruct((ADIM, 256), f32),
             jax.ShapeDtypeStruct((NB, 256, 256), bf16),
-            jax.ShapeDtypeStruct((SAM, 4 * C), bf16),
+            jax.ShapeDtypeStruct((8, SAM, 128), bf16),
         ),
         in_specs=[vmem] * 8,
         out_specs=(vmem,) * 4,
@@ -522,21 +577,23 @@
     padded = lambda v: jnp.pad(v, ((0, ROWS - rows), (0, 0))) if rows < ROWS else v
     if rows > ROWS:
         packed = [pack(params[r : r + ROWS]) for r in range(0, rows, ROWS)]
-        own = jnp.concatenate([p[0] for p in packed], axis=1)
+        own = jnp.concatenate([p[0].reshape(NB, ROWS, 256) for p in packed], axis=1)
         film_own = jnp.concatenate([p[1].reshape(4, ROWS, OBS) for p in packed], axis=1)
     else:
         own, film_own = pack(padded(params))
-        own = own[:, :rows]
+        own = own.reshape(NB, ROWS, 256)[:, :rows]
         film_own = film_own.reshape(4, ROWS, OBS)[:, :rows]
     weights = lax.all_gather(own, "wide", axis=1, tiled=True)
     film_rows = lax.all_gather(film_own, "wide", axis=1, tiled=True).reshape(4 * C, OBS)
     seen = lax.all_gather(obs_embed, "pair", axis=0, tiled=True).reshape(-1, OBS).astype(f32)
     cond, slope = mish_parts(seen)
     cond = cond.astype(bf16)
-    seen_film = dot_nt(cond, film_rows)
+    seen_film = dot_nt(cond, film_rows).reshape(4, 4, 4, 8, 32).transpose(0, 3, 1, 2, 4).reshape(4, 8, 4, 128)
+    seen_film = seen_film.reshape(4, 4, 8, 128)
     act, noisy_grad, grads, film_grad = train(
         weights, seen_film, obs_slot[None], noisy[0], action_mask, time_index, cotangent[0]
     )
+    film_grad = film_grad.reshape(8, SAM, 4, 32).transpose(1, 2, 0, 3).reshape(SAM, 4 * C)
     film_total = lax.psum(dot_tn(film_grad, cond), ("pair", "wide")).reshape(4, C, OBS)
     back = lax.psum_scatter(
         (dot_nn(film_grad, film_rows) * slope).reshape(-1, obs_embed.shape[1], OBS),
@@ -560,6 +617,507 @@
     return (act[None], noisy_grad[None], back, outs[0][0].reshape(()), *new)
 
 
+MESH = pl.DeviceIdType.MESH
+
+
+def flipped(v, bits):
+    out = v
+    for k in range(3):
+        if bits >> k & 1:
+            bit = (v // (1 << k)) % 2
+            out = out + (1 << k) * (1 - 2 * bit)
+    return out
+
+
+class Place:
+    def __init__(self):
+        self.p = lax.axis_index("pair")
+        self.w = lax.axis_index("wide")
+        self.x, self.y = self.p % 2, self.p // 2
+        self.c, self.z = self.w % 2, self.w // 2
+
+    def line(self, l):
+        return (self.p, flipped(self.w, l))
+
+    def plane(self, k):
+        return (flipped(self.p, k), self.w)
+
+
+def greet(me):
+    barrier = pltpu.get_barrier_semaphore()
+    for l in range(1, 8):
+        pl.semaphore_signal(barrier, inc=1, device_id=me.line(l), device_id_type=MESH)
+    for k in range(1, 4):
+        pl.semaphore_signal(barrier, inc=1, device_id=me.plane(k), device_id_type=MESH)
+
+
+def meet(me):
+    pl.semaphore_wait(pltpu.get_barrier_semaphore(), 10)
+
+
+def send(source, target, sems, at, device):
+    copy = pltpu.make_async_remote_copy(
+        src_ref=source, dst_ref=target, send_sem=sems[0].at[at], recv_sem=sems[1].at[at],
+        device_id=device, device_id_type=MESH,
+    )
+    copy.start()
+    return copy
+
+
+def fold_rows(v):
+    return jnp.concatenate([v[:, q * 256 : (q + 1) * 256] for q in range(4)], axis=0)
+
+
+def unfold_rows(v):
+    return jnp.concatenate([v[q * 4 : (q + 1) * 4] for q in range(4)], axis=1)
+
+
+def quarter_rows(parts):
+    quarter = (iota(parts[0].shape, 0) >> 2) & 3
+    return sum(jnp.where(quarter == q, part, 0.0) for q, part in enumerate(parts))
+
+
+class Gather:
+    def __init__(self, me, own, weights, seen, obs_all, film, film_part, film_line, sems):
+        self.me, self.own, self.weights, self.seen, self.obs_all, self.film = me, own, weights, seen, obs_all, film
+        self.film_part, self.film_line = film_part, film_line
+        (self.obs_sems, self.part_sems, self.film_sems, self.more_sems,
+         self.z_sems, self.x_sems, self.y_sems, self.f_sems, self.c_sems, self.local_sem) = sems
+        self.z, self.x, self.y, self.f, self.c = {}, {}, {}, {}, {}
+
+    def start_obs(self):
+        me = self.me
+        piece = self.obs_all.at[me.p, me.w]
+        self.obs_copies = [send(piece, piece, self.obs_sems, l - 1, me.line(l)) for l in range(1, 8)]
+
+    def start_rows(self, g):
+        me = self.me
+        for k in range(1, 4):
+            self.z[g, k] = send(
+                self.own.at[gather_group(g), me.p], self.weights.at[gather_group(g), me.p, me.z, me.c],
+                self.z_sems, g * 3 + k - 1, me.line(2 * k),
+            )
+        if g == 0:
+            self.local = pltpu.make_async_copy(self.own, self.weights.at[:, :, me.z, me.c], self.local_sem)
+            self.local.start()
+
+    def film_product(self):
+        me = self.me
+        for copy in self.obs_copies:
+            copy.wait()
+        cond = mish_parts(self.obs_all[me.p].reshape(128, 256).astype(f32))[0].astype(bf16)
+        film = quarter_rows([dot_nt(cond, self.film[:, q * 256 : (q + 1) * 256]) for q in range(4)])
+        row, col = iota((64, 128), 0), iota((64, 128), 1)
+        pick = one_hot(((row >> 3) == (col >> 4)) & ((row & 7) == (col & 3)))
+        self.film_part[...] = sum(dot_nn(pick, part) for part in split3(film)).reshape(8, 8, 128)
+        self.part_copies = [
+            send(self.film_part.at[flipped(me.w, l)], self.film_line.at[me.w], self.part_sems, l - 1, me.line(l))
+            for l in range(1, 8)
+        ]
+        self.film_line[me.w] = self.film_part[me.w]
+
+    def film_hop(self):
+        me = self.me
+        for copy in self.part_copies:
+            copy.wait()
+        for k in range(4):
+            self.seen[me.p, k] = self.film_line[2 * k] + pltpu.roll(self.film_line[2 * k + 1], 4, 0)
+        piece = self.seen.at[me.p]
+        self.film_copies = [send(piece, piece, self.film_sems, k - 1, me.plane(k)) for k in range(1, 4)]
+
+    def obs_hop(self):
+        me = self.me
+        piece = self.obs_all.at[me.p]
+        self.more_copies = [send(piece, piece, self.more_sems, k - 1, me.plane(k)) for k in range(1, 4)]
+
+    def film_done(self):
+        for copy in self.film_copies:
+            copy.wait()
+
+    def first_hop(self, g):
+        me = self.me
+        for k in range(1, 4):
+            self.z[g, k].wait_recv()
+            piece = self.weights.at[gather_group(g), me.p, flipped(me.z, k), me.c]
+            self.x[g, k] = send(piece, piece, self.x_sems, g * 3 + k - 1, me.plane(1))
+            self.y[g, k] = send(piece, piece, self.y_sems, g * 3 + k - 1, me.plane(2))
+            if g in GATHER_DIRECT:
+                self.f[g, k] = send(piece, piece, self.f_sems, g * 3 + k - 1, me.plane(3))
+
+    def second_hop(self, g):
+        me = self.me
+        for k in range(1, 4):
+            self.x[g, k].wait_recv()
+            self.y[g, k].wait_recv()
+            if g in GATHER_DIRECT:
+                continue
+            along_y = (g + k) % 2 == 0
+            piece = self.weights.at[gather_group(g), flipped(me.p, 1 if along_y else 2), flipped(me.z, k), me.c]
+            self.f[g, k] = send(piece, piece, self.f_sems, g * 3 + k - 1, me.plane(2 if along_y else 1))
+
+    def last_hop(self, g):
+        if g == 0:
+            self.local.wait()
+        if g in GATHER_DIRECT:
+            self.second_hop(g)
+        for k in range(1, 4):
+            self.f[g, k].wait_recv()
+        piece = self.weights.at[gather_group(g), :, :, self.me.c]
+        self.c[g] = send(piece, piece, self.c_sems, g, self.me.line(1))
+
+    def arrived(self, g):
+        self.c[g].wait_recv()
+
+    def finish(self):
+        for copy in self.more_copies:
+            copy.wait()
+        for copies in (self.z, self.x, self.y, self.f, self.c):
+            for copy in copies.values():
+                copy.wait_send()
+
+
+class Scatter:
+    def __init__(self, me, grad, film_grad, obs_all, film, out, film_out, back, square, buffers, sems):
+        self.me, self.grad, self.film_grad, self.obs_all, self.film = me, grad, film_grad, obs_all, film
+        self.out, self.film_out, self.back, self.square = out, film_out, back, square
+        (self.half, self.core, self.xb, self.yb, self.ub, self.vb, self.zb,
+         self.film_all, self.back_part, self.back_line, self.all_squares) = buffers
+        (self.g_sems, self.h_sems, self.b_sems, self.c_sems, self.x_sems, self.y_sems, self.u_sems, self.v_sems,
+         self.z_sems, self.r_sems, self.n_sems, self.m_sems) = sems
+        self.x, self.y, self.u, self.v, self.z, self.r, self.c = {}, {}, {}, {}, {}, {}, {}
+        self.squares = []
+
+    def start(self, g):
+        me = self.me
+        self.c[g] = send(
+            self.grad.at[group(g), :, :, 1 - me.c], self.core.at[group(g)], self.c_sems, g, me.line(1)
+        )
+
+    def core_sum(self, g):
+        me, (first, last) = self.me, GROUPS[g]
+        self.c[g].wait_recv()
+
+        def add(i, _):
+            j, q = first + i // 4, i % 4
+            total = self.grad[j, q, :, me.c].astype(f32) + self.core[j, q].astype(f32)
+            self.half[j, q // 2, q % 2] = total.astype(bf16)
+            return 0
+
+        lax.fori_loop(0, (last - first) * 4, add, 0)
+        self.x[g] = send(
+            self.half.at[group(g), :, 1 - me.x, LOW], self.xb.at[group(g)], self.x_sems, g, me.plane(1)
+        )
+        self.y[g] = send(
+            self.half.at[group(g), 1 - me.y, :, HIGH], self.yb.at[group(g)], self.y_sems, g, me.plane(2)
+        )
+
+    def first_sum(self, g):
+        me, half, (first, last) = self.me, self.half, GROUPS[g]
+        self.x[g].wait_recv()
+
+        def add_x(i, _):
+            j, q = first + i // 2, i % 2
+            total = half[j, q, me.x, LOW].astype(f32) + self.xb[j, q].astype(f32)
+            half[j, q, me.x, LOW] = total.astype(bf16)
+            return 0
+
+        lax.fori_loop(0, (last - first) * 2, add_x, 0)
+        self.u[g] = send(half.at[group(g), 1 - me.y, me.x, LOW], self.ub.at[group(g)], self.u_sems, g, me.plane(2))
+        self.y[g].wait_recv()
+
+        def add_y(i, _):
+            j, q = first + i // 2, i % 2
+            total = half[j, me.y, q, HIGH].astype(f32) + self.yb[j, q].astype(f32)
+            half[j, me.y, q, HIGH] = total.astype(bf16)
+            return 0
+
+        lax.fori_loop(0, (last - first) * 2, add_y, 0)
+        self.v[g] = send(half.at[group(g), me.y, 1 - me.x, HIGH], self.vb.at[group(g)], self.v_sems, g, me.plane(1))
+
+    def second_sum(self, g):
+        me, half = self.me, self.half
+        self.u[g].wait_recv()
+        self.v[g].wait_recv()
+        for j in range(*GROUPS[g]):
+            total = half[j, me.y, me.x, LOW].astype(f32) + self.ub[j].astype(f32)
+            half[j, me.y, me.x, LOW] = total.astype(bf16)
+            total = half[j, me.y, me.x, HIGH].astype(f32) + self.vb[j].astype(f32)
+            half[j, me.y, me.x, HIGH] = total.astype(bf16)
+        for k in range(1, 4):
+            self.z[g, k] = send(
+                half.at[group(g), me.y, me.x, flipped(me.z, k)], self.zb.at[k - 1, group(g)],
+                self.z_sems, g * 3 + k - 1, me.line(2 * k),
+            )
+
+    def last_sum(self, g):
+        me = self.me
+        for k in range(1, 4):
+            self.z[g, k].wait_recv()
+        for j in range(*GROUPS[g]):
+            total = self.half[j, me.y, me.x, me.z].astype(f32)
+            for k in range(3):
+                total = total + self.zb[k, j].astype(f32)
+            total = total.astype(bf16)
+            self.out[j, me.p] = total
+            self.squares.append(jnp.sum(jnp.square(total.astype(f32)).reshape(4, 8, 256), axis=0))
+        piece = self.out.at[group(g), me.p]
+        for k in range(1, 4):
+            self.r[g, k] = send(piece, piece, self.r_sems, g * 3 + k - 1, me.plane(k))
+
+    def film_start(self):
+        me = self.me
+        self.film_all[me.p, me.w] = self.film_grad[me.w]
+        self.g = [
+            send(self.film_grad.at[flipped(me.w, l)], self.film_all.at[me.p, me.w], self.g_sems, l - 1, me.line(l))
+            for l in range(1, 8)
+        ]
+
+    def film_hop(self):
+        me = self.me
+        for copy in self.g:
+            copy.wait()
+        piece = self.film_all.at[me.p]
+        self.h = [send(piece, piece, self.h_sems, k - 1, me.plane(k)) for k in range(1, 4)]
+
+    def film_products(self):
+        me = self.me
+        for copy in self.h:
+            copy.wait()
+        copies = [self.film_all[k].reshape(128, 128) for k in range(4)]
+        row, col = iota((128, 128), 0), iota((128, 128), 1)
+        mine = one_hot(((row >> 4) == (col >> 4)) & ((col & 15) == 4 * me.p + (row & 3)))
+        rows = [dot_nn(mine, piece).astype(bf16) for piece in copies]
+        parts = [sum(dot_nn(r, self.film[:, q * 256 : (q + 1) * 256]) for r in rows) for q in range(4)]
+        self.back_part[...] = quarter_rows(parts).astype(bf16).reshape(8, 16, 256)
+        self.b = [
+            send(self.back_part.at[flipped(me.w, l)], self.back_line.at[me.w], self.b_sems, l - 1, me.line(l))
+            for l in range(1, 8)
+        ]
+        self.back_line[me.w] = self.back_part[me.w]
+        row, col = iota((128, 512), 0), iota((128, 512), 1)
+        same = ((row >> 4) == ((col >> 4) & 7)) & (((row >> 2) & 3) == (col >> 7)) & ((row & 3) == (col & 3))
+        seen_all = self.obs_all[...].reshape(512, 256)
+        square = jnp.zeros((8, 256), f32)
+        for q in range(4):
+            pick = one_hot(same & (((col >> 2) & 3) == q))
+            cond = mish_parts(dot_nn(pick, seen_all))[0].astype(bf16)
+            total = sum(dot_tn(piece, cond) for piece in copies)
+            self.film_out[:, q * 256 : (q + 1) * 256] = total
+            square = square + jnp.sum(jnp.square(total).reshape(16, 8, 256), axis=0)
+        self.squares.append(0.25 * square)
+
+    def film_back(self):
+        me = self.me
+        for copy in self.b:
+            copy.wait()
+        total = jnp.sum(self.back_line[...].astype(f32), axis=0)
+        slope = mish_parts(self.obs_all[me.p, me.w].astype(f32))[1]
+        self.back[0] = unfold_rows(total * slope)
+
+    def norm(self):
+        me = self.me
+        total = sum(self.squares)
+        piece = self.all_squares.at[me.p, me.w]
+        self.all_squares[me.p, me.w] = total[:, :128] + total[:, 128:]
+        copies = [send(piece, piece, self.m_sems, l - 1, me.line(l)) for l in range(1, 8)]
+        for copy in copies:
+            copy.wait()
+        piece = self.all_squares.at[me.p]
+        copies = [send(piece, piece, self.n_sems, k - 1, me.plane(k)) for k in range(1, 4)]
+        for copy in copies + list(self.r.values()):
+            copy.wait()
+        self.square[...] = jnp.sum(self.all_squares[...].reshape(32, 8, 128), axis=0)
+        for copies in (self.c, self.x, self.y, self.u, self.v, self.z):
+            for copy in copies.values():
+                copy.wait_send()
+
+
+GATHER_GROUPS = ((0, 1), (1, 3), (3, 5), (5, 7), (7, 9))
+GATHER_DIRECT = (3, 4)
+GROUPS = ((0, 1), (1, 3), (3, 5), (5, 7), (7, 9))
+LOW, HIGH = pl.ds(0, 2), pl.ds(2, 2)
+
+
+def group(g):
+    return pl.ds(GROUPS[g][0], GROUPS[g][1] - GROUPS[g][0])
+
+
+def gather_group(g):
+    return pl.ds(GATHER_GROUPS[g][0], GATHER_GROUPS[g][1] - GATHER_GROUPS[g][0])
+
+
+def step_kernel(*refs):
+    (params, order, obs, slots, noisy, mask, levels, cotangent, table,
+     act, noisy_grad, back, out, film_out, square,
+     own, weights, seen, obs_all, film, film_part, film_line, grad, film_grad) = refs[:24]
+    buffers, sems = refs[24:35], refs[35:]
+    pairs = [(sems[2 * i], sems[2 * i + 1]) for i in range(21)]
+    me = Place()
+    gather = Gather(me, own, weights, seen, obs_all, film, film_part, film_line, pairs[:9] + [sems[42]])
+    scatter = Scatter(me, grad, film_grad, obs_all, film, out, film_out, back, square, buffers, pairs[9:])
+    obs_all[me.p, me.w] = fold_rows(obs[0].astype(f32)).astype(bf16)
+    greet(me)
+    pack_rows(params, order, own, film)
+    meet(me)
+    gather.start_obs()
+    gather.start_rows(0)
+    gather.start_rows(1)
+
+    def reach(point):
+        if point == 0:
+            gather.film_product()
+            gather.start_rows(2)
+            gather.start_rows(3)
+            gather.start_rows(4)
+            gather.first_hop(0)
+            gather.first_hop(1)
+            gather.second_hop(0)
+            gather.film_hop()
+            gather.first_hop(2)
+            gather.second_hop(1)
+            gather.last_hop(0)
+            gather.first_hop(3)
+            gather.second_hop(2)
+            gather.last_hop(1)
+            gather.arrived(0)
+        if point == 1:
+            gather.film_done()
+        if point == 2:
+            gather.first_hop(4)
+            gather.arrived(1)
+        if point == 3:
+            gather.last_hop(2)
+            gather.last_hop(3)
+            gather.arrived(2)
+        if point == 5:
+            gather.last_hop(4)
+            gather.arrived(3)
+        if point == 6:
+            gather.obs_hop()
+            gather.arrived(4)
+        if point == 8:
+            scatter.start(4)
+        if point == 9:
+            scatter.core_sum(4)
+            scatter.start(3)
+        if point == 10:
+            scatter.core_sum(3)
+        if point == 11:
+            scatter.start(2)
+        if point == 12:
+            scatter.core_sum(2)
+        if point == 13:
+            scatter.film_start()
+            scatter.start(1)
+
+    train_body(
+        Stacked(weights), seen, slots, noisy, mask, levels, cotangent, table,
+        act, noisy_grad, Stacked(grad), film_grad, reach,
+    )
+    scatter.start(0)
+    scatter.core_sum(1)
+    scatter.first_sum(4)
+    scatter.core_sum(0)
+    scatter.film_hop()
+    scatter.first_sum(3)
+    scatter.second_sum(4)
+    scatter.first_sum(2)
+    scatter.second_sum(3)
+    scatter.first_sum(1)
+    scatter.first_sum(0)
+    scatter.second_sum(2)
+    gather.finish()
+    scatter.film_products()
+    scatter.second_sum(1)
+    scatter.second_sum(0)
+    scatter.last_sum(4)
+    scatter.last_sum(3)
+    scatter.film_back()
+    scatter.last_sum(2)
+    scatter.last_sum(1)
+    scatter.last_sum(0)
+    scatter.norm()
+
+
+class Stacked:
+    def __init__(self, ref):
+        self.ref = ref
+
+    def _split(self, key):
+        if not isinstance(key, tuple):
+            return key, slice(None)
+        return key[0], key[2]
+
+    def __getitem__(self, key):
+        block, cols = self._split(key)
+        value = self.ref[block // 4, block % 4, :, :, :, cols]
+        return value.reshape(256, value.shape[-1])
+
+    def __setitem__(self, key, value):
+        block, cols = self._split(key)
+        self.ref[block // 4, block % 4, :, :, :, cols] = value.reshape(4, 2, ROWS, value.shape[-1])
+
+
+def step(params, obs, slots, noisy, mask, levels, cotangent):
+    vmem = pl.BlockSpec(memory_space=pltpu.VMEM)
+    pair = lambda n: [pltpu.SemaphoreType.DMA((n,))] * 2
+    n, count, parts = NB // 4, len(GROUPS), len(GATHER_GROUPS)
+    low = lambda *shape: pltpu.VMEM(shape, bf16)
+    return pl.pallas_call(
+        step_kernel,
+        out_shape=(
+            jax.ShapeDtypeStruct((C, 256), bf16),
+            jax.ShapeDtypeStruct((ADIM, 256), f32),
+            jax.ShapeDtypeStruct((1, 4, OBS), f32),
+            jax.ShapeDtypeStruct((n, 4, ROWS, 256), bf16),
+            jax.ShapeDtypeStruct((4 * ROWS, OBS), f32),
+            jax.ShapeDtypeStruct((8, 128), f32),
+        ),
+        in_specs=[vmem] * 9,
+        out_specs=(vmem,) * 6,
+        scratch_shapes=[
+            low(n, 4, ROWS, 256),
+            low(n, 4, 4, 2, ROWS, 256),
+            pltpu.VMEM((4, 4, 8, 128), f32),
+            low(4, 8, 16, 256),
+            low(4 * ROWS, OBS),
+            pltpu.VMEM((8, 8, 128), f32),
+            pltpu.VMEM((8, 8, 128), f32),
+            low(n, 4, 4, 2, ROWS, 256),
+            low(8, SAM, 128),
+            low(n, 2, 2, 4, ROWS, 256),
+            low(n, 4, 4, ROWS, 256),
+            low(n, 2, 2, ROWS, 256),
+            low(n, 2, 2, ROWS, 256),
+            low(n, 2, ROWS, 256),
+            low(n, 2, ROWS, 256),
+            low(3, n, ROWS, 256),
+            low(4, 8, 16, 128),
+            low(8, 16, 256),
+            low(8, 16, 256),
+            pltpu.VMEM((4, 8, 8, 128), f32),
+            *pair(7), *pair(7), *pair(3), *pair(3),
+            *pair(3 * parts), *pair(3 * parts), *pair(3 * parts), *pair(3 * parts), *pair(parts),
+            *pair(7), *pair(3), *pair(7),
+            *pair(count), *pair(count), *pair(count), *pair(count), *pair(count),
+            *pair(3 * count), *pair(3 * count), *pair(3), *pair(7),
+            pltpu.SemaphoreType.DMA,
+        ],
+        compiler_params=pltpu.CompilerParams(collective_id=0, has_side_effects=True, vmem_limit_bytes=60 << 20),
+        name="step",
+    )(params, jnp.asarray(first_order(), bf16), obs, slots, noisy, mask, levels, cotangent, jnp.asarray(level_table(), bf16))
+
+
+def local_fast(noisy, action_mask, time_index, obs_embed, obs_slot, cotangent, params, first_moment, second_moment):
+    act, noisy_grad, back, total, film_total, squares = step(
+        params, obs_embed, obs_slot[None], noisy[0], action_mask, time_index, cotangent[0]
+    )
+    norm, *new = adam(
+        total.reshape(NB, ROWS, 256), film_total, squares, params, first_moment, second_moment
+    )
+    return (act[None], noisy_grad[None], back, norm.reshape(()), *new)
+
+
 def solution(mesh):
     in_specs = (
         P("pair", None, "wide"),
@@ -582,4 +1140,5 @@
         P("wide", None),
         P("wide", None),
     )
-    return jax.shard_map(local_plain, mesh=mesh, in_specs=in_specs, out_specs=out_specs, check_vma=False)
+    fast = mesh.shape["pair"] == 4 and mesh.shape["wide"] == 8
+    return jax.shard_map(local_fast if fast else local_plain, mesh=mesh, in_specs=in_specs, out_specs=out_specs, check_vma=False)

time: 370 us -> 92.3 us (0.25)
  blocking collectives: 235 us -> 0 us
  waiting for transfers between devices: 71.7 us -> 0 us
  Pallas kernels: 22.3 us -> 88.8 us
  between operations: 15.2 us -> 0.65 us
  local copies, waits for them, and re-layouts: 12.7 us -> 2.6 us
  other arithmetic: 7.25 us -> 0 us
  matrix products: 5.6 us -> 0 us
    psum x1 -> x0, blocking collectives: 225 us -> none  [local_plain(): total = lax.psum(grads.astype(f32), ('pair', 'wide')).astype(bf16)]
    all_gather x2 -> x0, waiting for transfers between devices: 71 us -> none  [the longest x1 51 us: local_plain(): weights = lax.all_gather(own, 'wide', axis=1, tiled=True)]
    pallas_call x2 -> x1, Pallas kernels: 14.8 us -> 81.3 us  [step(): pl.pallas_call(step_kernel, out_shape=(jax.ShapeDtypeStruct((C, 256), bf1...]
    all_gather x1 -> x0, blocking collectives: 9.76 us -> none  [local_plain(): lax.all_gather(obs_embed, 'pair', axis=0, tiled=True).reshape(-1, OBS)]
    reduce_sum x2 -> x0, other arithmetic: 7.19 us -> none  [the longest x1 5.52 us: local_plain(): jnp.sum(jnp.square(total.astype(f32))) + jnp.sum(jnp.square(film_total))]
    unnamed x25 -> x7, local copies, waits for them, and re-layouts: 8.2 us -> 2.6 us
    dot_general x3 -> x0, matrix products: 5.6 us -> none  [the longest x1 2.83 us: dot_tn(): lax.dot_general(a, b, (((0,), (0,)), ((), ())), preferred_element_type=f32)]
    dynamic_slice x2 -> x0, local copies, waits for them, and re-layouts: 3.83 us -> none  [the longest x1 1.93 us: local_plain(): mine = lax.dynamic_slice_in_dim(total, here, rows, 1)]
  transfers between devices with their start and end apart: 3 -> 0, of which waited for: 2 -> 0; matrix products, arithmetic and copies ran while one was open for 4% -> 0% of each run, Pallas kernels for 2% -> 0%
where the time goes in v2:
time: 92.3 us; the launch traced here: 92.1 us
  Pallas kernels  88.8 us (96%)
  local copies, waits for them, and re-layouts  2.6 us (3%)
    pallas_call x1, Pallas kernels, step(): pl.pallas_call(step_kernel, out_shape=(jax.ShapeDtypeStruct((C, 256), bf1...  81.3 us
    pallas_call x1, Pallas kernels, adam(): pl.pallas_call(adam_kernel, out_shape=(jax.ShapeDtypeStruct((1, 1), f32),...  7.57 us
    unnamed x7, local copies, waits for them, and re-layouts  2.6 us

profile of v2, /device:TPU:0, one launch (start us, length us, event | category | flops | bytes accessed | tf_op | source)
XLA Modules:
  0.0 92.1 jit_solution(8199037552873146922)
XLA Ops:
  0.6 81.3 %step.1 = (bf16[256,256]{1,0:T(8,128)(2,1)}, f32[10,256]{1,0:T(8,128)}, f32[1,4,1024]{2,1,0:T(4,128)}, bf16[9,4,32,256]{3,2,1,0:T(8,128)(2,1)}, f32[128,1024]{1,0:T(8,128)}, /*index=5*/f32[8,128]{1,0:T(8,128)}) custom-call(f32[32,12627]{1,0:T(8,128)} %params_ref.1, bf16[128,128]{1,0:T(8,128)(2,1)} %constant.4.clone.refs_1_.order_ref, ...), custom_call_target="tpu_custom_call" | custom-call | tf_op jit(solution)/shard_map/step/pallas_call | solution.py:1066
  81.9 1.3 %copy.20 = f32[1,10,256]{2,0,1:T(1,128)} copy(f32[1,10,256]{2,1,0:T(8,128)} %bitcast.10) | data formatting | bytes 20480
  83.2 0.0 copy-start
  83.2 0.0 copy-start.1
  83.2 7.6 %adam.1 = (f32[1,1]{1,0:T(1,128)}, f32[32,12627]{1,0:T(8,128)}, f32[32,12627]{1,0:T(8,128)}, f32[32,12627]{1,0:T(8,128)}, bf16[32,12627]{1,0:T(8,128)(2,1)}) custom-call(bf16[36,32,256]{2,1,0:T(8,128)(2,1)} %bitcast.7, f32[128,1024]{1,0:T(8,128)} %get-tuple-element.23.film_ref, f32[8,128]{1,0:T(8,128)} %get-tuple-element.24.square_ref, ...), custom_call_target="tpu_custom_call" | custom-call | tf_op jit(solution)/shard_map/adam/pallas_call | solution.py:564
  90.8 0.0 copy-done
  90.8 0.7 copy.23
  91.5 0.0 copy-done.1
  91.5 0.6 copy.24
Async XLA Ops:
  83.2 7.6 %copy-start = (bf16[256,256]{1,0:T(8,128)(2,1)S(1)}, bf16[256,256]{1,0:T(8,128)(2,1)}, u32[]{:S(2)}) copy-start(bf16[256,256]{1,0:T(8,128)(2,1)} %get-tuple-element.19) | copy-start | bytes 393220
  83.2 8.2 %copy-start.1 = (f32[1,4,1024]{2,1,0:T(4,128)S(1)}, f32[1,4,1024]{2,1,0:T(4,128)}, u32[]{:S(2)}) copy-start(f32[1,4,1024]{2,1,0:T(4,128)} %get-tuple-element.48) | copy-start | bytes 49156

commit v3 on v2

--- a/solution.py
+++ b/solution.py
@@ -1,3 +1,4 @@
+import functools
 import math
 
 import jax
@@ -506,13 +507,10 @@
     )(weights, seen_film, slots, noisy, mask, levels, cotangent, jnp.asarray(level_table(), bf16))
 
 
-def adam_kernel(
-    own_ref, film_ref, square_ref, params_ref, first_ref, second_ref, order_ref,
-    norm_ref, new_params_ref, new_first_ref, new_second_ref, copy_ref, grad_ref,
-):
-    norm = jnp.sqrt(jnp.sum(square_ref[...], axis=(0, 1), keepdims=True))
-    norm_ref[...] = norm
-    factor = jnp.minimum(1.0, clip_limit / (norm + 1e-06))
+HALF = ROWS // 2
+
+
+def native_grads(own_ref, film_ref, order_ref, grad_ref):
     misc = own_ref[B_MISC]
     first = dot_nt(misc[:, :128], order_ref[...])
     misc = misc.astype(f32)
@@ -542,34 +540,76 @@
         for n, (at, h, _) in enumerate(places):
             begin = at + h * 128 * taps
             grad_ref[:, begin : begin + 128 * taps] = moved[n * ROWS : (n + 1) * ROWS]
+
+
+def adam_kernel(count, *refs):
+    own_ref, film_ref, square_ref, order_ref = refs[:4]
+    old_hbm, extra_in = refs[4:7], refs[7 : 7 + count]
+    norm_ref, new_hbm, extra_out = refs[7 + count], refs[8 + count : 12 + count], refs[12 + count : 12 + 2 * count]
+    grad_ref, old, new, in_sems, out_sems = refs[12 + 2 * count], refs[13 + 2 * count : 16 + 2 * count], refs[
+        16 + 2 * count : 20 + 2 * count
+    ], refs[-2], refs[-1]
+    rows = [pl.ds(h * HALF, HALF) for h in range(2)]
+    loads = [
+        [pltpu.make_async_copy(old_hbm[n].at[rows[h]], old[n].at[rows[h]], in_sems.at[h, n]) for n in range(3)]
+        for h in range(2)
+    ]
+    stores = [
+        [pltpu.make_async_copy(new[n].at[rows[h]], new_hbm[n].at[rows[h]], out_sems.at[h, n]) for n in range(4)]
+        for h in range(2)
+    ]
+    for half in loads:
+        for copy in half:
+            copy.start()
+    norm = jnp.sqrt(jnp.sum(square_ref[...], axis=(0, 1), keepdims=True))
+    norm_ref[...] = norm
+    factor = jnp.minimum(1.0, clip_limit / (norm + 1e-06))
+    for source, target in zip(extra_in, extra_out):
+        target[...] = source[...].reshape(target.shape)
+    native_grads(own_ref, film_ref, order_ref, grad_ref)
     width = 1024
-    for begin in range(0, Q, width):
-        cols = slice(begin, min(begin + width, Q))
-        clipped = grad_ref[:, cols] * factor
-        new_first = decay_first * first_ref[:, cols] + (1.0 - decay_first) * clipped
-        new_second = decay_second * second_ref[:, cols] + (1.0 - decay_second) * clipped * clipped
-        first_hat = new_first * (1.0 / (1.0 - decay_first**ADAM_STEP))
-        second_hat = new_second * (1.0 / (1.0 - decay_second**ADAM_STEP))
-        old = params_ref[:, cols]
-        new = old - learn_rate * (first_hat / (jnp.sqrt(second_hat) + adam_eps) + weight_decay * old)
-        new_first_ref[:, cols] = new_first
-        new_second_ref[:, cols] = new_second
-        new_params_ref[:, cols] = new
-        copy_ref[:, cols] = new.astype(bf16)
-
-
-def adam(own, film, squares, params, first, second):
+    for h in range(2):
+        for copy in loads[h]:
+            copy.wait()
+        for begin in range(0, Q, width):
+            at = (rows[h], slice(begin, min(begin + width, Q)))
+            clipped = grad_ref[at] * factor
+            new_first = decay_first * old[1][at] + (1.0 - decay_first) * clipped
+            new_second = decay_second * old[2][at] + (1.0 - decay_second) * clipped * clipped
+            first_hat = new_first * (1.0 / (1.0 - decay_first**ADAM_STEP))
+            second_hat = new_second * (1.0 / (1.0 - decay_second**ADAM_STEP))
+            before = old[0][at]
+            after = before - learn_rate * (first_hat / (jnp.sqrt(second_hat) + adam_eps) + weight_decay * before)
+            new[0][at] = after
+            new[1][at] = new_first
+            new[2][at] = new_second
+            new[3][at] = after.astype(bf16)
+        for copy in stores[h]:
+            copy.start()
+    for half in stores:
+        for copy in half:
+            copy.wait()
+
+
+def adam(own, film, squares, params, first, second, extras=(), extra_shapes=()):
     vmem = pl.BlockSpec(memory_space=pltpu.VMEM)
+    hbm = pl.BlockSpec(memory_space=pl.ANY)
     shape = jax.ShapeDtypeStruct((ROWS, Q), f32)
+    count = len(extras)
     return pl.pallas_call(
-        adam_kernel,
-        out_shape=(jax.ShapeDtypeStruct((1, 1), f32), shape, shape, shape, jax.ShapeDtypeStruct((ROWS, Q), bf16)),
-        in_specs=[vmem] * 7,
-        out_specs=(vmem,) * 5,
-        scratch_shapes=[pltpu.VMEM((ROWS, Q), f32)],
+        functools.partial(adam_kernel, count),
+        out_shape=(
+            jax.ShapeDtypeStruct((1, 1), f32),
+            shape, shape, shape, jax.ShapeDtypeStruct((ROWS, Q), bf16),
+            *(jax.ShapeDtypeStruct(dims, v.dtype) for dims, v in zip(extra_shapes, extras)),
+        ),
+        in_specs=[vmem] * 4 + [hbm] * 3 + [vmem] * count,
+        out_specs=(vmem,) + (hbm,) * 4 + (vmem,) * count,
+        scratch_shapes=[pltpu.VMEM((ROWS, Q), f32)] * 7
+        + [pltpu.VMEM((ROWS, Q), bf16), pltpu.SemaphoreType.DMA((2, 3)), pltpu.SemaphoreType.DMA((2, 4))],
         compiler_params=pltpu.CompilerParams(vmem_limit_bytes=56 << 20),
         name="adam",
-    )(own, film, squares, params, first, second, jnp.asarray(first_order(), bf16))
+    )(own, film, squares, jnp.asarray(first_order(), bf16), params, first, second, *extras)
 
 
 def local_plain(noisy, action_mask, time_index, obs_embed, obs_slot, cotangent, params, first_moment, second_moment):
@@ -639,6 +679,9 @@
     def line(self, l):
         return (self.p, flipped(self.w, l))
 
+    def others(self):
+        return [(flipped(self.p, k), flipped(self.w, l)) for k in range(1, 4) for l in range(1, 8)]
+
     def plane(self, k):
         return (flipped(self.p, k), self.w)
 
@@ -780,11 +823,11 @@
     def __init__(self, me, grad, film_grad, obs_all, film, out, film_out, back, square, buffers, sems):
         self.me, self.grad, self.film_grad, self.obs_all, self.film = me, grad, film_grad, obs_all, film
         self.out, self.film_out, self.back, self.square = out, film_out, back, square
-        (self.half, self.core, self.xb, self.yb, self.ub, self.vb, self.zb,
-         self.film_all, self.back_part, self.back_line, self.all_squares) = buffers
+        (self.half, self.core, self.xb, self.yb, self.ub, self.vb, self.zb, self.zq, self.pq,
+         self.film_all, self.back_part, self.back_line, self.cond, self.all_squares) = buffers
         (self.g_sems, self.h_sems, self.b_sems, self.c_sems, self.x_sems, self.y_sems, self.u_sems, self.v_sems,
-         self.z_sems, self.r_sems, self.n_sems, self.m_sems) = sems
-        self.x, self.y, self.u, self.v, self.z, self.r, self.c = {}, {}, {}, {}, {}, {}, {}
+         self.z_sems, self.r_sems, self.n_sems) = sems
+        self.x, self.y, self.u, self.v, self.z, self.r, self.c, self.q = {}, {}, {}, {}, {}, {}, {}, {}
         self.squares = []
 
     def start(self, g):
@@ -804,12 +847,39 @@
             return 0
 
         lax.fori_loop(0, (last - first) * 4, add, 0)
+        if g == Z_FIRST:
+            for k in range(1, 4):
+                self.z[g, k] = send(
+                    self.half.at[group(g), :, :, flipped(me.z, k)], self.zq.at[k - 1],
+                    self.z_sems, g * 3 + k - 1, me.line(2 * k),
+                )
+            return
         self.x[g] = send(
             self.half.at[group(g), :, 1 - me.x, LOW], self.xb.at[group(g)], self.x_sems, g, me.plane(1)
         )
         self.y[g] = send(
             self.half.at[group(g), 1 - me.y, :, HIGH], self.yb.at[group(g)], self.y_sems, g, me.plane(2)
         )
+
+    def z_sum(self, g):
+        me, half, (first, last) = self.me, self.half, GROUPS[g]
+        for k in range(1, 4):
+            self.z[g, k].wait_recv()
+        for j in range(first, last):
+            total = half[j, :, :, me.z].astype(f32)
+            for k in range(3):
+                total = total + self.zq[k, j - first].astype(f32)
+            half[j, :, :, me.z] = total.astype(bf16)
+        for k, sems in enumerate((self.x_sems, self.y_sems, self.u_sems)):
+            other = flipped(me.p, k + 1)
+            self.q[k] = send(
+                half.at[group(g), other // 2, other % 2, me.z], self.pq.at[k], sems, g, me.plane(k + 1)
+            )
+
+    def plane_sum(self, g):
+        for k in range(3):
+            self.q[k].wait_recv()
+        self.finish_sum(g, [lambda j, k=k: self.pq[k, j - GROUPS[g][0]] for k in range(3)])
 
     def first_sum(self, g):
         me, half, (first, last) = self.me, self.half, GROUPS[g]
@@ -850,13 +920,16 @@
             )
 
     def last_sum(self, g):
-        me = self.me
         for k in range(1, 4):
             self.z[g, k].wait_recv()
+        self.finish_sum(g, [lambda j, k=k: self.zb[k, j] for k in range(3)])
+
+    def finish_sum(self, g, terms):
+        me = self.me
         for j in range(*GROUPS[g]):
             total = self.half[j, me.y, me.x, me.z].astype(f32)
-            for k in range(3):
-                total = total + self.zb[k, j].astype(f32)
+            for term in terms:
+                total = total + term(j).astype(f32)
             total = total.astype(bf16)
             self.out[j, me.p] = total
             self.squares.append(jnp.sum(jnp.square(total.astype(f32)).reshape(4, 8, 256), axis=0))
@@ -879,31 +952,41 @@
         piece = self.film_all.at[me.p]
         self.h = [send(piece, piece, self.h_sems, k - 1, me.plane(k)) for k in range(1, 4)]
 
+    def film_inputs(self):
+        row, col = iota((128, 512), 0), iota((128, 512), 1)
+        same = ((row >> 4) == ((col >> 4) & 7)) & (((row >> 2) & 3) == (col >> 7)) & ((row & 3) == (col & 3))
+        seen_all = self.obs_all[...].reshape(512, 256)
+        for q in range(4):
+            pick = one_hot(same & (((col >> 2) & 3) == q))
+            self.cond[q] = mish_parts(dot_nn(pick, seen_all))[0].astype(bf16)
+
     def film_products(self):
         me = self.me
         for copy in self.h:
             copy.wait()
-        copies = [self.film_all[k].reshape(128, 128) for k in range(4)]
+        copies = [self.film_all[k].reshape(128, 128).astype(f32) for k in range(4)]
+        total = split2((copies[0] + copies[1]) + (copies[2] + copies[3]))
         row, col = iota((128, 128), 0), iota((128, 128), 1)
         mine = one_hot(((row >> 4) == (col >> 4)) & ((col & 15) == 4 * me.p + (row & 3)))
-        rows = [dot_nn(mine, piece).astype(bf16) for piece in copies]
-        parts = [sum(dot_nn(r, self.film[:, q * 256 : (q + 1) * 256]) for r in rows) for q in range(4)]
+        rows = [dot_nn(mine, part).astype(bf16) for part in total]
+        parts = [
+            dot_nn(rows[0], self.film[:, q * 256 : (q + 1) * 256])
+            + dot_nn(rows[1], self.film[:, q * 256 : (q + 1) * 256])
+            for q in range(4)
+        ]
         self.back_part[...] = quarter_rows(parts).astype(bf16).reshape(8, 16, 256)
         self.b = [
             send(self.back_part.at[flipped(me.w, l)], self.back_line.at[me.w], self.b_sems, l - 1, me.line(l))
             for l in range(1, 8)
         ]
         self.back_line[me.w] = self.back_part[me.w]
-        row, col = iota((128, 512), 0), iota((128, 512), 1)
-        same = ((row >> 4) == ((col >> 4) & 7)) & (((row >> 2) & 3) == (col >> 7)) & ((row & 3) == (col & 3))
-        seen_all = self.obs_all[...].reshape(512, 256)
         square = jnp.zeros((8, 256), f32)
+        turned = [part.T for part in total]
         for q in range(4):
-            pick = one_hot(same & (((col >> 2) & 3) == q))
-            cond = mish_parts(dot_nn(pick, seen_all))[0].astype(bf16)
-            total = sum(dot_tn(piece, cond) for piece in copies)
-            self.film_out[:, q * 256 : (q + 1) * 256] = total
-            square = square + jnp.sum(jnp.square(total).reshape(16, 8, 256), axis=0)
+            cond = self.cond[q]
+            product = dot_nn(turned[0], cond) + dot_nn(turned[1], cond)
+            self.film_out[:, q * 256 : (q + 1) * 256] = product
+            square = square + jnp.sum(jnp.square(product).reshape(16, 8, 256), axis=0)
         self.squares.append(0.25 * square)
 
     def film_back(self):
@@ -914,20 +997,19 @@
         slope = mish_parts(self.obs_all[me.p, me.w].astype(f32))[1]
         self.back[0] = unfold_rows(total * slope)
 
-    def norm(self):
+    def norm(self, hello):
         me = self.me
         total = sum(self.squares)
         piece = self.all_squares.at[me.p, me.w]
-        self.all_squares[me.p, me.w] = total[:, :128] + total[:, 128:]
-        copies = [send(piece, piece, self.m_sems, l - 1, me.line(l)) for l in range(1, 8)]
-        for copy in copies:
-            copy.wait()
-        piece = self.all_squares.at[me.p]
-        copies = [send(piece, piece, self.n_sems, k - 1, me.plane(k)) for k in range(1, 4)]
+        self.all_squares[me.p, me.w] = jnp.sum(total[:, :128] + total[:, 128:], axis=0, keepdims=True)
+        pl.semaphore_wait(hello, len(me.others()))
+        copies = [
+            send(piece, piece, self.n_sems, i - 1, (flipped(me.p, i % 4), flipped(me.w, i // 4))) for i in range(1, 32)
+        ]
         for copy in copies + list(self.r.values()):
             copy.wait()
-        self.square[...] = jnp.sum(self.all_squares[...].reshape(32, 8, 128), axis=0)
-        for copies in (self.c, self.x, self.y, self.u, self.v, self.z):
+        self.square[...] = jnp.sum(self.all_squares[...].reshape(32, 128), axis=0, keepdims=True)
+        for copies in (self.c, self.x, self.y, self.u, self.v, self.z, self.q):
             for copy in copies.values():
                 copy.wait_send()
 
@@ -935,6 +1017,7 @@
 GATHER_GROUPS = ((0, 1), (1, 3), (3, 5), (5, 7), (7, 9))
 GATHER_DIRECT = (3, 4)
 GROUPS = ((0, 1), (1, 3), (3, 5), (5, 7), (7, 9))
+Z_FIRST = 4
 LOW, HIGH = pl.ds(0, 2), pl.ds(2, 2)
 
 
@@ -950,10 +1033,10 @@
     (params, order, obs, slots, noisy, mask, levels, cotangent, table,
      act, noisy_grad, back, out, film_out, square,
      own, weights, seen, obs_all, film, film_part, film_line, grad, film_grad) = refs[:24]
-    buffers, sems = refs[24:35], refs[35:]
-    pairs = [(sems[2 * i], sems[2 * i + 1]) for i in range(21)]
+    buffers, sems, hello = refs[24:38], refs[38:-1], refs[-1]
+    pairs = [(sems[2 * i], sems[2 * i + 1]) for i in range(20)]
     me = Place()
-    gather = Gather(me, own, weights, seen, obs_all, film, film_part, film_line, pairs[:9] + [sems[42]])
+    gather = Gather(me, own, weights, seen, obs_all, film, film_part, film_line, pairs[:9] + [sems[40]])
     scatter = Scatter(me, grad, film_grad, obs_all, film, out, film_out, back, square, buffers, pairs[9:])
     obs_all[me.p, me.w] = fold_rows(obs[0].astype(f32)).astype(bf16)
     greet(me)
@@ -965,17 +1048,18 @@
 
     def reach(point):
         if point == 0:
+            gather.first_hop(0)
             gather.film_product()
-            gather.start_rows(2)
-            gather.start_rows(3)
-            gather.start_rows(4)
-            gather.first_hop(0)
+            for g in range(2, len(GATHER_GROUPS)):
+                gather.start_rows(g)
             gather.first_hop(1)
             gather.second_hop(0)
             gather.film_hop()
             gather.first_hop(2)
             gather.second_hop(1)
             gather.last_hop(0)
+            for device in me.others():
+                pl.semaphore_signal(hello, inc=1, device_id=device, device_id_type=MESH)
             gather.first_hop(3)
             gather.second_hop(2)
             gather.last_hop(1)
@@ -1006,6 +1090,7 @@
             scatter.start(2)
         if point == 12:
             scatter.core_sum(2)
+            scatter.first_sum(3)
         if point == 13:
             scatter.film_start()
             scatter.start(1)
@@ -1016,27 +1101,26 @@
     )
     scatter.start(0)
     scatter.core_sum(1)
-    scatter.first_sum(4)
+    scatter.first_sum(2)
     scatter.core_sum(0)
+    scatter.second_sum(3)
+    scatter.z_sum(4)
+    scatter.first_sum(1)
     scatter.film_hop()
-    scatter.first_sum(3)
-    scatter.second_sum(4)
-    scatter.first_sum(2)
-    scatter.second_sum(3)
-    scatter.first_sum(1)
+    scatter.second_sum(2)
     scatter.first_sum(0)
-    scatter.second_sum(2)
     gather.finish()
+    scatter.film_inputs()
+    scatter.plane_sum(4)
+    scatter.second_sum(1)
     scatter.film_products()
-    scatter.second_sum(1)
     scatter.second_sum(0)
-    scatter.last_sum(4)
     scatter.last_sum(3)
-    scatter.film_back()
     scatter.last_sum(2)
     scatter.last_sum(1)
+    scatter.film_back()
     scatter.last_sum(0)
-    scatter.norm()
+    scatter.norm(hello)
 
 
 class Stacked:
@@ -1071,7 +1155,7 @@
             jax.ShapeDtypeStruct((1, 4, OBS), f32),
             jax.ShapeDtypeStruct((n, 4, ROWS, 256), bf16),
             jax.ShapeDtypeStruct((4 * ROWS, OBS), f32),
-            jax.ShapeDtypeStruct((8, 128), f32),
+            jax.ShapeDtypeStruct((1, 128), f32),
         ),
         in_specs=[vmem] * 9,
         out_specs=(vmem,) * 6,
@@ -1092,16 +1176,20 @@
             low(n, 2, ROWS, 256),
             low(n, 2, ROWS, 256),
             low(3, n, ROWS, 256),
+            low(3, GROUPS[Z_FIRST][1] - GROUPS[Z_FIRST][0], 2, 2, ROWS, 256),
+            low(3, GROUPS[Z_FIRST][1] - GROUPS[Z_FIRST][0], ROWS, 256),
             low(4, 8, 16, 128),
             low(8, 16, 256),
             low(8, 16, 256),
-            pltpu.VMEM((4, 8, 8, 128), f32),
+            low(4, 128, 256),
+            pltpu.VMEM((4, 8, 1, 128), f32),
             *pair(7), *pair(7), *pair(3), *pair(3),
             *pair(3 * parts), *pair(3 * parts), *pair(3 * parts), *pair(3 * parts), *pair(parts),
             *pair(7), *pair(3), *pair(7),
             *pair(count), *pair(count), *pair(count), *pair(count), *pair(count),
-            *pair(3 * count), *pair(3 * count), *pair(3), *pair(7),
+            *pair(3 * count), *pair(3 * count), *pair(31),
             pltpu.SemaphoreType.DMA,
+            pltpu.SemaphoreType.REGULAR,
         ],
         compiler_params=pltpu.CompilerParams(collective_id=0, has_side_effects=True, vmem_limit_bytes=60 << 20),
         name="step",
@@ -1112,10 +1200,11 @@
     act, noisy_grad, back, total, film_total, squares = step(
         params, obs_embed, obs_slot[None], noisy[0], action_mask, time_index, cotangent[0]
     )
-    norm, *new = adam(
-        total.reshape(NB, ROWS, 256), film_total, squares, params, first_moment, second_moment
-    )
-    return (act[None], noisy_grad[None], back, norm.reshape(()), *new)
+    norm, *new, act, noisy_grad, back = adam(
+        total.reshape(NB, ROWS, 256), film_total, squares, params, first_moment, second_moment,
+        (act, noisy_grad, back), ((1, C, 256), (ADIM, 1, 256), (1, 4, OBS)),
+    )
+    return (act, noisy_grad.transpose(1, 0, 2), back, norm.reshape(()), *new)
 
 
 def solution(mesh):

time: 92.3 us -> 83.8 us (0.908)
  Pallas kernels: 88.8 us -> 82.8 us
  local copies, waits for them, and re-layouts: 2.6 us -> 0 us
    pallas_call x1, Pallas kernels: 81.3 us -> 76 us  [step(): pl.pallas_call(step_kernel, out_shape=(jax.ShapeDtypeStruct((C, 256), bf1...]
    unnamed x7 -> x0, local copies, waits for them, and re-layouts: 2.6 us -> none
where the time goes in v3:
time: 83.8 us; the launch traced here: 83.6 us
  Pallas kernels  82.8 us (99%)
    pallas_call x1, Pallas kernels, step(): pl.pallas_call(step_kernel, out_shape=(jax.ShapeDtypeStruct((C, 256), bf1...  76 us
    pallas_call x1, Pallas kernels, adam(): pl.pallas_call(functools.partial(adam_kernel, count), out_shape=(jax.Shap...  6.83 us

profile of v3, /device:TPU:0, one launch (start us, length us, event | category | flops | bytes accessed | tf_op | source)
XLA Modules:
  0.0 83.6 jit_solution(4901950536239363609)
XLA Ops:
  0.6 76.0 %step.1 = (bf16[256,256]{1,0:T(8,128)(2,1)}, f32[10,256]{1,0:T(8,128)}, f32[1,4,1024]{2,1,0:T(4,128)}, bf16[9,4,32,256]{3,2,1,0:T(8,128)(2,1)}, f32[128,1024]{1,0:T(8,128)}, /*index=5*/f32[1,128]{1,0:T(1,128)}) custom-call(f32[32,12627]{1,0:T(8,128)} %refs_4_.1, bf16[128,128]{1,0:T(8,128)(2,1)} %constant.4.clone.refs_1_.refs_3_, ...), custom_call_target="tpu_custom_call" | custom-call | tf_op jit(solution)/shard_map/step/pallas_call | solution.py:1150
  76.6 6.8 %adam.1 = (f32[1,1]{1,0:T(1,128)}, f32[32,12627]{1,0:T(8,128)}, f32[32,12627]{1,0:T(8,128)}, f32[32,12627]{1,0:T(8,128)}, bf16[32,12627]{1,0:T(8,128)(2,1)}, /*i...) custom-call(bf16[36,32,256]{2,1,0:T(8,128)(2,1)} %bitcast.6, ...), custom_call_target="tpu_custom_call" | custom-call | tf_op jit(solution)/shard_map/adam/pallas_call | solution.py:599

commit v4 on v3

--- a/solution.py
+++ b/solution.py
@@ -42,8 +42,8 @@
 AT_TIME = (12092, 12348)
 AT_UP_RES = 9276
 B_MISC, B_INNER, B_OUTER, B_FILM = 0, 1, 2, 3
-B_DS, B_POOL, B_SPREAD, B_UF, B_US, B_UR = 5, 10, 13, 18, 28, 33
-B_NONE = (17, 35)
+B_DS, B_POOL, B_SPREAD, B_UF, B_US, B_UR = 5, 10, 13, 17, 27, 32
+B_NONE = (34, 35)
 LANE_TAIL = 64
 CONVS = (
     (50, 5, 2, lambda t, h: B_DS + t),
@@ -134,6 +134,11 @@
 
 
 def pack_rows(params_ref, order_ref, own_ref, film_ref):
+    pack_first(params_ref, order_ref, own_ref)
+    pack_rest(params_ref, own_ref, film_ref)
+
+
+def pack_first(params_ref, order_ref, own_ref):
     own_ref = Blocks(own_ref)
 
     def low(start, width):
@@ -151,8 +156,17 @@
     own_ref[B_INNER] = low(AT_TIME[0], 256)
     own_ref[B_OUTER] = low(AT_TIME[1], 256)
     for q in range(4):
+        own_ref[B_FILM + q // 2, :, (q % 2) * 128 : (q % 2) * 128 + 128] = low(AT_FILM[q] + OBS, TE)
+
+
+def pack_rest(params_ref, own_ref, film_ref):
+    own_ref = Blocks(own_ref)
+
+    def low(start, width):
+        return params_ref[:, start : start + width].astype(bf16)
+
+    for q in range(4):
         film_ref[q * ROWS : (q + 1) * ROWS] = low(AT_FILM[q], OBS)
-        own_ref[B_FILM + q // 2, :, (q % 2) * 128 : (q % 2) * 128 + 128] = low(AT_FILM[q] + OBS, TE)
     own_ref[B_UR] = low(AT_UP_RES, 256)
     own_ref[B_UR + 1] = low(AT_UP_RES + 256, 256)
     for b in B_NONE:
@@ -234,10 +248,9 @@
 
 
 def norm_forward(before, gain, shift, ones):
-    (center,) = group_means([over_frames(before)], ones)
+    center, square = group_means([over_frames(before), over_frames(before * before)], ones)
+    scale = lax.rsqrt(jnp.maximum(square - center * center, 0.0) + norm_eps)
     away = minus(before, center)
-    (spread,) = group_means([over_frames(away * away)], ones)
-    scale = lax.rsqrt(spread + norm_eps)
     normal = times(away, scale)
     act, slope = mish_parts(normal * gain + shift)
     return act, normal, slope, scale
@@ -370,6 +383,9 @@
     odd_out = dot_nt(pooled_next, w_ref[B_SPREAD]) + dot_nt(pooled, w_ref[B_SPREAD + 2])
     wide = (interleave(even_out, odd_out) + vec(SB)).astype(bf16)
     joined = (wide, skip)
+    turned = upstream_low.T
+    for h in range(2):
+        grad_ref[B_UR + h] = dot_nn(turned, joined[h]).astype(bf16)
     reach(5)
     up_first = [lambda t, h=h: w_ref[B_UF + 2 * t + h] for h in range(2)]
     pre = conv_forward(wide, up_first[0]) + conv_forward(skip, up_first[1]) + vec(U_B1)
@@ -380,8 +396,7 @@
     up = lambda t: w_ref[B_US + t]
     pre = conv_forward(mid_three, up) + vec(U_B2)
     act, normal_four, slope_four, scale_four = norm_forward(pre, vec(U_G2), vec(U_S2), ones)
-    result = act + dot_nt(wide, w_ref[B_UR]) + dot_nt(skip, w_ref[B_UR + 1]) + vec(U_RB)
-    act_ref[...] = dot_tn(result.astype(bf16), swap).astype(bf16)
+    act_four = act
 
     single_grads = {}
 
@@ -397,9 +412,6 @@
     single_grads[U_B2] = row_sum(grad)
     low = grad.astype(bf16)
     conv_weights(low, mid_three, lambda t: B_US + t)
-    turned = upstream_low.T
-    for h in range(2):
-        grad_ref[B_UR + h] = dot_nn(turned, joined[h]).astype(bf16)
     reach(8)
     grad_mid = conv_source(low, up)
     shift_three = over_frames(grad_mid)
@@ -409,6 +421,7 @@
     )
     single_grads[U_B1] = row_sum(grad)
     low = grad.astype(bf16)
+    reach(15)
     for h in range(2):
         conv_weights(low, joined[h], lambda t, h=h: B_UF + 2 * t + h)
     single_grads[U_RB] = row_sum(upstream)
@@ -467,13 +480,6 @@
     for k in range(8):
         film_grad_ref[k] = jnp.concatenate([v[:, k * 32 : (k + 1) * 32] for v in at_slots], axis=1).astype(bf16)
     reach(13)
-    back = back + dot_nn(low, misc_first)
-    grad_start = back[:, 50:60]
-    for t in range(5):
-        grad_start = grad_start + step_frames(back[:, t * ADIM : (t + 1) * ADIM], 2 - t)
-    grad_cols = sum(dot_tn(part, swap) for part in split3(jnp.concatenate([grad_start, jnp.zeros((256, 6), f32)], axis=1)))
-    noisy_grad_ref[...] = grad_cols[:ADIM] * keep
-
     grad_embed = back_cond * cond_slope
     single_grads[T_OUT] = jnp.concatenate(
         [jnp.sum(grad_embed, axis=0, keepdims=True), jnp.zeros((1, C - TE), f32)], axis=1
@@ -488,6 +494,15 @@
     stack = jnp.concatenate(stack + [jnp.zeros((128 - LANE_TAIL - TAIL, 256), f32)], axis=0)
     grad_ref[B_MISC, :, :128] = (misc_grad + stack.T).astype(bf16)
     grad_ref[B_MISC, :, 128:] = jnp.zeros((256, 128), bf16)
+    reach(14)
+    result = act_four + dot_nt(wide, w_ref[B_UR]) + dot_nt(skip, w_ref[B_UR + 1]) + vec(U_RB)
+    act_ref[...] = dot_tn(result.astype(bf16), swap).astype(bf16)
+    back = back + dot_nn(low, misc_first)
+    grad_start = back[:, 50:60]
+    for t in range(5):
+        grad_start = grad_start + step_frames(back[:, t * ADIM : (t + 1) * ADIM], 2 - t)
+    grad_cols = sum(dot_tn(part, swap) for part in split3(jnp.concatenate([grad_start, jnp.zeros((256, 6), f32)], axis=1)))
+    noisy_grad_ref[...] = grad_cols[:ADIM] * keep
 
 
 def train(weights, seen_film, slots, noisy, mask, levels, cotangent):
@@ -542,37 +557,42 @@
             grad_ref[:, begin : begin + 128 * taps] = moved[n * ROWS : (n + 1) * ROWS]
 
 
+def unpack_kernel(own_ref, film_ref, order_ref, grad_ref):
+    native_grads(own_ref, film_ref, order_ref, grad_ref)
+
+
+def unpack(own, film):
+    vmem = pl.BlockSpec(memory_space=pltpu.VMEM)
+    return pl.pallas_call(
+        unpack_kernel,
+        out_shape=jax.ShapeDtypeStruct((ROWS, Q), f32),
+        in_specs=[vmem] * 3,
+        out_specs=vmem,
+        compiler_params=pltpu.CompilerParams(vmem_limit_bytes=30 << 20),
+        name="unpack",
+    )(own, film, jnp.asarray(first_order(), bf16))
+
+
 def adam_kernel(count, *refs):
-    own_ref, film_ref, square_ref, order_ref = refs[:4]
-    old_hbm, extra_in = refs[4:7], refs[7 : 7 + count]
-    norm_ref, new_hbm, extra_out = refs[7 + count], refs[8 + count : 12 + count], refs[12 + count : 12 + 2 * count]
-    grad_ref, old, new, in_sems, out_sems = refs[12 + 2 * count], refs[13 + 2 * count : 16 + 2 * count], refs[
-        16 + 2 * count : 20 + 2 * count
-    ], refs[-2], refs[-1]
-    rows = [pl.ds(h * HALF, HALF) for h in range(2)]
-    loads = [
-        [pltpu.make_async_copy(old_hbm[n].at[rows[h]], old[n].at[rows[h]], in_sems.at[h, n]) for n in range(3)]
-        for h in range(2)
-    ]
-    stores = [
-        [pltpu.make_async_copy(new[n].at[rows[h]], new_hbm[n].at[rows[h]], out_sems.at[h, n]) for n in range(4)]
-        for h in range(2)
-    ]
-    for half in loads:
-        for copy in half:
-            copy.start()
+    grad_ref, square_ref = refs[:2]
+    old, extra_in = refs[2:5], refs[5 : 5 + count]
+    norm_ref, new_hbm, extra_out = refs[5 + count], refs[6 + count : 10 + count], refs[10 + count : 10 + 2 * count]
+    new, sems = refs[10 + 2 * count : 14 + 2 * count], refs[-1]
     norm = jnp.sqrt(jnp.sum(square_ref[...], axis=(0, 1), keepdims=True))
     norm_ref[...] = norm
     factor = jnp.minimum(1.0, clip_limit / (norm + 1e-06))
-    for source, target in zip(extra_in, extra_out):
-        target[...] = source[...].reshape(target.shape)
-    native_grads(own_ref, film_ref, order_ref, grad_ref)
+    stores = {}
+
+    def store(n, height, at):
+        rows = pl.ds(at, height)
+        stores[n, at] = pltpu.make_async_copy(new[n].at[rows], new_hbm[n].at[rows], sems.at[n, at // 8])
+        stores[n, at].start()
+
     width = 1024
-    for h in range(2):
-        for copy in loads[h]:
-            copy.wait()
+    for row in range(0, ROWS, 16):
         for begin in range(0, Q, width):
-            at = (rows[h], slice(begin, min(begin + width, Q)))
+            cols = slice(begin, min(begin + width, Q))
+            at = (slice(row, row + 16), cols)
             clipped = grad_ref[at] * factor
             new_first = decay_first * old[1][at] + (1.0 - decay_first) * clipped
             new_second = decay_second * old[2][at] + (1.0 - decay_second) * clipped * clipped
@@ -584,14 +604,15 @@
             new[1][at] = new_first
             new[2][at] = new_second
             new[3][at] = after.astype(bf16)
-        for copy in stores[h]:
-            copy.start()
-    for half in stores:
-        for copy in half:
-            copy.wait()
-
-
-def adam(own, film, squares, params, first, second, extras=(), extra_shapes=()):
+        for n in range(4):
+            store(n, 16, row)
+    for source, target in zip(extra_in, extra_out):
+        target[...] = source[...].reshape(target.shape)
+    for copy in stores.values():
+        copy.wait()
+
+
+def adam(grads, squares, params, first, second, extras=(), extra_shapes=()):
     vmem = pl.BlockSpec(memory_space=pltpu.VMEM)
     hbm = pl.BlockSpec(memory_space=pl.ANY)
     shape = jax.ShapeDtypeStruct((ROWS, Q), f32)
@@ -603,13 +624,13 @@
             shape, shape, shape, jax.ShapeDtypeStruct((ROWS, Q), bf16),
             *(jax.ShapeDtypeStruct(dims, v.dtype) for dims, v in zip(extra_shapes, extras)),
         ),
-        in_specs=[vmem] * 4 + [hbm] * 3 + [vmem] * count,
+        in_specs=[vmem] * (5 + count),
         out_specs=(vmem,) + (hbm,) * 4 + (vmem,) * count,
-        scratch_shapes=[pltpu.VMEM((ROWS, Q), f32)] * 7
-        + [pltpu.VMEM((ROWS, Q), bf16), pltpu.SemaphoreType.DMA((2, 3)), pltpu.SemaphoreType.DMA((2, 4))],
-        compiler_params=pltpu.CompilerParams(vmem_limit_bytes=56 << 20),
+        scratch_shapes=[pltpu.VMEM((ROWS, Q), f32)] * 3
+        + [pltpu.VMEM((ROWS, Q), bf16), pltpu.SemaphoreType.DMA((4, ROWS // 8))],
+        compiler_params=pltpu.CompilerParams(vmem_limit_bytes=30 << 20),
         name="adam",
-    )(own, film, squares, jnp.asarray(first_order(), bf16), params, first, second, *extras)
+    )(grads, squares, params, first, second, *extras)
 
 
 def local_plain(noisy, action_mask, time_index, obs_embed, obs_slot, cotangent, params, first_moment, second_moment):
@@ -649,7 +670,7 @@
         take = lambda v: jnp.pad(v[:, r : r + ROWS], ((0, 0), (0, max(0, ROWS - rows)), (0, 0)))
         outs.append(
             adam(
-                take(mine), take(film_mine).reshape(4 * ROWS, OBS), squares.reshape(1, 1),
+                unpack(take(mine), take(film_mine).reshape(4 * ROWS, OBS)), squares.reshape(1, 1),
                 *(padded(v)[r : r + ROWS] for v in (params, first_moment, second_moment)),
             )
         )
@@ -660,30 +681,32 @@
 MESH = pl.DeviceIdType.MESH
 
 
-def flipped(v, bits):
-    out = v
-    for k in range(3):
-        if bits >> k & 1:
-            bit = (v // (1 << k)) % 2
-            out = out + (1 << k) * (1 - 2 * bit)
-    return out
-
-
 class Place:
     def __init__(self):
-        self.p = lax.axis_index("pair")
-        self.w = lax.axis_index("wide")
-        self.x, self.y = self.p % 2, self.p // 2
-        self.c, self.z = self.w % 2, self.w // 2
+        p = lax.axis_index("pair")
+        w = lax.axis_index("wide")
+        self.p, self.w = p, w
+        self.x, self.y = lax.rem(p, 2), lax.div(p, 2)
+        self.c, self.z = lax.rem(w, 2), lax.div(w, 2)
+        turn = [1 - 2 * self.x, 2 - 4 * self.y]
+        self.p_flip = [p, p + turn[0], p + turn[1], p + (turn[0] + turn[1])]
+        z_turn = [1 - 2 * lax.rem(self.z, 2), 2 - 4 * lax.div(self.z, 2)]
+        self.z_flip = [self.z, self.z + z_turn[0], self.z + z_turn[1], self.z + (z_turn[0] + z_turn[1])]
+        self.w_flip = []
+        for z in self.z_flip:
+            self.w_flip += [2 * z + self.c, 2 * z + (1 - self.c)]
+        self.w_flip[0] = w
+        self.x_of = [lax.rem(v, 2) for v in self.p_flip]
+        self.y_of = [lax.div(v, 2) for v in self.p_flip]
 
     def line(self, l):
-        return (self.p, flipped(self.w, l))
+        return (self.p, self.w_flip[l])
 
     def others(self):
-        return [(flipped(self.p, k), flipped(self.w, l)) for k in range(1, 4) for l in range(1, 8)]
+        return [(self.p_flip[k], self.w_flip[l]) for k in range(1, 4) for l in range(1, 8)]
 
     def plane(self, k):
-        return (flipped(self.p, k), self.w)
+        return (self.p_flip[k], self.w)
 
 
 def greet(me):
@@ -698,13 +721,36 @@
     pl.semaphore_wait(pltpu.get_barrier_semaphore(), 10)
 
 
-def send(source, target, sems, at, device):
-    copy = pltpu.make_async_remote_copy(
-        src_ref=source, dst_ref=target, send_sem=sems[0].at[at], recv_sem=sems[1].at[at],
-        device_id=device, device_id_type=MESH,
-    )
-    copy.start()
-    return copy
+def drain(size, semaphore):
+    pltpu.make_async_copy(size, size, semaphore).wait()
+
+
+class Pool:
+    def __init__(self, ref):
+        self.ref, self.used = ref, 0
+
+    def new(self):
+        self.used += 1
+        return self.ref.at[self.used - 1]
+
+    def several(self, keys):
+        return {key: self.new() for key in keys}
+
+
+class Lane:
+    def __init__(self, pool):
+        self.sent, self.bytes = pool.new(), 0
+
+    def send(self, source, target, arrival, device):
+        pltpu.make_async_remote_copy(
+            src_ref=source, dst_ref=target, send_sem=self.sent, recv_sem=arrival,
+            device_id=device, device_id_type=MESH,
+        ).start()
+        self.bytes += math.prod(source.shape) * source.dtype.itemsize
+
+    def finish(self, size):
+        assert math.prod(size.shape) * size.dtype.itemsize == self.bytes
+        drain(size, self.sent)
 
 
 def fold_rows(v):
@@ -721,169 +767,187 @@
 
 
 class Gather:
-    def __init__(self, me, own, weights, seen, obs_all, film, film_part, film_line, sems):
+    def __init__(self, me, own, weights, seen, obs_all, film, film_part, film_line, pool, local_sem):
         self.me, self.own, self.weights, self.seen, self.obs_all, self.film = me, own, weights, seen, obs_all, film
-        self.film_part, self.film_line = film_part, film_line
-        (self.obs_sems, self.part_sems, self.film_sems, self.more_sems,
-         self.z_sems, self.x_sems, self.y_sems, self.f_sems, self.c_sems, self.local_sem) = sems
-        self.z, self.x, self.y, self.f, self.c = {}, {}, {}, {}, {}
+        self.film_part, self.film_line, self.local_sem = film_part, film_line, local_sem
+        self.z, self.x, self.y, self.f, self.c, self.small = (Lane(pool) for _ in range(6))
+        self.parts, self.films, self.more = (Lane(pool) for _ in range(3))
+        pieces = [(g, k) for g in range(len(GATHER_GROUPS)) for k in range(1, 4)]
+        self.z_in = pool.several(pieces)
+        near = [(g, k) for g, k in pieces if g not in GATHER_DIRECT] + list(GATHER_DIRECT)
+        self.x_in, self.y_in = pool.several(near), pool.several(near)
+        self.f_in = pool.several(range(len(GATHER_GROUPS)))
+        self.c_in = pool.several(range(len(GATHER_GROUPS)))
+        self.obs_in, self.part_in, self.film_in, self.more_in = (pool.new() for _ in range(4))
 
     def start_obs(self):
         me = self.me
         piece = self.obs_all.at[me.p, me.w]
-        self.obs_copies = [send(piece, piece, self.obs_sems, l - 1, me.line(l)) for l in range(1, 8)]
+        for l in range(1, 8):
+            self.small.send(piece, piece, self.obs_in, me.line(l))
 
     def start_rows(self, g):
         me = self.me
         for k in range(1, 4):
-            self.z[g, k] = send(
+            self.z.send(
                 self.own.at[gather_group(g), me.p], self.weights.at[gather_group(g), me.p, me.z, me.c],
-                self.z_sems, g * 3 + k - 1, me.line(2 * k),
+                self.z_in[g, k], me.line(2 * k),
             )
-        if g == 0:
-            self.local = pltpu.make_async_copy(self.own, self.weights.at[:, :, me.z, me.c], self.local_sem)
-            self.local.start()
+
+    def start_local(self):
+        self.local = pltpu.make_async_copy(self.own, self.weights.at[:, :, self.me.z, self.me.c], self.local_sem)
+        self.local.start()
 
     def film_product(self):
         me = self.me
-        for copy in self.obs_copies:
-            copy.wait()
+        drain(self.obs_all.at[0, 0:7], self.obs_in)
         cond = mish_parts(self.obs_all[me.p].reshape(128, 256).astype(f32))[0].astype(bf16)
         film = quarter_rows([dot_nt(cond, self.film[:, q * 256 : (q + 1) * 256]) for q in range(4)])
         row, col = iota((64, 128), 0), iota((64, 128), 1)
         pick = one_hot(((row >> 3) == (col >> 4)) & ((row & 7) == (col & 3)))
         self.film_part[...] = sum(dot_nn(pick, part) for part in split3(film)).reshape(8, 8, 128)
-        self.part_copies = [
-            send(self.film_part.at[flipped(me.w, l)], self.film_line.at[me.w], self.part_sems, l - 1, me.line(l))
-            for l in range(1, 8)
-        ]
+        for l in range(1, 8):
+            self.parts.send(self.film_part.at[me.w_flip[l]], self.film_line.at[me.w], self.part_in, me.line(l))
         self.film_line[me.w] = self.film_part[me.w]
 
     def film_hop(self):
         me = self.me
-        for copy in self.part_copies:
-            copy.wait()
+        drain(self.film_line.at[0:7], self.part_in)
         for k in range(4):
             self.seen[me.p, k] = self.film_line[2 * k] + pltpu.roll(self.film_line[2 * k + 1], 4, 0)
         piece = self.seen.at[me.p]
-        self.film_copies = [send(piece, piece, self.film_sems, k - 1, me.plane(k)) for k in range(1, 4)]
+        for k in range(1, 4):
+            self.films.send(piece, piece, self.film_in, me.plane(k))
 
     def obs_hop(self):
         me = self.me
         piece = self.obs_all.at[me.p]
-        self.more_copies = [send(piece, piece, self.more_sems, k - 1, me.plane(k)) for k in range(1, 4)]
+        for k in range(1, 4):
+            self.more.send(piece, piece, self.more_in, me.plane(k))
 
     def film_done(self):
-        for copy in self.film_copies:
-            copy.wait()
+        drain(self.seen.at[0:3], self.film_in)
 
     def first_hop(self, g):
         me = self.me
         for k in range(1, 4):
-            self.z[g, k].wait_recv()
-            piece = self.weights.at[gather_group(g), me.p, flipped(me.z, k), me.c]
-            self.x[g, k] = send(piece, piece, self.x_sems, g * 3 + k - 1, me.plane(1))
-            self.y[g, k] = send(piece, piece, self.y_sems, g * 3 + k - 1, me.plane(2))
+            piece = self.weights.at[gather_group(g), me.p, me.z_flip[k], me.c]
+            drain(piece, self.z_in[g, k])
+            key = g if g in GATHER_DIRECT else (g, k)
+            self.x.send(piece, piece, self.x_in[key], me.plane(1))
+            self.y.send(piece, piece, self.y_in[key], me.plane(2))
             if g in GATHER_DIRECT:
-                self.f[g, k] = send(piece, piece, self.f_sems, g * 3 + k - 1, me.plane(3))
+                self.f.send(piece, piece, self.f_in[g], me.plane(3))
 
     def second_hop(self, g):
         me = self.me
+        if g in GATHER_DIRECT:
+            three = self.weights.at[gather_group(g), 0, 0:3, 0]
+            drain(three, self.x_in[g])
+            drain(three, self.y_in[g])
+            return
         for k in range(1, 4):
-            self.x[g, k].wait_recv()
-            self.y[g, k].wait_recv()
-            if g in GATHER_DIRECT:
-                continue
+            one = self.weights.at[gather_group(g), 0, 0, 0]
+            drain(one, self.x_in[g, k])
+            drain(one, self.y_in[g, k])
             along_y = (g + k) % 2 == 0
-            piece = self.weights.at[gather_group(g), flipped(me.p, 1 if along_y else 2), flipped(me.z, k), me.c]
-            self.f[g, k] = send(piece, piece, self.f_sems, g * 3 + k - 1, me.plane(2 if along_y else 1))
+            piece = self.weights.at[gather_group(g), me.p_flip[1 if along_y else 2], me.z_flip[k], me.c]
+            self.f.send(piece, piece, self.f_in[g], me.plane(2 if along_y else 1))
 
     def last_hop(self, g):
         if g == 0:
             self.local.wait()
         if g in GATHER_DIRECT:
             self.second_hop(g)
-        for k in range(1, 4):
-            self.f[g, k].wait_recv()
+        drain(self.weights.at[gather_group(g), 0, 0:3, 0], self.f_in[g])
         piece = self.weights.at[gather_group(g), :, :, self.me.c]
-        self.c[g] = send(piece, piece, self.c_sems, g, self.me.line(1))
+        self.c.send(piece, piece, self.c_in[g], self.me.line(1))
 
     def arrived(self, g):
-        self.c[g].wait_recv()
+        drain(self.weights.at[gather_group(g), :, :, 0], self.c_in[g])
+
+    def obs_done(self):
+        drain(self.obs_all.at[0:3], self.more_in)
 
     def finish(self):
-        for copy in self.more_copies:
-            copy.wait()
-        for copies in (self.z, self.x, self.y, self.f, self.c):
-            for copy in copies.values():
-                copy.wait_send()
+        three = self.weights.at[:, 0, 0:3, 0]
+        for lane in (self.z, self.x, self.y, self.f):
+            lane.finish(three)
+        self.c.finish(self.weights.at[:, :, :, 0])
+        self.small.finish(self.obs_all.at[0, 0:7])
+        self.parts.finish(self.film_line.at[0:7])
+        self.films.finish(self.seen.at[0:3])
+        self.more.finish(self.obs_all.at[0:3])
 
 
 class Scatter:
-    def __init__(self, me, grad, film_grad, obs_all, film, out, film_out, back, square, buffers, sems):
+    def __init__(self, me, grad, film_grad, obs_all, film, out, film_out, back, square, buffers, pool):
         self.me, self.grad, self.film_grad, self.obs_all, self.film = me, grad, film_grad, obs_all, film
         self.out, self.film_out, self.back, self.square = out, film_out, back, square
-        (self.half, self.core, self.xb, self.yb, self.ub, self.vb, self.zb, self.zq, self.pq,
+        (self.half, self.core, self.xb, self.yb, self.ub, self.vb, self.zb, self.zq, self.pq, self.db,
          self.film_all, self.back_part, self.back_line, self.cond, self.all_squares) = buffers
-        (self.g_sems, self.h_sems, self.b_sems, self.c_sems, self.x_sems, self.y_sems, self.u_sems, self.v_sems,
-         self.z_sems, self.r_sems, self.n_sems) = sems
-        self.x, self.y, self.u, self.v, self.z, self.r, self.c, self.q = {}, {}, {}, {}, {}, {}, {}, {}
+        self.c, self.x, self.y, self.u, self.v, self.z = (Lane(pool) for _ in range(6))
+        self.zf, self.q, self.d, self.r, self.g, self.h, self.b, self.n = (Lane(pool) for _ in range(8))
+        groups = range(len(GROUPS))
+        self.staged = [g for g in groups if g != Z_FIRST and g not in PLANE_DIRECT]
+        self.c_in = pool.several(groups)
+        self.x_in, self.y_in, self.u_in, self.v_in = (pool.several(self.staged) for _ in range(4))
+        self.d_in = pool.several(PLANE_DIRECT)
+        self.z_in = pool.several(g for g in groups if g != Z_FIRST)
+        self.zf_in, self.q_in, self.r_in, self.g_in, self.h_in, self.b_in, self.n_in = (pool.new() for _ in range(7))
         self.squares = []
 
     def start(self, g):
         me = self.me
-        self.c[g] = send(
-            self.grad.at[group(g), :, :, 1 - me.c], self.core.at[group(g)], self.c_sems, g, me.line(1)
-        )
+        self.c.send(self.grad.at[group(g), :, :, 1 - me.c], self.core.at[group(g)], self.c_in[g], me.line(1))
 
     def core_sum(self, g):
-        me, (first, last) = self.me, GROUPS[g]
-        self.c[g].wait_recv()
+        me, half, (first, last) = self.me, self.half, GROUPS[g]
+        drain(self.core.at[group(g)], self.c_in[g])
 
         def add(i, _):
             j, q = first + i // 4, i % 4
             total = self.grad[j, q, :, me.c].astype(f32) + self.core[j, q].astype(f32)
-            self.half[j, q // 2, q % 2] = total.astype(bf16)
+            half[j, q // 2, q % 2] = total.astype(bf16)
             return 0
 
         lax.fori_loop(0, (last - first) * 4, add, 0)
         if g == Z_FIRST:
+            self.z_send(g, 0)
+        elif g in PLANE_DIRECT:
             for k in range(1, 4):
-                self.z[g, k] = send(
-                    self.half.at[group(g), :, :, flipped(me.z, k)], self.zq.at[k - 1],
-                    self.z_sems, g * 3 + k - 1, me.line(2 * k),
-                )
-            return
-        self.x[g] = send(
-            self.half.at[group(g), :, 1 - me.x, LOW], self.xb.at[group(g)], self.x_sems, g, me.plane(1)
-        )
-        self.y[g] = send(
-            self.half.at[group(g), 1 - me.y, :, HIGH], self.yb.at[group(g)], self.y_sems, g, me.plane(2)
-        )
+                piece = half.at[group(g), me.y_of[k], me.x_of[k]]
+                self.d.send(piece, self.db.at[k - 1, group(g)], self.d_in[g], me.plane(k))
+        else:
+            self.x.send(half.at[group(g), :, 1 - me.x, LOW], self.xb.at[group(g)], self.x_in[g], me.plane(1))
+            self.y.send(half.at[group(g), 1 - me.y, :, HIGH], self.yb.at[group(g)], self.y_in[g], me.plane(2))
+
+    def z_send(self, g, n):
+        me = self.me
+        for k in range(1, 4):
+            self.zf.send(
+                self.half.at[GROUPS[g][0] + n, :, :, me.z_flip[k]], self.zq.at[k - 1, n], self.zf_in, me.line(2 * k)
+            )
 
     def z_sum(self, g):
         me, half, (first, last) = self.me, self.half, GROUPS[g]
-        for k in range(1, 4):
-            self.z[g, k].wait_recv()
+        drain(self.zq, self.zf_in)
         for j in range(first, last):
             total = half[j, :, :, me.z].astype(f32)
             for k in range(3):
                 total = total + self.zq[k, j - first].astype(f32)
             half[j, :, :, me.z] = total.astype(bf16)
-        for k, sems in enumerate((self.x_sems, self.y_sems, self.u_sems)):
-            other = flipped(me.p, k + 1)
-            self.q[k] = send(
-                half.at[group(g), other // 2, other % 2, me.z], self.pq.at[k], sems, g, me.plane(k + 1)
-            )
+        for k in range(1, 4):
+            piece = half.at[group(g), me.y_of[k], me.x_of[k], me.z]
+            self.q.send(piece, self.pq.at[k - 1], self.q_in, me.plane(k))
 
     def plane_sum(self, g):
-        for k in range(3):
-            self.q[k].wait_recv()
+        drain(self.pq, self.q_in)
         self.finish_sum(g, [lambda j, k=k: self.pq[k, j - GROUPS[g][0]] for k in range(3)])
 
     def first_sum(self, g):
         me, half, (first, last) = self.me, self.half, GROUPS[g]
-        self.x[g].wait_recv()
+        drain(self.xb.at[group(g)], self.x_in[g])
 
         def add_x(i, _):
             j, q = first + i // 2, i % 2
@@ -892,8 +956,8 @@
             return 0
 
         lax.fori_loop(0, (last - first) * 2, add_x, 0)
-        self.u[g] = send(half.at[group(g), 1 - me.y, me.x, LOW], self.ub.at[group(g)], self.u_sems, g, me.plane(2))
-        self.y[g].wait_recv()
+        self.u.send(half.at[group(g), 1 - me.y, me.x, LOW], self.ub.at[group(g)], self.u_in[g], me.plane(2))
+        drain(self.yb.at[group(g)], self.y_in[g])
 
         def add_y(i, _):
             j, q = first + i // 2, i % 2
@@ -902,26 +966,37 @@
             return 0
 
         lax.fori_loop(0, (last - first) * 2, add_y, 0)
-        self.v[g] = send(half.at[group(g), me.y, 1 - me.x, HIGH], self.vb.at[group(g)], self.v_sems, g, me.plane(1))
+        self.v.send(half.at[group(g), me.y, 1 - me.x, HIGH], self.vb.at[group(g)], self.v_in[g], me.plane(1))
+
+    def direct_sum(self, g):
+        me, half = self.me, self.half
+        drain(self.db.at[:, group(g)], self.d_in[g])
+        for j in range(*GROUPS[g]):
+            total = half[j, me.y, me.x].astype(f32)
+            for k in range(3):
+                total = total + self.db[k, j].astype(f32)
+            half[j, me.y, me.x] = total.astype(bf16)
+        self.send_z(g)
 
     def second_sum(self, g):
         me, half = self.me, self.half
-        self.u[g].wait_recv()
-        self.v[g].wait_recv()
+        drain(self.ub.at[group(g)], self.u_in[g])
+        drain(self.vb.at[group(g)], self.v_in[g])
         for j in range(*GROUPS[g]):
             total = half[j, me.y, me.x, LOW].astype(f32) + self.ub[j].astype(f32)
             half[j, me.y, me.x, LOW] = total.astype(bf16)
             total = half[j, me.y, me.x, HIGH].astype(f32) + self.vb[j].astype(f32)
             half[j, me.y, me.x, HIGH] = total.astype(bf16)
+        self.send_z(g)
+
+    def send_z(self, g):
+        me = self.me
         for k in range(1, 4):
-            self.z[g, k] = send(
-                half.at[group(g), me.y, me.x, flipped(me.z, k)], self.zb.at[k - 1, group(g)],
-                self.z_sems, g * 3 + k - 1, me.line(2 * k),
-            )
+            piece = self.half.at[group(g), me.y, me.x, me.z_flip[k]]
+            self.z.send(piece, self.zb.at[k - 1, group(g)], self.z_in[g], me.line(2 * k))
 
     def last_sum(self, g):
-        for k in range(1, 4):
-            self.z[g, k].wait_recv()
+        drain(self.zb.at[:, group(g)], self.z_in[g])
         self.finish_sum(g, [lambda j, k=k: self.zb[k, j] for k in range(3)])
 
     def finish_sum(self, g, terms):
@@ -935,22 +1010,20 @@
             self.squares.append(jnp.sum(jnp.square(total.astype(f32)).reshape(4, 8, 256), axis=0))
         piece = self.out.at[group(g), me.p]
         for k in range(1, 4):
-            self.r[g, k] = send(piece, piece, self.r_sems, g * 3 + k - 1, me.plane(k))
+            self.r.send(piece, piece, self.r_in, me.plane(k))
 
     def film_start(self):
         me = self.me
         self.film_all[me.p, me.w] = self.film_grad[me.w]
-        self.g = [
-            send(self.film_grad.at[flipped(me.w, l)], self.film_all.at[me.p, me.w], self.g_sems, l - 1, me.line(l))
-            for l in range(1, 8)
-        ]
+        for l in range(1, 8):
+            self.g.send(self.film_grad.at[me.w_flip[l]], self.film_all.at[me.p, me.w], self.g_in, me.line(l))
 
     def film_hop(self):
         me = self.me
-        for copy in self.g:
-            copy.wait()
+        drain(self.film_all.at[0, 0:7], self.g_in)
         piece = self.film_all.at[me.p]
-        self.h = [send(piece, piece, self.h_sems, k - 1, me.plane(k)) for k in range(1, 4)]
+        for k in range(1, 4):
+            self.h.send(piece, piece, self.h_in, me.plane(k))
 
     def film_inputs(self):
         row, col = iota((128, 512), 0), iota((128, 512), 1)
@@ -962,8 +1035,7 @@
 
     def film_products(self):
         me = self.me
-        for copy in self.h:
-            copy.wait()
+        drain(self.film_all.at[0:3], self.h_in)
         copies = [self.film_all[k].reshape(128, 128).astype(f32) for k in range(4)]
         total = split2((copies[0] + copies[1]) + (copies[2] + copies[3]))
         row, col = iota((128, 128), 0), iota((128, 128), 1)
@@ -975,10 +1047,8 @@
             for q in range(4)
         ]
         self.back_part[...] = quarter_rows(parts).astype(bf16).reshape(8, 16, 256)
-        self.b = [
-            send(self.back_part.at[flipped(me.w, l)], self.back_line.at[me.w], self.b_sems, l - 1, me.line(l))
-            for l in range(1, 8)
-        ]
+        for l in range(1, 8):
+            self.b.send(self.back_part.at[me.w_flip[l]], self.back_line.at[me.w], self.b_in, me.line(l))
         self.back_line[me.w] = self.back_part[me.w]
         square = jnp.zeros((8, 256), f32)
         turned = [part.T for part in total]
@@ -991,33 +1061,50 @@
 
     def film_back(self):
         me = self.me
-        for copy in self.b:
-            copy.wait()
+        drain(self.back_line.at[0:7], self.b_in)
         total = jnp.sum(self.back_line[...].astype(f32), axis=0)
         slope = mish_parts(self.obs_all[me.p, me.w].astype(f32))[1]
         self.back[0] = unfold_rows(total * slope)
 
-    def norm(self, hello):
+    def norm(self, hello, native):
         me = self.me
         total = sum(self.squares)
-        piece = self.all_squares.at[me.p, me.w]
-        self.all_squares[me.p, me.w] = jnp.sum(total[:, :128] + total[:, 128:], axis=0, keepdims=True)
+        here = me.p * 8 + me.w
+        piece = self.all_squares.at[here]
+        self.all_squares[here] = jnp.sum(total[:, :128] + total[:, 128:], axis=0, keepdims=True)
         pl.semaphore_wait(hello, len(me.others()))
-        copies = [
-            send(piece, piece, self.n_sems, i - 1, (flipped(me.p, i % 4), flipped(me.w, i // 4))) for i in range(1, 32)
-        ]
-        for copy in copies + list(self.r.values()):
-            copy.wait()
+        for i in range(1, 32):
+            self.n.send(piece, piece, self.n_in, (me.p_flip[i % 4], me.w_flip[i // 4]))
+        drain(self.zb, self.r_in)
+        native()
+        drain(self.all_squares.at[0:31], self.n_in)
         self.square[...] = jnp.sum(self.all_squares[...].reshape(32, 128), axis=0, keepdims=True)
-        for copies in (self.c, self.x, self.y, self.u, self.v, self.z, self.q):
-            for copy in copies.values():
-                copy.wait_send()
+
+    def finish(self):
+        size = lambda gs: sum(GROUPS[g][1] - GROUPS[g][0] for g in gs)
+        staged = size(self.staged)
+        self.c.finish(self.grad.at[:, :, :, 0])
+        self.x.finish(self.xb.at[0:staged])
+        self.y.finish(self.yb.at[0:staged])
+        self.u.finish(self.ub.at[0:staged])
+        self.v.finish(self.vb.at[0:staged])
+        self.d.finish(self.db.at[:, 0 : size(PLANE_DIRECT)])
+        self.z.finish(self.zb.at[:, 0 : staged + size(PLANE_DIRECT)])
+        self.zf.finish(self.zq)
+        self.q.finish(self.pq)
+        self.r.finish(self.zb)
+        self.g.finish(self.film_all.at[0, 0:7])
+        self.h.finish(self.film_all.at[0:3])
+        self.b.finish(self.back_line.at[0:7])
+        self.n.finish(self.all_squares.at[0:31])
 
 
 GATHER_GROUPS = ((0, 1), (1, 3), (3, 5), (5, 7), (7, 9))
 GATHER_DIRECT = (3, 4)
-GROUPS = ((0, 1), (1, 3), (3, 5), (5, 7), (7, 9))
-Z_FIRST = 4
+GROUPS = ((0, 1), (1, 3), (3, 5), (5, 7), (7, 8), (8, 9))
+Z_FIRST = 3
+PLANE_DIRECT = (0,)
+SEMAPHORES = 109
 LOW, HIGH = pl.ds(0, 2), pl.ds(2, 2)
 
 
@@ -1030,21 +1117,37 @@
 
 
 def step_kernel(*refs):
-    (params, order, obs, slots, noisy, mask, levels, cotangent, table,
-     act, noisy_grad, back, out, film_out, square,
-     own, weights, seen, obs_all, film, film_part, film_line, grad, film_grad) = refs[:24]
-    buffers, sems, hello = refs[24:38], refs[38:-1], refs[-1]
-    pairs = [(sems[2 * i], sems[2 * i + 1]) for i in range(20)]
+    params_out = refs[16]
+    targets = (params_out,) + refs[19:27]
+    loads = [
+        pltpu.make_async_copy(source, target, refs[-2].at[i])
+        for i, (source, target) in enumerate(zip(refs[:11], targets + refs[17:19]))
+    ]
+    for i in (0, 2, 1, 3, 4, 5, 6, 7, 8):
+        loads[i].start()
+    refs = targets + refs[9:11] + refs[11:16] + refs[17:19] + refs[27:-2] + refs[-1:]
+    (params, order, obs, slots, noisy, mask, levels, cotangent, table, first, second,
+     act, noisy_grad, back, native, square, first_out, second_out,
+     own, weights, seen, obs_all, film, film_part, film_line, grad, film_grad, out, film_out) = refs[:29]
+    buffers, (semaphores, local_sem, hello) = refs[29:44], refs[44:]
+    pool = Pool(semaphores)
     me = Place()
-    gather = Gather(me, own, weights, seen, obs_all, film, film_part, film_line, pairs[:9] + [sems[40]])
-    scatter = Scatter(me, grad, film_grad, obs_all, film, out, film_out, back, square, buffers, pairs[9:])
+    gather = Gather(me, own, weights, seen, obs_all, film, film_part, film_line, pool, local_sem)
+    scatter = Scatter(me, grad, film_grad, obs_all, film, out, film_out, back, square, buffers, pool)
+    greet(me)
+    loads[0].wait()
+    loads[1].wait()
+    pack_first(params, order, own)
+    loads[2].wait()
     obs_all[me.p, me.w] = fold_rows(obs[0].astype(f32)).astype(bf16)
-    greet(me)
-    pack_rows(params, order, own, film)
     meet(me)
+    gather.start_rows(0)
     gather.start_obs()
-    gather.start_rows(0)
+    pack_rest(params, own, film)
+    gather.start_local()
     gather.start_rows(1)
+    for i in range(3, 9):
+        loads[i].wait()
 
     def reach(point):
         if point == 0:
@@ -1060,11 +1163,11 @@
             gather.last_hop(0)
             for device in me.others():
                 pl.semaphore_signal(hello, inc=1, device_id=device, device_id_type=MESH)
+            gather.arrived(0)
+        if point == 1:
             gather.first_hop(3)
             gather.second_hop(2)
             gather.last_hop(1)
-            gather.arrived(0)
-        if point == 1:
             gather.film_done()
         if point == 2:
             gather.first_hop(4)
@@ -1078,11 +1181,16 @@
             gather.arrived(3)
         if point == 6:
             gather.obs_hop()
+            loads[9].start()
+            loads[10].start()
             gather.arrived(4)
         if point == 8:
+            scatter.start(5)
             scatter.start(4)
+        if point == 15:
+            scatter.core_sum(5)
+            scatter.core_sum(4)
         if point == 9:
-            scatter.core_sum(4)
             scatter.start(3)
         if point == 10:
             scatter.core_sum(3)
@@ -1090,37 +1198,46 @@
             scatter.start(2)
         if point == 12:
             scatter.core_sum(2)
-            scatter.first_sum(3)
+            scatter.first_sum(5)
+            scatter.first_sum(4)
         if point == 13:
             scatter.film_start()
+            scatter.z_send(Z_FIRST, 1)
             scatter.start(1)
+        if point == 14:
+            scatter.start(0)
+            scatter.core_sum(1)
+            scatter.second_sum(5)
+            scatter.second_sum(4)
+            scatter.core_sum(0)
+            scatter.first_sum(2)
 
     train_body(
         Stacked(weights), seen, slots, noisy, mask, levels, cotangent, table,
         act, noisy_grad, Stacked(grad), film_grad, reach,
     )
-    scatter.start(0)
-    scatter.core_sum(1)
-    scatter.first_sum(2)
-    scatter.core_sum(0)
-    scatter.second_sum(3)
-    scatter.z_sum(4)
+    scatter.film_hop()
     scatter.first_sum(1)
-    scatter.film_hop()
+    gather.obs_done()
+    scatter.film_inputs()
     scatter.second_sum(2)
-    scatter.first_sum(0)
-    gather.finish()
-    scatter.film_inputs()
-    scatter.plane_sum(4)
+    scatter.z_sum(3)
+    scatter.film_products()
     scatter.second_sum(1)
-    scatter.film_products()
-    scatter.second_sum(0)
-    scatter.last_sum(3)
+    scatter.direct_sum(0)
+    scatter.plane_sum(3)
+    scatter.last_sum(5)
+    scatter.last_sum(4)
     scatter.last_sum(2)
     scatter.last_sum(1)
     scatter.film_back()
     scatter.last_sum(0)
-    scatter.norm(hello)
+    loads[9].wait()
+    loads[10].wait()
+    scatter.norm(hello, lambda: native_grads(Blocks(out), film_out, order, native))
+    gather.finish()
+    scatter.finish()
+    assert pool.used <= SEMAPHORES
 
 
 class Stacked:
@@ -1142,10 +1259,14 @@
         self.ref[block // 4, block % 4, :, :, :, cols] = value.reshape(4, 2, ROWS, value.shape[-1])
 
 
-def step(params, obs, slots, noisy, mask, levels, cotangent):
+def step(params, obs, slots, noisy, mask, levels, cotangent, first, second):
     vmem = pl.BlockSpec(memory_space=pltpu.VMEM)
-    pair = lambda n: [pltpu.SemaphoreType.DMA((n,))] * 2
-    n, count, parts = NB // 4, len(GROUPS), len(GATHER_GROUPS)
+    n = NB // 4
+    inputs = (
+        params, jnp.asarray(first_order(), bf16), obs, slots, noisy, mask, levels, cotangent,
+        jnp.asarray(level_table(), bf16), first, second,
+    )
+    inputs = tuple(pltpu.with_memory_space_constraint(v, pltpu.HBM) for v in inputs)
     low = lambda *shape: pltpu.VMEM(shape, bf16)
     return pl.pallas_call(
         step_kernel,
@@ -1153,13 +1274,14 @@
             jax.ShapeDtypeStruct((C, 256), bf16),
             jax.ShapeDtypeStruct((ADIM, 256), f32),
             jax.ShapeDtypeStruct((1, 4, OBS), f32),
-            jax.ShapeDtypeStruct((n, 4, ROWS, 256), bf16),
-            jax.ShapeDtypeStruct((4 * ROWS, OBS), f32),
+            jax.ShapeDtypeStruct((ROWS, Q), f32),
             jax.ShapeDtypeStruct((1, 128), f32),
+            *[jax.ShapeDtypeStruct((ROWS, Q), f32)] * 3,
         ),
-        in_specs=[vmem] * 9,
-        out_specs=(vmem,) * 6,
+        in_specs=[pl.BlockSpec(memory_space=pltpu.HBM)] * 11,
+        out_specs=(vmem,) * 8,
         scratch_shapes=[
+            *(pltpu.VMEM(v.shape, v.dtype) for v in inputs[1:9]),
             low(n, 4, ROWS, 256),
             low(n, 4, 4, 2, ROWS, 256),
             pltpu.VMEM((4, 4, 8, 128), f32),
@@ -1169,6 +1291,8 @@
             pltpu.VMEM((8, 8, 128), f32),
             low(n, 4, 4, 2, ROWS, 256),
             low(8, SAM, 128),
+            low(n, 4, ROWS, 256),
+            pltpu.VMEM((4 * ROWS, OBS), f32),
             low(n, 2, 2, 4, ROWS, 256),
             low(n, 4, 4, ROWS, 256),
             low(n, 2, 2, ROWS, 256),
@@ -1178,30 +1302,30 @@
             low(3, n, ROWS, 256),
             low(3, GROUPS[Z_FIRST][1] - GROUPS[Z_FIRST][0], 2, 2, ROWS, 256),
             low(3, GROUPS[Z_FIRST][1] - GROUPS[Z_FIRST][0], ROWS, 256),
+            low(3, GROUPS[max(PLANE_DIRECT)][1], 4, ROWS, 256),
             low(4, 8, 16, 128),
             low(8, 16, 256),
             low(8, 16, 256),
             low(4, 128, 256),
-            pltpu.VMEM((4, 8, 1, 128), f32),
-            *pair(7), *pair(7), *pair(3), *pair(3),
-            *pair(3 * parts), *pair(3 * parts), *pair(3 * parts), *pair(3 * parts), *pair(parts),
-            *pair(7), *pair(3), *pair(7),
-            *pair(count), *pair(count), *pair(count), *pair(count), *pair(count),
-            *pair(3 * count), *pair(3 * count), *pair(31),
+            pltpu.VMEM((32, 1, 128), f32),
+            pltpu.SemaphoreType.DMA((SEMAPHORES,)),
             pltpu.SemaphoreType.DMA,
+            pltpu.SemaphoreType.DMA((11,)),
             pltpu.SemaphoreType.REGULAR,
         ],
-        compiler_params=pltpu.CompilerParams(collective_id=0, has_side_effects=True, vmem_limit_bytes=60 << 20),
+        compiler_params=pltpu.CompilerParams(collective_id=0, has_side_effects=True, vmem_limit_bytes=34 << 20),
+        cost_estimate=pl.CostEstimate(flops=3 * 10**9, bytes_accessed=200 * 10**6, transcendentals=10**6),
         name="step",
-    )(params, jnp.asarray(first_order(), bf16), obs, slots, noisy, mask, levels, cotangent, jnp.asarray(level_table(), bf16))
+    )(*inputs)
 
 
 def local_fast(noisy, action_mask, time_index, obs_embed, obs_slot, cotangent, params, first_moment, second_moment):
-    act, noisy_grad, back, total, film_total, squares = step(
-        params, obs_embed, obs_slot[None], noisy[0], action_mask, time_index, cotangent[0]
+    act, noisy_grad, back, native, squares, params, first_moment, second_moment = step(
+        params, obs_embed, obs_slot[None], noisy[0], action_mask, time_index, cotangent[0],
+        first_moment, second_moment,
     )
     norm, *new, act, noisy_grad, back = adam(
-        total.reshape(NB, ROWS, 256), film_total, squares, params, first_moment, second_moment,
+        native, squares, params, first_moment, second_moment,
         (act, noisy_grad, back), ((1, C, 256), (ADIM, 1, 256), (1, 4, OBS)),
     )
     return (act, noisy_grad.transpose(1, 0, 2), back, norm.reshape(()), *new)

time: 83.8 us -> 75.6 us (0.902)
  Pallas kernels: 82.8 us -> 74.7 us
    pallas_call x1, Pallas kernels: 76 us -> 70.5 us  [step(): pl.pallas_call(step_kernel, out_shape=(jax.ShapeDtypeStruct((C, 256), bf1...]
    pallas_call x1, Pallas kernels: 6.83 us -> 4.15 us  [adam(): pl.pallas_call(functools.partial(adam_kernel, count), out_shape=(jax.Shap...]
where the time goes in v4:
time: 75.6 us; the launch traced here: 75.5 us
  Pallas kernels  74.7 us (99%)
  between operations  0.8 us (1%)
    pallas_call x1, Pallas kernels, step(): pl.pallas_call(step_kernel, out_shape=(jax.ShapeDtypeStruct((C, 256), bf1...  70.5 us
    pallas_call x1, Pallas kernels, adam(): pl.pallas_call(functools.partial(adam_kernel, count), out_shape=(jax.Shap...  4.15 us

profile of v4, /device:TPU:0, one launch (start us, length us, event | category | flops | bytes accessed | tf_op | source)
XLA Modules:
  0.0 75.5 jit_solution(1166758874193341827)
XLA Ops:
  0.6 70.5 %step.1 = (bf16[256,256]{1,0:T(8,128)(2,1)S(1)}, f32[10,256]{1,0:T(8,128)S(1)}, f32[1,4,1024]{2,1,0:T(4,128)S(1)}, f32[32,12627]{1,0:T(8,128)S(1)}, f32[1,128]{1...) custom-call(f32[32,12627]{1,0:T(8,128)} %refs_0_.1, ...), custom_call_target="tpu_custom_call" | custom-call | flops 3000000000 | bytes 200000000 | tf_op jit(solution)/shard_map/step/pallas_call | solution.py:1271
  71.2 4.1 %adam.1 = (f32[1,1]{1,0:T(1,128)}, f32[32,12627]{1,0:T(8,128)}, f32[32,12627]{1,0:T(8,128)}, f32[32,12627]{1,0:T(8,128)}, bf16[32,12627]{1,0:T(8,128)(2,1)}, /*i...) custom-call(f32[32,12627]{1,0:T(8,128)S(1)} %get-tuple-element.24.refs_0_, ...), custom_call_target="tpu_custom_call" | custom-call | tf_op jit(solution)/shard_map/adam/pallas_call | solution.py:620

commit v5 on v4

--- a/solution.py
+++ b/solution.py
@@ -43,7 +43,6 @@
 AT_UP_RES = 9276
 B_MISC, B_INNER, B_OUTER, B_FILM = 0, 1, 2, 3
 B_DS, B_POOL, B_SPREAD, B_UF, B_US, B_UR = 5, 10, 13, 17, 27, 32
-B_NONE = (34, 35)
 LANE_TAIL = 64
 CONVS = (
     (50, 5, 2, lambda t, h: B_DS + t),
@@ -167,10 +166,8 @@
 
     for q in range(4):
         film_ref[q * ROWS : (q + 1) * ROWS] = low(AT_FILM[q], OBS)
-    own_ref[B_UR] = low(AT_UP_RES, 256)
-    own_ref[B_UR + 1] = low(AT_UP_RES + 256, 256)
-    for b in B_NONE:
-        own_ref[b] = jnp.zeros((ROWS, 256), bf16)
+    for i in range(4):
+        own_ref[B_UR + i, :, 0:128] = low(AT_UP_RES + i * 128, 128)
     for taps in (5, 3, 4):
         places = [(at, h, block) for at, k, groups, block in CONVS if k == taps for h in range(groups)]
         stacked = jnp.concatenate([low(at + h * 128 * taps, 128 * taps) for at, h, _ in places], axis=0)
@@ -299,6 +296,8 @@
 
 
 def train_kernel(*refs):
+    for b in range(B_UR, NB):
+        refs[10][b, :, 128:] = jnp.zeros((256, 128), bf16)
     train_body(*refs, lambda point: None)
 
 
@@ -310,8 +309,6 @@
     col = iota((256, 256), 1)
     ones = jnp.where((row >> 5) == (col >> 5), 1.0, 0.0).astype(bf16)
     swap = jnp.where(col == ((row & 15) << 4) + (row >> 4), 1.0, 0.0).astype(bf16)
-    for b in B_NONE:
-        grad_ref[b] = jnp.zeros((256, 256), bf16)
     spread_mask = one_hot((iota((SAM, 256), 1) >> 4) == iota((SAM, 256), 0))
     keep = dot_nn(mask_ref[...].astype(f32).astype(bf16), spread_mask)
     start_cols = noisy_ref[...].astype(f32) * keep
@@ -383,9 +380,12 @@
     odd_out = dot_nt(pooled_next, w_ref[B_SPREAD]) + dot_nt(pooled, w_ref[B_SPREAD + 2])
     wide = (interleave(even_out, odd_out) + vec(SB)).astype(bf16)
     joined = (wide, skip)
+    up_res = lambda h: jnp.concatenate([w_ref[B_UR + 2 * h + i, :, 0:128] for i in range(2)], axis=1)
     turned = upstream_low.T
     for h in range(2):
-        grad_ref[B_UR + h] = dot_nn(turned, joined[h]).astype(bf16)
+        product = dot_nn(turned, joined[h]).astype(bf16)
+        for i in range(2):
+            grad_ref[B_UR + 2 * h + i, :, 0:128] = product[:, i * 128 : (i + 1) * 128]
     reach(5)
     up_first = [lambda t, h=h: w_ref[B_UF + 2 * t + h] for h in range(2)]
     pre = conv_forward(wide, up_first[0]) + conv_forward(skip, up_first[1]) + vec(U_B1)
@@ -426,8 +426,8 @@
         conv_weights(low, joined[h], lambda t, h=h: B_UF + 2 * t + h)
     single_grads[U_RB] = row_sum(upstream)
     reach(9)
-    grad_wide = conv_source(low, up_first[0]) + dot_nn(upstream_low, w_ref[B_UR])
-    grad_skip = conv_source(low, up_first[1]) + dot_nn(upstream_low, w_ref[B_UR + 1])
+    grad_wide = conv_source(low, up_first[0]) + dot_nn(upstream_low, up_res(0))
+    grad_skip = conv_source(low, up_first[1]) + dot_nn(upstream_low, up_res(1))
     single_grads[SB] = row_sum(grad_wide)
     low_even, low_odd = halves(grad_wide.astype(bf16))
     turned_even, turned_odd = low_even.T, low_odd.T
@@ -495,7 +495,7 @@
     grad_ref[B_MISC, :, :128] = (misc_grad + stack.T).astype(bf16)
     grad_ref[B_MISC, :, 128:] = jnp.zeros((256, 128), bf16)
     reach(14)
-    result = act_four + dot_nt(wide, w_ref[B_UR]) + dot_nt(skip, w_ref[B_UR + 1]) + vec(U_RB)
+    result = act_four + dot_nt(wide, up_res(0)) + dot_nt(skip, up_res(1)) + vec(U_RB)
     act_ref[...] = dot_tn(result.astype(bf16), swap).astype(bf16)
     back = back + dot_nn(low, misc_first)
     grad_start = back[:, 50:60]
@@ -526,6 +526,11 @@
 
 
 def native_grads(own_ref, film_ref, order_ref, grad_ref):
+    native_most(own_ref, film_ref, grad_ref)
+    native_rest(own_ref, order_ref, grad_ref)
+
+
+def native_rest(own_ref, order_ref, grad_ref):
     misc = own_ref[B_MISC]
     first = dot_nt(misc[:, :128], order_ref[...])
     misc = misc.astype(f32)
@@ -534,12 +539,22 @@
     grad_ref[:, AT_TAIL : AT_TAIL + TAIL] = misc[:, LANE_TAIL : LANE_TAIL + TAIL]
     grad_ref[:, AT_TIME[0] : AT_TIME[0] + 256] = own_ref[B_INNER].astype(f32)
     grad_ref[:, AT_TIME[1] : AT_TIME[1] + 256] = own_ref[B_OUTER].astype(f32)
+    native_film(own_ref, grad_ref, 0)
+
+
+def native_film(own_ref, grad_ref, side):
+    for q in (2 * side, 2 * side + 1):
+        part = own_ref[B_FILM + side, :, (q % 2) * 128 : (q % 2) * 128 + 128]
+        grad_ref[:, AT_FILM[q] + OBS : AT_FILM[q] + OBS + TE] = part.astype(f32)
+
+
+def native_most(own_ref, film_ref, grad_ref):
     for q in range(4):
         grad_ref[:, AT_FILM[q] : AT_FILM[q] + OBS] = film_ref[q * ROWS : (q + 1) * ROWS]
-        part = own_ref[B_FILM + q // 2, :, (q % 2) * 128 : (q % 2) * 128 + 128]
-        grad_ref[:, AT_FILM[q] + OBS : AT_FILM[q] + OBS + TE] = part.astype(f32)
-    grad_ref[:, AT_UP_RES : AT_UP_RES + 256] = own_ref[B_UR].astype(f32)
-    grad_ref[:, AT_UP_RES + 256 : AT_UP_RES + 512] = own_ref[B_UR + 1].astype(f32)
+    native_film(own_ref, grad_ref, 1)
+    for i in range(4):
+        begin = AT_UP_RES + i * 128
+        grad_ref[:, begin : begin + 128] = own_ref[B_UR + i, :, 0:128].astype(f32)
     for taps in (5, 3, 4):
         places = [(at, h, block) for at, k, groups, block in CONVS if k == taps for h in range(groups)]
         stacked = jnp.concatenate(
@@ -589,23 +604,24 @@
         stores[n, at].start()
 
     width = 1024
-    for row in range(0, ROWS, 16):
+    for row in range(0, ROWS, 8):
         for begin in range(0, Q, width):
-            cols = slice(begin, min(begin + width, Q))
-            at = (slice(row, row + 16), cols)
+            at = (slice(row, row + 8), slice(begin, min(begin + width, Q)))
             clipped = grad_ref[at] * factor
             new_first = decay_first * old[1][at] + (1.0 - decay_first) * clipped
             new_second = decay_second * old[2][at] + (1.0 - decay_second) * clipped * clipped
             first_hat = new_first * (1.0 / (1.0 - decay_first**ADAM_STEP))
             second_hat = new_second * (1.0 / (1.0 - decay_second**ADAM_STEP))
             before = old[0][at]
-            after = before - learn_rate * (first_hat / (jnp.sqrt(second_hat) + adam_eps) + weight_decay * before)
-            new[0][at] = after
+            new[0][at] = before - learn_rate * (first_hat / (jnp.sqrt(second_hat) + adam_eps) + weight_decay * before)
             new[1][at] = new_first
             new[2][at] = new_second
-            new[3][at] = after.astype(bf16)
-        for n in range(4):
-            store(n, 16, row)
+        for n in range(3):
+            store(n, 8, row)
+        if row % 16:
+            rows = slice(row - 8, row + 8)
+            new[3][rows] = new[0][rows].astype(bf16)
+            store(3, 16, row - 8)
     for source, target in zip(extra_in, extra_out):
         target[...] = source[...].reshape(target.shape)
     for copy in stores.values():
@@ -771,7 +787,7 @@
         self.me, self.own, self.weights, self.seen, self.obs_all, self.film = me, own, weights, seen, obs_all, film
         self.film_part, self.film_line, self.local_sem = film_part, film_line, local_sem
         self.z, self.x, self.y, self.f, self.c, self.small = (Lane(pool) for _ in range(6))
-        self.parts, self.films, self.more = (Lane(pool) for _ in range(3))
+        self.parts, self.films, self.more, self.narrow = (Lane(pool) for _ in range(4))
         pieces = [(g, k) for g in range(len(GATHER_GROUPS)) for k in range(1, 4)]
         self.z_in = pool.several(pieces)
         near = [(g, k) for g, k in pieces if g not in GATHER_DIRECT] + list(GATHER_DIRECT)
@@ -788,9 +804,11 @@
 
     def start_rows(self, g):
         me = self.me
+        lane = self.narrow if g == NARROW else self.z
         for k in range(1, 4):
-            self.z.send(
-                self.own.at[gather_group(g), me.p], self.weights.at[gather_group(g), me.p, me.z, me.c],
+            lane.send(
+                self.own.at[gather_group(g), me.p, :, cols(g)],
+                self.weights.at[gather_group(g), me.p, me.z, me.c, :, cols(g)],
                 self.z_in[g, k], me.line(2 * k),
             )
 
@@ -830,21 +848,24 @@
 
     def first_hop(self, g):
         me = self.me
+        lanes = [self.narrow] * 3 if g == NARROW else [self.x, self.y, self.f]
         for k in range(1, 4):
-            piece = self.weights.at[gather_group(g), me.p, me.z_flip[k], me.c]
+            piece = self.weights.at[gather_group(g), me.p, me.z_flip[k], me.c, :, cols(g)]
             drain(piece, self.z_in[g, k])
             key = g if g in GATHER_DIRECT else (g, k)
-            self.x.send(piece, piece, self.x_in[key], me.plane(1))
-            self.y.send(piece, piece, self.y_in[key], me.plane(2))
+            lanes[0].send(piece, piece, self.x_in[key], me.plane(1))
+            lanes[1].send(piece, piece, self.y_in[key], me.plane(2))
             if g in GATHER_DIRECT:
-                self.f.send(piece, piece, self.f_in[g], me.plane(3))
+                lanes[2].send(piece, piece, self.f_in[g], me.plane(3))
+
+    def three(self, g):
+        return self.weights.at[gather_group(g), 0, 0:3, 0, :, cols(g)]
 
     def second_hop(self, g):
         me = self.me
         if g in GATHER_DIRECT:
-            three = self.weights.at[gather_group(g), 0, 0:3, 0]
-            drain(three, self.x_in[g])
-            drain(three, self.y_in[g])
+            drain(self.three(g), self.x_in[g])
+            drain(self.three(g), self.y_in[g])
             return
         for k in range(1, 4):
             one = self.weights.at[gather_group(g), 0, 0, 0]
@@ -859,21 +880,22 @@
             self.local.wait()
         if g in GATHER_DIRECT:
             self.second_hop(g)
-        drain(self.weights.at[gather_group(g), 0, 0:3, 0], self.f_in[g])
-        piece = self.weights.at[gather_group(g), :, :, self.me.c]
-        self.c.send(piece, piece, self.c_in[g], self.me.line(1))
+        drain(self.three(g), self.f_in[g])
+        piece = self.weights.at[gather_group(g), :, :, self.me.c, :, cols(g)]
+        (self.narrow if g == NARROW else self.c).send(piece, piece, self.c_in[g], self.me.line(1))
 
     def arrived(self, g):
-        drain(self.weights.at[gather_group(g), :, :, 0], self.c_in[g])
+        drain(self.weights.at[gather_group(g), :, :, 0, :, cols(g)], self.c_in[g])
 
     def obs_done(self):
         drain(self.obs_all.at[0:3], self.more_in)
 
     def finish(self):
-        three = self.weights.at[:, 0, 0:3, 0]
+        wide = pl.ds(0, GATHER_GROUPS[NARROW][0])
         for lane in (self.z, self.x, self.y, self.f):
-            lane.finish(three)
-        self.c.finish(self.weights.at[:, :, :, 0])
+            lane.finish(self.weights.at[wide, 0, 0:3, 0])
+        self.c.finish(self.weights.at[wide, :, :, 0])
+        self.narrow.finish(self.weights.at[0:7, :, 0, 0, :, cols(NARROW)])
         self.small.finish(self.obs_all.at[0, 0:7])
         self.parts.finish(self.film_line.at[0:7])
         self.films.finish(self.seen.at[0:3])
@@ -888,6 +910,7 @@
          self.film_all, self.back_part, self.back_line, self.cond, self.all_squares) = buffers
         self.c, self.x, self.y, self.u, self.v, self.z = (Lane(pool) for _ in range(6))
         self.zf, self.q, self.d, self.r, self.g, self.h, self.b, self.n = (Lane(pool) for _ in range(8))
+        self.narrow, self.narrow_end = Lane(pool), Lane(pool)
         groups = range(len(GROUPS))
         self.staged = [g for g in groups if g != Z_FIRST and g not in PLANE_DIRECT]
         self.c_in = pool.several(groups)
@@ -895,20 +918,25 @@
         self.d_in = pool.several(PLANE_DIRECT)
         self.z_in = pool.several(g for g in groups if g != Z_FIRST)
         self.zf_in, self.q_in, self.r_in, self.g_in, self.h_in, self.b_in, self.n_in = (pool.new() for _ in range(7))
+        self.narrow_in, self.r_last = pool.new(), pool.new()
         self.squares = []
 
     def start(self, g):
         me = self.me
-        self.c.send(self.grad.at[group(g), :, :, 1 - me.c], self.core.at[group(g)], self.c_in[g], me.line(1))
+        lane = self.narrow if g == NARROW else self.c
+        lane.send(
+            self.grad.at[group(g), :, :, 1 - me.c, :, cols(g)], self.core.at[group(g), :, :, :, cols(g)],
+            self.c_in[g], me.line(1),
+        )
 
     def core_sum(self, g):
         me, half, (first, last) = self.me, self.half, GROUPS[g]
-        drain(self.core.at[group(g)], self.c_in[g])
+        drain(self.core.at[group(g), :, :, :, cols(g)], self.c_in[g])
 
         def add(i, _):
             j, q = first + i // 4, i % 4
-            total = self.grad[j, q, :, me.c].astype(f32) + self.core[j, q].astype(f32)
-            half[j, q // 2, q % 2] = total.astype(bf16)
+            total = self.grad[j, q, :, me.c, :, cols(g)].astype(f32) + self.core[j, q, :, :, cols(g)].astype(f32)
+            half[j, q // 2, q % 2, :, :, cols(g)] = total.astype(bf16)
             return 0
 
         lax.fori_loop(0, (last - first) * 4, add, 0)
@@ -919,8 +947,15 @@
                 piece = half.at[group(g), me.y_of[k], me.x_of[k]]
                 self.d.send(piece, self.db.at[k - 1, group(g)], self.d_in[g], me.plane(k))
         else:
-            self.x.send(half.at[group(g), :, 1 - me.x, LOW], self.xb.at[group(g)], self.x_in[g], me.plane(1))
-            self.y.send(half.at[group(g), 1 - me.y, :, HIGH], self.yb.at[group(g)], self.y_in[g], me.plane(2))
+            lanes = [self.narrow] * 2 if g == NARROW else [self.x, self.y]
+            lanes[0].send(
+                half.at[group(g), :, 1 - me.x, LOW, :, cols(g)], self.xb.at[group(g), :, :, :, cols(g)],
+                self.x_in[g], me.plane(1),
+            )
+            lanes[1].send(
+                half.at[group(g), 1 - me.y, :, HIGH, :, cols(g)], self.yb.at[group(g), :, :, :, cols(g)],
+                self.y_in[g], me.plane(2),
+            )
 
     def z_send(self, g, n):
         me = self.me
@@ -947,26 +982,33 @@
 
     def first_sum(self, g):
         me, half, (first, last) = self.me, self.half, GROUPS[g]
-        drain(self.xb.at[group(g)], self.x_in[g])
+        lanes = [self.narrow] * 2 if g == NARROW else [self.u, self.v]
+        drain(self.xb.at[group(g), :, :, :, cols(g)], self.x_in[g])
 
         def add_x(i, _):
             j, q = first + i // 2, i % 2
-            total = half[j, q, me.x, LOW].astype(f32) + self.xb[j, q].astype(f32)
-            half[j, q, me.x, LOW] = total.astype(bf16)
+            total = half[j, q, me.x, LOW, :, cols(g)].astype(f32) + self.xb[j, q, :, :, cols(g)].astype(f32)
+            half[j, q, me.x, LOW, :, cols(g)] = total.astype(bf16)
             return 0
 
         lax.fori_loop(0, (last - first) * 2, add_x, 0)
-        self.u.send(half.at[group(g), 1 - me.y, me.x, LOW], self.ub.at[group(g)], self.u_in[g], me.plane(2))
-        drain(self.yb.at[group(g)], self.y_in[g])
+        lanes[0].send(
+            half.at[group(g), 1 - me.y, me.x, LOW, :, cols(g)], self.ub.at[group(g), :, :, cols(g)],
+            self.u_in[g], me.plane(2),
+        )
+        drain(self.yb.at[group(g), :, :, :, cols(g)], self.y_in[g])
 
         def add_y(i, _):
             j, q = first + i // 2, i % 2
-            total = half[j, me.y, q, HIGH].astype(f32) + self.yb[j, q].astype(f32)
-            half[j, me.y, q, HIGH] = total.astype(bf16)
+            total = half[j, me.y, q, HIGH, :, cols(g)].astype(f32) + self.yb[j, q, :, :, cols(g)].astype(f32)
+            half[j, me.y, q, HIGH, :, cols(g)] = total.astype(bf16)
             return 0
 
         lax.fori_loop(0, (last - first) * 2, add_y, 0)
-        self.v.send(half.at[group(g), me.y, 1 - me.x, HIGH], self.vb.at[group(g)], self.v_in[g], me.plane(1))
+        lanes[1].send(
+            half.at[group(g), me.y, 1 - me.x, HIGH, :, cols(g)], self.vb.at[group(g), :, :, cols(g)],
+            self.v_in[g], me.plane(1),
+        )
 
     def direct_sum(self, g):
         me, half = self.me, self.half
@@ -980,37 +1022,44 @@
 
     def second_sum(self, g):
         me, half = self.me, self.half
-        drain(self.ub.at[group(g)], self.u_in[g])
-        drain(self.vb.at[group(g)], self.v_in[g])
+        drain(self.ub.at[group(g), :, :, cols(g)], self.u_in[g])
+        drain(self.vb.at[group(g), :, :, cols(g)], self.v_in[g])
         for j in range(*GROUPS[g]):
-            total = half[j, me.y, me.x, LOW].astype(f32) + self.ub[j].astype(f32)
-            half[j, me.y, me.x, LOW] = total.astype(bf16)
-            total = half[j, me.y, me.x, HIGH].astype(f32) + self.vb[j].astype(f32)
-            half[j, me.y, me.x, HIGH] = total.astype(bf16)
+            for part, more in ((LOW, self.ub), (HIGH, self.vb)):
+                total = half[j, me.y, me.x, part, :, cols(g)].astype(f32) + more[j, :, :, cols(g)].astype(f32)
+                half[j, me.y, me.x, part, :, cols(g)] = total.astype(bf16)
         self.send_z(g)
 
     def send_z(self, g):
         me = self.me
+        lane = self.narrow_end if g == NARROW else self.z
         for k in range(1, 4):
-            piece = self.half.at[group(g), me.y, me.x, me.z_flip[k]]
-            self.z.send(piece, self.zb.at[k - 1, group(g)], self.z_in[g], me.line(2 * k))
+            piece = self.half.at[group(g), me.y, me.x, me.z_flip[k], :, cols(g)]
+            lane.send(piece, self.zb.at[k - 1, group(g), :, cols(g)], self.z_in[g], me.line(2 * k))
 
     def last_sum(self, g):
-        drain(self.zb.at[:, group(g)], self.z_in[g])
-        self.finish_sum(g, [lambda j, k=k: self.zb[k, j] for k in range(3)])
+        drain(self.zb.at[:, group(g), :, cols(g)], self.z_in[g])
+        self.finish_sum(g, [lambda j, k=k: self.zb[k, j, :, cols(g)] for k in range(3)])
 
     def finish_sum(self, g, terms):
         me = self.me
         for j in range(*GROUPS[g]):
-            total = self.half[j, me.y, me.x, me.z].astype(f32)
+            total = self.half[j, me.y, me.x, me.z, :, cols(g)].astype(f32)
             for term in terms:
                 total = total + term(j).astype(f32)
             total = total.astype(bf16)
-            self.out[j, me.p] = total
-            self.squares.append(jnp.sum(jnp.square(total.astype(f32)).reshape(4, 8, 256), axis=0))
-        piece = self.out.at[group(g), me.p]
+            self.out[j, me.p, :, cols(g)] = total
+            self.count(jnp.square(total.astype(f32)))
+        piece = self.out.at[group(g), me.p, :, cols(g)]
+        lane, arrival = (self.narrow_end, self.narrow_in) if g == NARROW else (self.r, self.r_in)
+        if g == 0:
+            arrival = self.r_last
         for k in range(1, 4):
-            self.r.send(piece, piece, self.r_in, me.plane(k))
+            lane.send(piece, piece, arrival, me.plane(k))
+
+    def count(self, squares):
+        folded = jnp.sum(squares.reshape(-1, 8, squares.shape[1]), axis=0)
+        self.squares += [folded[:, i : i + 128] for i in range(0, squares.shape[1], 128)]
 
     def film_start(self):
         me = self.me
@@ -1050,14 +1099,12 @@
         for l in range(1, 8):
             self.b.send(self.back_part.at[me.w_flip[l]], self.back_line.at[me.w], self.b_in, me.line(l))
         self.back_line[me.w] = self.back_part[me.w]
-        square = jnp.zeros((8, 256), f32)
         turned = [part.T for part in total]
         for q in range(4):
             cond = self.cond[q]
             product = dot_nn(turned[0], cond) + dot_nn(turned[1], cond)
             self.film_out[:, q * 256 : (q + 1) * 256] = product
-            square = square + jnp.sum(jnp.square(product).reshape(16, 8, 256), axis=0)
-        self.squares.append(0.25 * square)
+            self.count(0.25 * jnp.square(product))
 
     def film_back(self):
         me = self.me
@@ -1066,24 +1113,27 @@
         slope = mish_parts(self.obs_all[me.p, me.w].astype(f32))[1]
         self.back[0] = unfold_rows(total * slope)
 
-    def norm(self, hello, native):
+    def norm(self, hello, most, rest):
         me = self.me
         total = sum(self.squares)
         here = me.p * 8 + me.w
         piece = self.all_squares.at[here]
-        self.all_squares[here] = jnp.sum(total[:, :128] + total[:, 128:], axis=0, keepdims=True)
+        self.all_squares[here] = jnp.sum(total, axis=0, keepdims=True)
         pl.semaphore_wait(hello, len(me.others()))
         for i in range(1, 32):
             self.n.send(piece, piece, self.n_in, (me.p_flip[i % 4], me.w_flip[i // 4]))
-        drain(self.zb, self.r_in)
-        native()
+        drain(self.zb.at[:, GROUPS[0][1] : GROUPS[NARROW][0]], self.r_in)
+        drain(self.zb.at[:, 0:1, :, cols(NARROW)], self.narrow_in)
+        most()
+        drain(self.zb.at[:, group(0)], self.r_last)
+        rest()
         drain(self.all_squares.at[0:31], self.n_in)
         self.square[...] = jnp.sum(self.all_squares[...].reshape(32, 128), axis=0, keepdims=True)
 
     def finish(self):
-        size = lambda gs: sum(GROUPS[g][1] - GROUPS[g][0] for g in gs)
-        staged = size(self.staged)
-        self.c.finish(self.grad.at[:, :, :, 0])
+        size = lambda gs: sum(GROUPS[g][1] - GROUPS[g][0] for g in gs if g != NARROW)
+        staged, wide = size(self.staged), pl.ds(0, GROUPS[NARROW][0])
+        self.c.finish(self.grad.at[wide, :, :, 0])
         self.x.finish(self.xb.at[0:staged])
         self.y.finish(self.yb.at[0:staged])
         self.u.finish(self.ub.at[0:staged])
@@ -1092,20 +1142,29 @@
         self.z.finish(self.zb.at[:, 0 : staged + size(PLANE_DIRECT)])
         self.zf.finish(self.zq)
         self.q.finish(self.pq)
-        self.r.finish(self.zb)
+        self.r.finish(self.zb.at[:, wide])
+        self.narrow.finish(self.grad.at[0:7, :, 0, 0, :, cols(NARROW)])
+        self.narrow_end.finish(self.zb.at[:, 0:2, :, cols(NARROW)])
         self.g.finish(self.film_all.at[0, 0:7])
         self.h.finish(self.film_all.at[0:3])
         self.b.finish(self.back_line.at[0:7])
         self.n.finish(self.all_squares.at[0:31])
 
 
-GATHER_GROUPS = ((0, 1), (1, 3), (3, 5), (5, 7), (7, 9))
-GATHER_DIRECT = (3, 4)
+GATHER_GROUPS = ((0, 1), (1, 3), (3, 5), (5, 7), (7, 8), (8, 9))
+GATHER_DIRECT = (4, 5)
 GROUPS = ((0, 1), (1, 3), (3, 5), (5, 7), (7, 8), (8, 9))
 Z_FIRST = 3
 PLANE_DIRECT = (0,)
-SEMAPHORES = 109
+SEMAPHORES = 125
 LOW, HIGH = pl.ds(0, 2), pl.ds(2, 2)
+
+
+NARROW = 5
+
+
+def cols(g):
+    return pl.ds(0, 128 if g == NARROW else 256)
 
 
 def group(g):
@@ -1159,8 +1218,8 @@
             gather.second_hop(0)
             gather.film_hop()
             gather.first_hop(2)
+            gather.last_hop(0)
             gather.second_hop(1)
-            gather.last_hop(0)
             for device in me.others():
                 pl.semaphore_signal(hello, inc=1, device_id=device, device_id_type=MESH)
             gather.arrived(0)
@@ -1170,14 +1229,17 @@
             gather.last_hop(1)
             gather.film_done()
         if point == 2:
+            gather.arrived(1)
             gather.first_hop(4)
-            gather.arrived(1)
         if point == 3:
             gather.last_hop(2)
+            gather.second_hop(3)
+            gather.arrived(2)
+        if point == 4:
             gather.last_hop(3)
-            gather.arrived(2)
         if point == 5:
             gather.last_hop(4)
+            gather.first_hop(5)
             gather.arrived(3)
         if point == 6:
             gather.obs_hop()
@@ -1185,6 +1247,7 @@
             loads[10].start()
             gather.arrived(4)
         if point == 8:
+            gather.last_hop(5)
             scatter.start(5)
             scatter.start(4)
         if point == 15:
@@ -1192,6 +1255,7 @@
             scatter.core_sum(4)
         if point == 9:
             scatter.start(3)
+            gather.arrived(5)
         if point == 10:
             scatter.core_sum(3)
         if point == 11:
@@ -1234,7 +1298,11 @@
     scatter.last_sum(0)
     loads[9].wait()
     loads[10].wait()
-    scatter.norm(hello, lambda: native_grads(Blocks(out), film_out, order, native))
+    scatter.norm(
+        hello,
+        lambda: native_most(Blocks(out), film_out, native),
+        lambda: native_rest(Blocks(out), order, native),
+    )
     gather.finish()
     scatter.finish()
     assert pool.used <= SEMAPHORES

time: 75.6 us -> 74.4 us (0.984)
  Pallas kernels: 74.7 us -> 73.4 us
    pallas_call x1, Pallas kernels: 70.5 us -> 69.7 us  [step(): pl.pallas_call(step_kernel, out_shape=(jax.ShapeDtypeStruct((C, 256), bf1...]
where the time goes in v5:
time: 74.4 us; the launch traced here: 74.2 us
  Pallas kernels  73.4 us (99%)
  between operations  0.8 us (1%)
    pallas_call x1, Pallas kernels, step(): pl.pallas_call(step_kernel, out_shape=(jax.ShapeDtypeStruct((C, 256), bf1...  69.7 us
    pallas_call x1, Pallas kernels, adam(): pl.pallas_call(functools.partial(adam_kernel, count), out_shape=(jax.Shap...  3.74 us

profile of v5, /device:TPU:0, one launch (start us, length us, event | category | flops | bytes accessed | tf_op | source)
XLA Modules:
  0.0 74.2 jit_solution(5788396333783231601)
XLA Ops:
  0.6 69.7 %step.1 = (bf16[256,256]{1,0:T(8,128)(2,1)S(1)}, f32[10,256]{1,0:T(8,128)S(1)}, f32[1,4,1024]{2,1,0:T(4,128)S(1)}, f32[32,12627]{1,0:T(8,128)S(1)}, f32[1,128]{1...) custom-call(f32[32,12627]{1,0:T(8,128)} %refs_0_.1, ...), custom_call_target="tpu_custom_call" | custom-call | flops 3000000000 | bytes 200000000 | tf_op jit(solution)/shard_map/step/pallas_call | solution.py:1339
  70.3 3.7 %adam.1 = (f32[1,1]{1,0:T(1,128)}, f32[32,12627]{1,0:T(8,128)}, f32[32,12627]{1,0:T(8,128)}, f32[32,12627]{1,0:T(8,128)}, bf16[32,12627]{1,0:T(8,128)(2,1)}, /*i...) custom-call(f32[32,12627]{1,0:T(8,128)S(1)} %get-tuple-element.24.refs_0_, ...), custom_call_target="tpu_custom_call" | custom-call | tf_op jit(solution)/shard_map/adam/pallas_call | solution.py:636

commit v6 on v5

--- a/solution.py
+++ b/solution.py
@@ -400,6 +400,10 @@
 
     single_grads = {}
 
+    def film_weights(q, grad_low):
+        columns = slice((q % 2) * 128, (q % 2) * 128 + 128)
+        grad_ref[B_FILM + q // 2, :, columns] = dot_tn(grad_low, cond_low).astype(bf16)
+
     def conv_weights(grad_low, source, block):
         turned = grad_low.T
         for t in range(5):
@@ -458,6 +462,8 @@
     single_grads[D_B2] = row_sum(grad)
     low = grad.astype(bf16)
     conv_weights(low, mid_one, lambda t: B_DS + t)
+    film_weights(2, gain_three.astype(bf16))
+    film_weights(3, shift_three.astype(bf16))
     reach(12)
     grad_mid = conv_source(low, down)
     shift_one = over_frames(grad_mid)
@@ -473,7 +479,8 @@
     back_cond = None
     for q in range(4):
         single_grads[(D_FS, D_FO, U_FS, U_FO)[q]] = jnp.sum(film_grads[q], axis=0, keepdims=True)
-        grad_ref[B_FILM + q // 2, :, (q % 2) * 128 : (q % 2) * 128 + 128] = dot_tn(film_low[q], cond_low).astype(bf16)
+        if q < 2:
+            film_weights(q, film_low[q])
         part = dot_nn(film_low[q], film_time(q))
         back_cond = part if back_cond is None else back_cond + part
     at_slots = [dot_nn(at_slot, v) for v in film_low]
@@ -1214,10 +1221,10 @@
             gather.film_product()
             for g in range(2, len(GATHER_GROUPS)):
                 gather.start_rows(g)
+            gather.second_hop(0)
             gather.first_hop(1)
-            gather.second_hop(0)
+            gather.first_hop(2)
             gather.film_hop()
-            gather.first_hop(2)
             gather.last_hop(0)
             gather.second_hop(1)
             for device in me.others():
@@ -1264,17 +1271,17 @@
             scatter.core_sum(2)
             scatter.first_sum(5)
             scatter.first_sum(4)
+            scatter.start(1)
         if point == 13:
             scatter.film_start()
             scatter.z_send(Z_FIRST, 1)
-            scatter.start(1)
         if point == 14:
             scatter.start(0)
             scatter.core_sum(1)
             scatter.second_sum(5)
             scatter.second_sum(4)
+            scatter.first_sum(2)
             scatter.core_sum(0)
-            scatter.first_sum(2)
 
     train_body(
         Stacked(weights), seen, slots, noisy, mask, levels, cotangent, table,

time: 74.4 us -> 73.8 us (level)
  no operation moved by 1% of the time
where the time goes in v6:
time: 73.8 us; the launch traced here: 73.7 us
  Pallas kernels  72.9 us (99%)
  between operations  0.8 us (1%)
    pallas_call x1, Pallas kernels, step(): pl.pallas_call(step_kernel, out_shape=(jax.ShapeDtypeStruct((C, 256), bf1...  69.2 us
    pallas_call x1, Pallas kernels, adam(): pl.pallas_call(functools.partial(adam_kernel, count), out_shape=(jax.Shap...  3.74 us

profile of v6, /device:TPU:0, one launch (start us, length us, event | category | flops | bytes accessed | tf_op | source)
XLA Modules:
  0.0 73.7 jit_solution(4626238802356803345)
XLA Ops:
  0.6 69.2 %step.1 = (bf16[256,256]{1,0:T(8,128)(2,1)S(1)}, f32[10,256]{1,0:T(8,128)S(1)}, f32[1,4,1024]{2,1,0:T(4,128)S(1)}, f32[32,12627]{1,0:T(8,128)S(1)}, f32[1,128]{1...) custom-call(f32[32,12627]{1,0:T(8,128)} %refs_0_.1, ...), custom_call_target="tpu_custom_call" | custom-call | flops 3000000000 | bytes 200000000 | tf_op jit(solution)/shard_map/step/pallas_call | solution.py:1346
  69.8 3.7 %adam.1 = (f32[1,1]{1,0:T(1,128)}, f32[32,12627]{1,0:T(8,128)}, f32[32,12627]{1,0:T(8,128)}, f32[32,12627]{1,0:T(8,128)}, bf16[32,12627]{1,0:T(8,128)(2,1)}, /*i...) custom-call(f32[32,12627]{1,0:T(8,128)S(1)} %get-tuple-element.24.refs_0_, ...), custom_call_target="tpu_custom_call" | custom-call | tf_op jit(solution)/shard_map/adam/pallas_call | solution.py:643

commit v7 on v6

--- a/solution.py
+++ b/solution.py
@@ -298,7 +298,7 @@
 def train_kernel(*refs):
     for b in range(B_UR, NB):
         refs[10][b, :, 128:] = jnp.zeros((256, 128), bf16)
-    train_body(*refs, lambda point: None)
+    train_body(*refs, lambda point: None)()
 
 
 def train_body(
@@ -502,14 +502,18 @@
     grad_ref[B_MISC, :, :128] = (misc_grad + stack.T).astype(bf16)
     grad_ref[B_MISC, :, 128:] = jnp.zeros((256, 128), bf16)
     reach(14)
-    result = act_four + dot_nt(wide, up_res(0)) + dot_nt(skip, up_res(1)) + vec(U_RB)
-    act_ref[...] = dot_tn(result.astype(bf16), swap).astype(bf16)
-    back = back + dot_nn(low, misc_first)
-    grad_start = back[:, 50:60]
-    for t in range(5):
-        grad_start = grad_start + step_frames(back[:, t * ADIM : (t + 1) * ADIM], 2 - t)
-    grad_cols = sum(dot_tn(part, swap) for part in split3(jnp.concatenate([grad_start, jnp.zeros((256, 6), f32)], axis=1)))
-    noisy_grad_ref[...] = grad_cols[:ADIM] * keep
+
+    def outputs():
+        result = act_four + dot_nt(wide, up_res(0)) + dot_nt(skip, up_res(1)) + vec(U_RB)
+        act_ref[...] = dot_tn(result.astype(bf16), swap).astype(bf16)
+        total = back + dot_nn(low, misc_first)
+        grad_start = total[:, 50:60]
+        for t in range(5):
+            grad_start = grad_start + step_frames(total[:, t * ADIM : (t + 1) * ADIM], 2 - t)
+        grad_cols = sum(dot_tn(part, swap) for part in split3(jnp.concatenate([grad_start, jnp.zeros((256, 6), f32)], axis=1)))
+        noisy_grad_ref[...] = grad_cols[:ADIM] * keep
+
+    return outputs
 
 
 def train(weights, seen_film, slots, noisy, mask, levels, cotangent):
@@ -1185,11 +1189,12 @@
 def step_kernel(*refs):
     params_out = refs[16]
     targets = (params_out,) + refs[19:27]
+    targets = targets[:2] + (refs[2],) + targets[3:4] + (refs[4],) + targets[5:]
     loads = [
         pltpu.make_async_copy(source, target, refs[-2].at[i])
         for i, (source, target) in enumerate(zip(refs[:11], targets + refs[17:19]))
     ]
-    for i in (0, 2, 1, 3, 4, 5, 6, 7, 8):
+    for i in (0, 1, 3, 5, 6, 7, 8):
         loads[i].start()
     refs = targets + refs[9:11] + refs[11:16] + refs[17:19] + refs[27:-2] + refs[-1:]
     (params, order, obs, slots, noisy, mask, levels, cotangent, table, first, second,
@@ -1204,7 +1209,6 @@
     loads[0].wait()
     loads[1].wait()
     pack_first(params, order, own)
-    loads[2].wait()
     obs_all[me.p, me.w] = fold_rows(obs[0].astype(f32)).astype(bf16)
     meet(me)
     gather.start_rows(0)
@@ -1212,7 +1216,7 @@
     pack_rest(params, own, film)
     gather.start_local()
     gather.start_rows(1)
-    for i in range(3, 9):
+    for i in (3, 5, 6, 7, 8):
         loads[i].wait()
 
     def reach(point):
@@ -1283,7 +1287,7 @@
             scatter.first_sum(2)
             scatter.core_sum(0)
 
-    train_body(
+    outputs = train_body(
         Stacked(weights), seen, slots, noisy, mask, levels, cotangent, table,
         act, noisy_grad, Stacked(grad), film_grad, reach,
     )
@@ -1300,6 +1304,7 @@
     scatter.last_sum(5)
     scatter.last_sum(4)
     scatter.last_sum(2)
+    outputs()
     scatter.last_sum(1)
     scatter.film_back()
     scatter.last_sum(0)
@@ -1353,7 +1358,7 @@
             jax.ShapeDtypeStruct((1, 128), f32),
             *[jax.ShapeDtypeStruct((ROWS, Q), f32)] * 3,
         ),
-        in_specs=[pl.BlockSpec(memory_space=pltpu.HBM)] * 11,
+        in_specs=[vmem if i in (2, 4) else pl.BlockSpec(memory_space=pltpu.HBM) for i in range(11)],
         out_specs=(vmem,) * 8,
         scratch_shapes=[
             *(pltpu.VMEM(v.shape, v.dtype) for v in inputs[1:9]),

time: 73.8 us -> 74.3 us (level)
  no operation moved by 1% of the time
where the time goes in v7:
time: 74.3 us; the launch traced here: 74.1 us
  Pallas kernels  73.3 us (99%)
  between operations  0.8 us (1%)
    pallas_call x1, Pallas kernels, step(): pl.pallas_call(step_kernel, out_shape=(jax.ShapeDtypeStruct((C, 256), bf1...  69.5 us
    pallas_call x1, Pallas kernels, adam(): pl.pallas_call(functools.partial(adam_kernel, count), out_shape=(jax.Shap...  3.74 us

profile of v7, /device:TPU:0, one launch (start us, length us, event | category | flops | bytes accessed | tf_op | source)
XLA Modules:
  0.0 74.1 jit_solution(6942387931291784335)
XLA Ops:
  0.6 69.5 %step.1 = (bf16[256,256]{1,0:T(8,128)(2,1)S(1)}, f32[10,256]{1,0:T(8,128)S(1)}, f32[1,4,1024]{2,1,0:T(4,128)S(1)}, f32[32,12627]{1,0:T(8,128)S(1)}, f32[1,128]{1...) custom-call(f32[32,12627]{1,0:T(8,128)} %refs_0_.1, ...), custom_call_target="tpu_custom_call" | custom-call | flops 3000000000 | bytes 200000000 | tf_op jit(solution)/shard_map/step/pallas_call | solution.py:1351
  70.2 3.7 %adam.1 = (f32[1,1]{1,0:T(1,128)}, f32[32,12627]{1,0:T(8,128)}, f32[32,12627]{1,0:T(8,128)}, f32[32,12627]{1,0:T(8,128)}, bf16[32,12627]{1,0:T(8,128)(2,1)}, /*i...) custom-call(f32[32,12627]{1,0:T(8,128)S(1)} %get-tuple-element.24.refs_0_, ...), custom_call_target="tpu_custom_call" | custom-call | tf_op jit(solution)/shard_map/adam/pallas_call | solution.py:647
